TPU v7x, 32 devices: a whole 2x2x4 slice. The times are simulated.
32 devices in a mesh: dp: 4 (over x, core), fsdp: 8 (over z, y).
Axes of the slice: x: 2, y: 2, z: 4, core: 2. Of those that a mesh axis runs over, the one named last changes fastest.
Arguments:
- tokens: bfloat16 [32768, 768], P(('dp', 'fsdp')), may hold values from -6 to 6
- segment_index: int32 [64, 512], P(('dp', 'fsdp')), may hold values from 0 to 7, never falling along the last dimension, each value on 1 to 128 neighbouring positions
- start_vectors: bfloat16 [64, 8, 768], P(('dp', 'fsdp')), may hold values from -6 to 6
- first_gain: bfloat16 [768], P('fsdp'), may hold values from 0.5 to 1.5
- query_weight: bfloat16 [768, 768], P('fsdp'), may hold values from -0.109375 to 0.109375
- key_weight: bfloat16 [768, 768], P('fsdp'), may hold values from -0.109375 to 0.109375
- value_weight: bfloat16 [768, 768], P('fsdp'), may hold values from -0.21875 to 0.21875
- output_weight: bfloat16 [768, 768], P('fsdp'), may hold values from -0.4375 to 0.4375
- position_table: float32 [32, 12], replicated, may hold values from -4 to 4
- second_gain: bfloat16 [768], P('fsdp'), may hold values from 0.5 to 1.5
- inner_weight: bfloat16 [768, 3072], P('fsdp'), may hold values from -0.21875 to 0.21875
- outer_weight: bfloat16 [3072, 768], P('fsdp'), may hold values from -0.15625 to 0.15625
- start_gain: bfloat16 [768], P('fsdp'), may hold values from 0.5 to 1.5
- self_value: bfloat16 [768, 768], P('fsdp'), may hold values from -0.21875 to 0.21875
- self_output: bfloat16 [768, 768], P('fsdp'), may hold values from -0.21875 to 0.21875
- middle_gain: bfloat16 [768], P('fsdp'), may hold values from 0.5 to 1.5
- cross_query: bfloat16 [768, 768], P('fsdp'), may hold values from -0.109375 to 0.109375
- cross_key: bfloat16 [768, 768], P('fsdp'), may hold values from -0.078125 to 0.078125
- cross_value: bfloat16 [768, 768], P('fsdp'), may hold values from -0.21875 to 0.21875
- cross_output: bfloat16 [768, 768], P('fsdp'), may hold values from -0.4375 to 0.4375
- final_gain: bfloat16 [768], P('fsdp'), may hold values from 0.5 to 1.5
- decoder_inner: bfloat16 [768, 3072], P('fsdp'), may hold values from -0.21875 to 0.21875
- decoder_outer: bfloat16 [3072, 768], P('fsdp'), may hold values from -0.15625 to 0.15625
- encoded_cotangent: bfloat16 [32768, 768], P(('dp', 'fsdp')), may hold values from -6 to 6
- decoded_cotangent: bfloat16 [64, 8, 768], P(('dp', 'fsdp')), may hold values from -6 to 6
Outputs:
- encoded: bfloat16 [32768, 768], P(('dp', 'fsdp'))
- decoded: bfloat16 [64, 8, 768], P(('dp', 'fsdp'))
- tokens_grad: float32 [32768, 768], P(('dp', 'fsdp'))
- start_grad: float32 [64, 8, 768], P(('dp', 'fsdp'))
- first_gain_grad: float32 [768], P('fsdp')
- query_weight_grad: float32 [768, 768], P('fsdp')
- key_weight_grad: float32 [768, 768], P('fsdp')
- value_weight_grad: float32 [768, 768], P('fsdp')
- output_weight_grad: float32 [768, 768], P('fsdp')
- position_table_grad: float32 [32, 12], replicated
- second_gain_grad: float32 [768], P('fsdp')
- inner_weight_grad: float32 [768, 3072], P('fsdp')
- outer_weight_grad: float32 [3072, 768], P('fsdp')
- start_gain_grad: float32 [768], P('fsdp')
- self_value_grad: float32 [768, 768], P('fsdp')
- self_output_grad: float32 [768, 768], P('fsdp')
- middle_gain_grad: float32 [768], P('fsdp')
- cross_query_grad: float32 [768, 768], P('fsdp')
- cross_key_grad: float32 [768, 768], P('fsdp')
- cross_value_grad: float32 [768, 768], P('fsdp')
- cross_output_grad: float32 [768, 768], P('fsdp')
- final_gain_grad: float32 [768], P('fsdp')
- decoder_inner_grad: float32 [768, 3072], P('fsdp')
- decoder_outer_grad: float32 [3072, 768], P('fsdp')
Inputs may be any that keep to these rules, and one draw needn't show every extreme that they name: `segment_index`: within each row of 512 tokens the pair numbers never fall, and each of the 8 numbers holds 1 to 128 consecutive tokens, one exactly 128.
All inputs are finite; a program needn't handle non-finite values.
Results may differ from a plain program's by a relative error of at most 0.025.
Values may be sent and summed in bfloat16 or wider, within the bound.
A program may use at most 320 MiB of HBM per device.

v0:
```python
import jax
import jax.numpy as jnp
from jax import lax
from jax.sharding import PartitionSpec as P

HEADS = 12
KV = 64


epsilon = 1e-06
negative_fill = -1e30
bucket_edges = (12, 16, 23, 32, 46, 64, 91)


def relative_buckets(length):
    places = jnp.arange(length, dtype=jnp.int32)
    offset = places[None, :] - places[:, None]
    distance = jnp.abs(offset)
    far_bucket = 8 + sum(((distance >= boundary).astype(jnp.int32) for boundary in bucket_edges))
    near_bucket = jnp.where(distance < 8, distance, far_bucket)
    return jnp.where(offset > 0, 16, 0) + near_bucket


def bucket_onehot(length, bucket_count):
    flat_buckets = relative_buckets(length).reshape(length * length)
    choices_row = jnp.arange(bucket_count, dtype=jnp.int32)
    return (flat_buckets[:, None] == choices_row[None, :]).astype(jnp.float32)


def product(left, right):
    return jnp.dot(left, right, preferred_element_type=jnp.float32)


def product_left(left, right):
    return lax.dot_general(
        left, right, (((0,), (0,)), ((), ())), preferred_element_type=jnp.float32
    )


def product_right(left, right):
    return lax.dot_general(
        left, right, (((1,), (1,)), ((), ())), preferred_element_type=jnp.float32
    )


def gelu_back(before, grad_out):
    unused, pullback = jax.vjp(jax.nn.gelu, before)
    return pullback(grad_out)[0]


def root_scale(field):
    return lax.rsqrt(jnp.mean(field * field, axis=-1, keepdims=True) + epsilon)


def norm_back(grad_normed, field, scale, gain):
    gain_grad = jnp.sum(grad_normed * field * scale, axis=0)
    weighted = grad_normed * gain
    field_grad = scale * weighted - field * (scale * scale * scale) * jnp.mean(
        weighted * field, axis=-1, keepdims=True
    )
    return (field_grad, gain_grad)


def split_heads(matrix):
    return matrix.reshape(matrix.shape[0], HEADS, KV)


def masked_scores(asking, key_rows, extra, allowed):
    scores = (
        jnp.einsum(
            "qhd,khd->hqk",
            split_heads(asking),
            split_heads(key_rows),
            preferred_element_type=jnp.float32,
        )
        + extra
    )
    return jnp.where(allowed[None], scores, negative_fill)


def attend_forward(asking, key_rows, value_rows, extra, allowed):
    scores = masked_scores(asking, key_rows, extra, allowed)
    highest_score = jnp.max(scores, axis=-1, keepdims=True)
    log_total = highest_score + jnp.log(
        jnp.sum(jnp.exp(scores - highest_score), axis=-1, keepdims=True)
    )
    shares = jnp.exp(scores - log_total).astype(jnp.bfloat16)
    mixed = jnp.einsum(
        "hqk,khd->qhd", shares, split_heads(value_rows), preferred_element_type=jnp.float32
    )
    return (mixed.reshape(asking.shape[0], HEADS * KV).astype(jnp.bfloat16), log_total)


def attend_backward(asking, key_rows, value_rows, extra, allowed, log_total, grad_mixed):
    scores = masked_scores(asking, key_rows, extra, allowed)
    shares = jnp.exp(scores - log_total)
    grad_heads = split_heads(grad_mixed)
    grad_shares = jnp.einsum(
        "qhd,khd->hqk", grad_heads, split_heads(value_rows), preferred_element_type=jnp.float32
    )
    grad_value = jnp.einsum(
        "hqk,qhd->khd", shares.astype(jnp.bfloat16), grad_heads, preferred_element_type=jnp.float32
    )
    grad_scores = shares * (grad_shares - jnp.sum(shares * grad_shares, axis=-1, keepdims=True))
    narrow = grad_scores.astype(jnp.bfloat16)
    grad_query = jnp.einsum(
        "hqk,khd->qhd", narrow, split_heads(key_rows), preferred_element_type=jnp.float32
    )
    grad_key = jnp.einsum(
        "hqk,qhd->khd", narrow, split_heads(asking), preferred_element_type=jnp.float32
    )
    query_count = asking.shape[0]
    key_count = key_rows.shape[0]
    return (
        grad_query.reshape(query_count, HEADS * KV),
        grad_key.reshape(key_count, HEADS * KV),
        grad_value.reshape(key_count, HEADS * KV),
        grad_scores,
    )


def on_device(
    tokens,
    segment_index,
    start_vectors,
    first_gain,
    query_weight,
    key_weight,
    value_weight,
    output_weight,
    position_table,
    second_gain,
    inner_weight,
    outer_weight,
    start_gain,
    self_value,
    self_output,
    middle_gain,
    cross_query,
    cross_key,
    cross_value,
    cross_output,
    final_gain,
    decoder_inner,
    decoder_outer,
    encoded_cotangent,
    decoded_cotangent,
):
    row_count = segment_index.shape[0]
    length = segment_index.shape[1]
    slot_count = start_vectors.shape[1]
    width = tokens.shape[1]
    encoder_full = (
        lax.all_gather(first_gain, "fsdp", axis=0, tiled=True),
        lax.all_gather(query_weight, "fsdp", axis=0, tiled=True),
        lax.all_gather(key_weight, "fsdp", axis=0, tiled=True),
        lax.all_gather(value_weight, "fsdp", axis=0, tiled=True),
        lax.all_gather(output_weight, "fsdp", axis=0, tiled=True),
        lax.all_gather(second_gain, "fsdp", axis=0, tiled=True),
        lax.all_gather(inner_weight, "fsdp", axis=0, tiled=True),
        lax.all_gather(outer_weight, "fsdp", axis=0, tiled=True),
    )
    gain_one, query_full, key_full, value_full, output_full, gain_two, inner_full, outer_full = (
        encoder_full
    )
    gain_one = gain_one.astype(jnp.float32)
    gain_two = gain_two.astype(jnp.float32)
    onehot = bucket_onehot(length, position_table.shape[0])
    extra = lax.dot_general(
        position_table, onehot, (((0,), (1,)), ((), ())), precision=lax.Precision.HIGHEST
    ).reshape(HEADS, length, length)
    field = tokens.astype(jnp.float32)
    scale_one = root_scale(field)
    normed_one = (field * scale_one * gain_one).astype(jnp.bfloat16)
    query_all = product(normed_one, query_full).astype(jnp.bfloat16)
    key_all = product(normed_one, key_full).astype(jnp.bfloat16)
    value_all = product(normed_one, value_full).astype(jnp.bfloat16)
    contexts = []
    kept_totals = []
    for row_index in range(row_count):
        row_begin = row_index * length
        row_end = row_begin + length
        segment_row = segment_index[row_index]
        allowed = segment_row[:, None] == segment_row[None, :]
        mixed, log_total = attend_forward(
            query_all[row_begin:row_end],
            key_all[row_begin:row_end],
            value_all[row_begin:row_end],
            extra,
            allowed,
        )
        contexts.append(mixed)
        kept_totals.append(log_total)
    context = jnp.concatenate(contexts, axis=0)
    hidden = field + product(context, output_full)
    scale_two = root_scale(hidden)
    normed_two = (hidden * scale_two * gain_two).astype(jnp.bfloat16)
    inner_before = product(normed_two, inner_full)
    active = jax.nn.gelu(inner_before).astype(jnp.bfloat16)
    encoded_full = hidden + product(active, outer_full)
    memory = encoded_full.astype(jnp.bfloat16)
    decoder_full = (
        lax.all_gather(start_gain, "fsdp", axis=0, tiled=True),
        lax.all_gather(self_value, "fsdp", axis=0, tiled=True),
        lax.all_gather(self_output, "fsdp", axis=0, tiled=True),
        lax.all_gather(middle_gain, "fsdp", axis=0, tiled=True),
        lax.all_gather(cross_query, "fsdp", axis=0, tiled=True),
        lax.all_gather(cross_key, "fsdp", axis=0, tiled=True),
        lax.all_gather(cross_value, "fsdp", axis=0, tiled=True),
        lax.all_gather(cross_output, "fsdp", axis=0, tiled=True),
        lax.all_gather(final_gain, "fsdp", axis=0, tiled=True),
        lax.all_gather(decoder_inner, "fsdp", axis=0, tiled=True),
        lax.all_gather(decoder_outer, "fsdp", axis=0, tiled=True),
    )
    (
        start_full,
        self_value_full,
        self_output_full,
        middle_full,
        cross_query_full,
        cross_key_full,
        cross_value_full,
        cross_output_full,
        final_full,
        decoder_inner_full,
        decoder_outer_full,
    ) = decoder_full
    start_full = start_full.astype(jnp.float32)
    middle_full = middle_full.astype(jnp.float32)
    final_full = final_full.astype(jnp.float32)
    start_field = start_vectors.astype(jnp.float32).reshape(row_count * slot_count, width)
    scale_start = root_scale(start_field)
    normed_start = (start_field * scale_start * start_full).astype(jnp.bfloat16)
    own_value = product(normed_start, self_value_full).astype(jnp.bfloat16)
    first_field = start_field + product(own_value, self_output_full)
    scale_mid = root_scale(first_field)
    normed_mid = (first_field * scale_mid * middle_full).astype(jnp.bfloat16)
    asking = product(normed_mid, cross_query_full).astype(jnp.bfloat16)
    cross_keys = product(memory, cross_key_full).astype(jnp.bfloat16)
    cross_values = product(memory, cross_value_full).astype(jnp.bfloat16)
    slot_index = jnp.arange(slot_count, dtype=jnp.int32)
    cross_parts = []
    cross_totals = []
    for row_index in range(row_count):
        row_begin = row_index * length
        row_end = row_begin + length
        slot_begin = row_index * slot_count
        slot_end = slot_begin + slot_count
        allowed = slot_index[:, None] == segment_index[row_index][None, :]
        mixed, log_total = attend_forward(
            asking[slot_begin:slot_end],
            cross_keys[row_begin:row_end],
            cross_values[row_begin:row_end],
            0.0,
            allowed,
        )
        cross_parts.append(mixed)
        cross_totals.append(log_total)
    cross_context = jnp.concatenate(cross_parts, axis=0)
    second_field = first_field + product(cross_context, cross_output_full)
    scale_fin = root_scale(second_field)
    normed_fin = (second_field * scale_fin * final_full).astype(jnp.bfloat16)
    decoder_before = product(normed_fin, decoder_inner_full)
    decoder_active = jax.nn.gelu(decoder_before).astype(jnp.bfloat16)
    decoded_full = second_field + product(decoder_active, decoder_outer_full)
    decoder_back = (
        lax.all_gather(start_gain, "fsdp", axis=0, tiled=True),
        lax.all_gather(self_value, "fsdp", axis=0, tiled=True),
        lax.all_gather(self_output, "fsdp", axis=0, tiled=True),
        lax.all_gather(middle_gain, "fsdp", axis=0, tiled=True),
        lax.all_gather(cross_query, "fsdp", axis=0, tiled=True),
        lax.all_gather(cross_key, "fsdp", axis=0, tiled=True),
        lax.all_gather(cross_value, "fsdp", axis=0, tiled=True),
        lax.all_gather(cross_output, "fsdp", axis=0, tiled=True),
        lax.all_gather(final_gain, "fsdp", axis=0, tiled=True),
        lax.all_gather(decoder_inner, "fsdp", axis=0, tiled=True),
        lax.all_gather(decoder_outer, "fsdp", axis=0, tiled=True),
    )
    encoder_back = (
        lax.all_gather(first_gain, "fsdp", axis=0, tiled=True),
        lax.all_gather(query_weight, "fsdp", axis=0, tiled=True),
        lax.all_gather(key_weight, "fsdp", axis=0, tiled=True),
        lax.all_gather(value_weight, "fsdp", axis=0, tiled=True),
        lax.all_gather(output_weight, "fsdp", axis=0, tiled=True),
        lax.all_gather(second_gain, "fsdp", axis=0, tiled=True),
        lax.all_gather(inner_weight, "fsdp", axis=0, tiled=True),
        lax.all_gather(outer_weight, "fsdp", axis=0, tiled=True),
    )
    (
        back_start,
        back_self_value,
        back_self_output,
        back_middle,
        back_cross_query,
        back_cross_key,
        back_cross_value,
        back_cross_output,
        back_final,
        back_decoder_inner,
        back_decoder_outer,
    ) = decoder_back
    (
        back_gain_one,
        back_query,
        back_key,
        back_value,
        back_output,
        back_gain_two,
        back_inner,
        back_outer,
    ) = encoder_back
    grad_second = decoded_cotangent.astype(jnp.float32).reshape(row_count * slot_count, width)
    grad_branch = grad_second.astype(jnp.bfloat16)
    grad_decoder_outer = product_left(decoder_active, grad_branch)
    grad_active = product_right(grad_branch, back_decoder_outer)
    grad_before = gelu_back(decoder_before, grad_active).astype(jnp.bfloat16)
    grad_decoder_inner = product_left(normed_fin, grad_before)
    grad_normed = product_right(grad_before, back_decoder_inner)
    field_part, grad_final = norm_back(
        grad_normed, second_field, scale_fin, back_final.astype(jnp.float32)
    )
    grad_second = grad_second + field_part
    grad_branch = grad_second.astype(jnp.bfloat16)
    grad_cross_output = product_left(cross_context, grad_branch)
    grad_cross_context = product_right(grad_branch, back_cross_output).astype(jnp.bfloat16)
    ask_parts = []
    key_parts = []
    value_parts = []
    for row_index in range(row_count):
        row_begin = row_index * length
        row_end = row_begin + length
        slot_begin = row_index * slot_count
        slot_end = slot_begin + slot_count
        allowed = slot_index[:, None] == segment_index[row_index][None, :]
        grad_ask_row, grad_key_row, grad_value_row, unused_scores = attend_backward(
            asking[slot_begin:slot_end],
            cross_keys[row_begin:row_end],
            cross_values[row_begin:row_end],
            0.0,
            allowed,
            cross_totals[row_index],
            grad_cross_context[slot_begin:slot_end],
        )
        ask_parts.append(grad_ask_row)
        key_parts.append(grad_key_row)
        value_parts.append(grad_value_row)
    grad_asking = jnp.concatenate(ask_parts, axis=0).astype(jnp.bfloat16)
    grad_cross_keys = jnp.concatenate(key_parts, axis=0).astype(jnp.bfloat16)
    grad_cross_values = jnp.concatenate(value_parts, axis=0).astype(jnp.bfloat16)
    grad_cross_query = product_left(normed_mid, grad_asking)
    grad_cross_key = product_left(memory, grad_cross_keys)
    grad_cross_value = product_left(memory, grad_cross_values)
    grad_memory = product_right(grad_cross_keys, back_cross_key) + product_right(
        grad_cross_values, back_cross_value
    )
    grad_normed = product_right(grad_asking, back_cross_query)
    field_part, grad_middle = norm_back(
        grad_normed, first_field, scale_mid, back_middle.astype(jnp.float32)
    )
    grad_first = grad_second + field_part
    grad_branch = grad_first.astype(jnp.bfloat16)
    grad_self_output = product_left(own_value, grad_branch)
    grad_own = product_right(grad_branch, back_self_output).astype(jnp.bfloat16)
    grad_self_value = product_left(normed_start, grad_own)
    grad_normed = product_right(grad_own, back_self_value)
    field_part, grad_start_gain = norm_back(
        grad_normed, start_field, scale_start, back_start.astype(jnp.float32)
    )
    start_grad = (grad_first + field_part).reshape(row_count, slot_count, width)
    (
        start_gain_grad,
        self_value_grad,
        self_output_grad,
        middle_gain_grad,
        cross_query_grad,
        cross_key_grad,
        cross_value_grad,
        cross_output_grad,
        final_gain_grad,
        decoder_inner_grad,
        decoder_outer_grad,
    ) = (
        lax.psum_scatter(grad_start_gain, "fsdp", scatter_dimension=0, tiled=True),
        lax.psum_scatter(grad_self_value, "fsdp", scatter_dimension=0, tiled=True),
        lax.psum_scatter(grad_self_output, "fsdp", scatter_dimension=0, tiled=True),
        lax.psum_scatter(grad_middle, "fsdp", scatter_dimension=0, tiled=True),
        lax.psum_scatter(grad_cross_query, "fsdp", scatter_dimension=0, tiled=True),
        lax.psum_scatter(grad_cross_key, "fsdp", scatter_dimension=0, tiled=True),
        lax.psum_scatter(grad_cross_value, "fsdp", scatter_dimension=0, tiled=True),
        lax.psum_scatter(grad_cross_output, "fsdp", scatter_dimension=0, tiled=True),
        lax.psum_scatter(grad_final, "fsdp", scatter_dimension=0, tiled=True),
        lax.psum_scatter(grad_decoder_inner, "fsdp", scatter_dimension=0, tiled=True),
        lax.psum_scatter(grad_decoder_outer, "fsdp", scatter_dimension=0, tiled=True),
    )
    (
        start_gain_grad,
        self_value_grad,
        self_output_grad,
        middle_gain_grad,
        cross_query_grad,
        cross_key_grad,
        cross_value_grad,
        cross_output_grad,
        final_gain_grad,
        decoder_inner_grad,
        decoder_outer_grad,
    ) = (
        lax.psum(start_gain_grad.astype(jnp.bfloat16), "dp").astype(jnp.float32),
        lax.psum(self_value_grad.astype(jnp.bfloat16), "dp").astype(jnp.float32),
        lax.psum(self_output_grad.astype(jnp.bfloat16), "dp").astype(jnp.float32),
        lax.psum(middle_gain_grad.astype(jnp.bfloat16), "dp").astype(jnp.float32),
        lax.psum(cross_query_grad.astype(jnp.bfloat16), "dp").astype(jnp.float32),
        lax.psum(cross_key_grad.astype(jnp.bfloat16), "dp").astype(jnp.float32),
        lax.psum(cross_value_grad.astype(jnp.bfloat16), "dp").astype(jnp.float32),
        lax.psum(cross_output_grad.astype(jnp.bfloat16), "dp").astype(jnp.float32),
        lax.psum(final_gain_grad.astype(jnp.bfloat16), "dp").astype(jnp.float32),
        lax.psum(decoder_inner_grad.astype(jnp.bfloat16), "dp").astype(jnp.float32),
        lax.psum(decoder_outer_grad.astype(jnp.bfloat16), "dp").astype(jnp.float32),
    )
    grad_encoded = encoded_cotangent.astype(jnp.float32) + grad_memory
    grad_branch = grad_encoded.astype(jnp.bfloat16)
    grad_outer = product_left(active, grad_branch)
    grad_active = product_right(grad_branch, back_outer)
    grad_before = gelu_back(inner_before, grad_active).astype(jnp.bfloat16)
    grad_inner = product_left(normed_two, grad_before)
    grad_normed = product_right(grad_before, back_inner)
    field_part, grad_gain_two = norm_back(
        grad_normed, hidden, scale_two, back_gain_two.astype(jnp.float32)
    )
    grad_hidden = grad_encoded + field_part
    grad_branch = grad_hidden.astype(jnp.bfloat16)
    grad_output = product_left(context, grad_branch)
    grad_context = product_right(grad_branch, back_output).astype(jnp.bfloat16)
    query_parts = []
    key_parts = []
    value_parts = []
    bias_grad = jnp.zeros((HEADS, length, length), jnp.float32)
    for row_index in range(row_count):
        row_begin = row_index * length
        row_end = row_begin + length
        segment_row = segment_index[row_index]
        allowed = segment_row[:, None] == segment_row[None, :]
        grad_query_row, grad_key_row, grad_value_row, grad_scores = attend_backward(
            query_all[row_begin:row_end],
            key_all[row_begin:row_end],
            value_all[row_begin:row_end],
            extra,
            allowed,
            kept_totals[row_index],
            grad_context[row_begin:row_end],
        )
        query_parts.append(grad_query_row)
        key_parts.append(grad_key_row)
        value_parts.append(grad_value_row)
        bias_grad = bias_grad + grad_scores
    grad_query_all = jnp.concatenate(query_parts, axis=0).astype(jnp.bfloat16)
    grad_key_all = jnp.concatenate(key_parts, axis=0).astype(jnp.bfloat16)
    grad_value_all = jnp.concatenate(value_parts, axis=0).astype(jnp.bfloat16)
    grad_query = product_left(normed_one, grad_query_all)
    grad_key = product_left(normed_one, grad_key_all)
    grad_value = product_left(normed_one, grad_value_all)
    grad_normed = (
        product_right(grad_query_all, back_query)
        + product_right(grad_key_all, back_key)
        + product_right(grad_value_all, back_value)
    )
    field_part, grad_gain_one = norm_back(
        grad_normed, field, scale_one, back_gain_one.astype(jnp.float32)
    )
    tokens_grad = grad_hidden + field_part
    table_grad = lax.dot_general(
        onehot,
        bias_grad.reshape(HEADS, length * length),
        (((0,), (1,)), ((), ())),
        precision=lax.Precision.HIGHEST,
    )
    (
        first_gain_grad,
        query_weight_grad,
        key_weight_grad,
        value_weight_grad,
        output_weight_grad,
        second_gain_grad,
        inner_weight_grad,
        outer_weight_grad,
    ) = (
        lax.psum_scatter(grad_gain_one, "fsdp", scatter_dimension=0, tiled=True),
        lax.psum_scatter(grad_query, "fsdp", scatter_dimension=0, tiled=True),
        lax.psum_scatter(grad_key, "fsdp", scatter_dimension=0, tiled=True),
        lax.psum_scatter(grad_value, "fsdp", scatter_dimension=0, tiled=True),
        lax.psum_scatter(grad_output, "fsdp", scatter_dimension=0, tiled=True),
        lax.psum_scatter(grad_gain_two, "fsdp", scatter_dimension=0, tiled=True),
        lax.psum_scatter(grad_inner, "fsdp", scatter_dimension=0, tiled=True),
        lax.psum_scatter(grad_outer, "fsdp", scatter_dimension=0, tiled=True),
    )
    (
        first_gain_grad,
        query_weight_grad,
        key_weight_grad,
        value_weight_grad,
        output_weight_grad,
        second_gain_grad,
        inner_weight_grad,
        outer_weight_grad,
    ) = (
        lax.psum(first_gain_grad.astype(jnp.bfloat16), "dp").astype(jnp.float32),
        lax.psum(query_weight_grad.astype(jnp.bfloat16), "dp").astype(jnp.float32),
        lax.psum(key_weight_grad.astype(jnp.bfloat16), "dp").astype(jnp.float32),
        lax.psum(value_weight_grad.astype(jnp.bfloat16), "dp").astype(jnp.float32),
        lax.psum(output_weight_grad.astype(jnp.bfloat16), "dp").astype(jnp.float32),
        lax.psum(second_gain_grad.astype(jnp.bfloat16), "dp").astype(jnp.float32),
        lax.psum(inner_weight_grad.astype(jnp.bfloat16), "dp").astype(jnp.float32),
        lax.psum(outer_weight_grad.astype(jnp.bfloat16), "dp").astype(jnp.float32),
    )
    position_table_grad = lax.psum(table_grad, ("dp", "fsdp"))
    decoded = decoded_full.reshape(row_count, slot_count, width).astype(jnp.bfloat16)
    return (
        encoded_full.astype(jnp.bfloat16),
        decoded,
        tokens_grad,
        start_grad,
        first_gain_grad,
        query_weight_grad,
        key_weight_grad,
        value_weight_grad,
        output_weight_grad,
        position_table_grad,
        second_gain_grad,
        inner_weight_grad,
        outer_weight_grad,
        start_gain_grad,
        self_value_grad,
        self_output_grad,
        middle_gain_grad,
        cross_query_grad,
        cross_key_grad,
        cross_value_grad,
        cross_output_grad,
        final_gain_grad,
        decoder_inner_grad,
        decoder_outer_grad,
    )


def solution(mesh):
    placed = (
        P(("dp", "fsdp"), None),
        P(("dp", "fsdp"), None),
        P(("dp", "fsdp"), None, None),
        P("fsdp"),
        P("fsdp", None),
        P("fsdp", None),
        P("fsdp", None),
        P("fsdp", None),
        P(),
        P("fsdp"),
        P("fsdp", None),
        P("fsdp", None),
        P("fsdp"),
        P("fsdp", None),
        P("fsdp", None),
        P("fsdp"),
        P("fsdp", None),
        P("fsdp", None),
        P("fsdp", None),
        P("fsdp", None),
        P("fsdp"),
        P("fsdp", None),
        P("fsdp", None),
        P(("dp", "fsdp"), None),
        P(("dp", "fsdp"), None, None),
    )
    return jax.shard_map(
        on_device,
        mesh=mesh,
        in_specs=placed,
        out_specs=(
            P(("dp", "fsdp"), None),
            P(("dp", "fsdp"), None, None),
            P(("dp", "fsdp"), None),
            P(("dp", "fsdp"), None, None),
            P("fsdp"),
            P("fsdp", None),
            P("fsdp", None),
            P("fsdp", None),
            P("fsdp", None),
            P(),
            P("fsdp"),
            P("fsdp", None),
            P("fsdp", None),
            P("fsdp"),
            P("fsdp", None),
            P("fsdp", None),
            P("fsdp"),
            P("fsdp", None),
            P("fsdp", None),
            P("fsdp", None),
            P("fsdp", None),
            P("fsdp"),
            P("fsdp", None),
            P("fsdp", None),
        ),
        check_vma=False,
    )
```

profile of v0, /device:TPU:1, one launch (start us, length us, event | category | flops | bytes accessed | tf_op | source)
XLA Modules:
  0.0 2313.0 jit_solution(2261429452144677492)
XLA Ops:
  23.0 31.3 %all-reduce.11 = (bf16[768]{0:T(1024)(128)(2,1)S(1)}, bf16[768]{0:T(1024)(128)(2,1)S(1)}, bf16[768]{0:T(1024)(128)(2,1)S(1)}, bf16[768]{0:T(1024)(128)(2,1)S(1)}, bf16[768]{0:T(1024)(128)(2,1)S(1)}) all-reduce(bf16[768]{0:T(1024)(128)(2,1)S(1)} %dynamic-update-slice, ...), channel_id=1, replica_groups=mesh['dp'=4,'fsdp'=8] {'fsdp'}, use_global_device_ids=true, to_apply=%add | all-reduce | flops 3840 | bytes 15360
  61.9 11.5 fusion.1
  73.4 19.4 copy.199
  92.8 10.7 slice.106
  103.5 13.0 copy.148
  120.4 16.0 all-gather.33.cloned.1.call-done
  138.8 39.5 %all-gather.17.cloned.1.call-done = bf16[768,768]{1,0:T(8,128)(2,1)} async-done(((bf16[96,768]{1,0:T(8,128)(2,1)}), bf16[768,768]{1,0:T(8,128)(2,1)}) %all-gather.17.cloned.1.call-update) | async-done | bytes 1179664 | tf_op jit(solution)/shard_map/all_gather | solution.py:155
  182.4 37.8 %all-gather.19.cloned.1.call-done = bf16[768,768]{1,0:T(8,128)(2,1)} async-done(((bf16[96,768]{1,0:T(8,128)(2,1)}), bf16[768,768]{1,0:T(8,128)(2,1)}) %all-gather.19.cloned.1.call-update) | async-done | bytes 1179664 | tf_op jit(solution)/shard_map/all_gather | solution.py:156
  223.2 38.9 %all-gather.15.cloned.1.call-done = bf16[768,768]{1,0:T(8,128)(2,1)} async-done(((bf16[96,768]{1,0:T(8,128)(2,1)}), bf16[768,768]{1,0:T(8,128)(2,1)}) %all-gather.15.cloned.1.call-update) | async-done | bytes 1179664 | tf_op jit(solution)/shard_map/all_gather | solution.py:157
  266.5 6.1 fusion.152
  274.5 11.5 fusion.153
  286.1 6.6 exponential_reduce_fusion.1
  299.7 4.4 all-gather.21.cloned.1.call-done
  304.1 4.5 multiply_reduce_fusion.4
  308.7 76.6 %all-gather.23.cloned.1.call-done = bf16[768,3072]{1,0:T(8,128)(2,1)} async-done(((bf16[96,3072]{1,0:T(8,128)(2,1)}), bf16[768,3072]{1,0:T(8,128)(2,1)}) %all-gather.23.cloned.1.call-update) | async-done | bytes 4718608 | tf_op jit(solution)/shard_map/all_gather | solution.py:160
  385.3 11.1 fusion.135
  396.3 69.2 %all-gather.25.cloned.1.call-done = bf16[3072,768]{1,0:T(8,128)(2,1)} async-done(((bf16[384,768]{1,0:T(8,128)(2,1)}), bf16[3072,768]{1,0:T(8,128)(2,1)}) %all-gather.25.cloned.1.call-update) | async-done | bytes 4718608 | tf_op jit(solution)/shard_map/all_gather | solution.py:161
  465.5 11.2 add_convert_fusion
  476.7 29.8 %all-gather.35.cloned.1.call-done = bf16[768,768]{1,0:T(8,128)(2,1)} async-done(((bf16[96,768]{1,0:T(8,128)(2,1)}), bf16[768,768]{1,0:T(8,128)(2,1)}) %all-gather.35.cloned.1.call-update) | async-done | bytes 1179664 | tf_op jit(solution)/shard_map/all_gather | solution.py:208
  510.4 38.1 %all-gather.31.cloned.1.call-done = bf16[768,768]{1,0:T(8,128)(2,1)} async-done(((bf16[96,768]{1,0:T(8,128)(2,1)}), bf16[768,768]{1,0:T(8,128)(2,1)}) %all-gather.31.cloned.1.call-update) | async-done | bytes 1179664 | tf_op jit(solution)/shard_map/all_gather | solution.py:209
  548.6 3.2 convolution_convert_fusion.2
  562.7 27.7 %all-gather.37.cloned.1.call-done = bf16[768,768]{1,0:T(8,128)(2,1)} async-done(((bf16[96,768]{1,0:T(8,128)(2,1)}), bf16[768,768]{1,0:T(8,128)(2,1)}) %all-gather.37.cloned.1.call-update) | async-done | bytes 1179664 | tf_op jit(solution)/shard_map/all_gather | solution.py:210
  593.3 78.3 %all-gather.39.cloned.1.call-done = bf16[768,3072]{1,0:T(8,128)(2,1)} async-done(((bf16[96,3072]{1,0:T(8,128)(2,1)}), bf16[768,3072]{1,0:T(8,128)(2,1)}) %all-gather.39.cloned.1.call-update) | async-done | bytes 4718608 | tf_op jit(solution)/shard_map/all_gather | solution.py:212
  671.6 3.8 fusion.133
  675.4 76.3 %all-gather.41.cloned.1.call-done = bf16[3072,768]{1,0:T(8,128)(2,1)} async-done(((bf16[384,768]{1,0:T(8,128)(2,1)}), bf16[3072,768]{1,0:T(8,128)(2,1)}) %all-gather.41.cloned.1.call-update) | async-done | bytes 4718608 | tf_op jit(solution)/shard_map/all_gather | solution.py:213
  751.7 3.9 fusion.73
  780.5 4.4 fusion.58
  785.0 3.3 fusion.60
  788.3 4.6 add_add_fusion.1
  792.9 17.4 fusion.10
  810.3 10.3 multiply_reduce_fusion.2
  823.0 2.9 fusion.61
  842.3 3.5 convolution_convert_fusion
  846.6 6.8 fusion.42
  856.4 2.9 fusion.53
  859.8 9.1 multiply_reduce_fusion.1
  868.9 9.0 multiply_reduce_fusion
  877.9 26.9 %fusion.13 = (f32[12,512,512]{1,2,0:T(8,128)}, bf16[12,512,512]{1,2,0:T(8,128)(2,1)}, bf16[12,512,512]{1,2,0:T(8,128)(2,1)}) fusion(f32[12,512,512]{1,2,0:T(8,128)} %get-tuple-element.211, f32[12,512]{1,0:T(8,128)S(1)} %get-tuple-element.210, f32[12,512,512]{1,2,0:T(8,128)} %get-tuple-element.193, f32[12,512]{1,0:T(8,128)S(1)} %copy-done.61, ...), kind=kLoop, calls=%fused_computation.33 | loop fusion | flops 28311552 | bytes 75595776 | tf_op jit(solution)/shard_map/add | solution.py:455
  904.8 5.0 convolution_convert_fusion.10
  915.8 3.9 convolution_convert_fusion.12
  919.7 4.2 convolution_convert_fusion.13
  927.9 14.4 fusion.64
  942.4 10.4 fusion.134
  953.8 5.0 fusion.90
  959.7 5.0 fusion.132
  967.8 12.8 copy.178
  994.7 61.5 %reduce-scatter.31.cloned.1.call-done = f32[96,768]{1,0:T(8,128)} async-done(((f32[768,768]{1,0:T(8,128)}), f32[96,768]{1,0:T(8,128)}) %reduce-scatter.31.cloned.1.call-update) | async-done | bytes 294928 | tf_op jit(solution)/shard_map/reduce_scatter | solution.py:387
  1057.8 69.9 %reduce-scatter.29.cloned.1.call-done = f32[96,768]{1,0:T(8,128)} async-done(((f32[768,768]{1,0:T(8,128)}), f32[96,768]{1,0:T(8,128)}) %reduce-scatter.29.cloned.1.call-update) | async-done | bytes 294928 | tf_op jit(solution)/shard_map/reduce_scatter | solution.py:385
  1129.4 69.8 %reduce-scatter.37.cloned.1.call-done = f32[96,768]{1,0:T(8,128)} async-done(((f32[768,768]{1,0:T(8,128)}), f32[96,768]{1,0:T(8,128)}) %reduce-scatter.37.cloned.1.call-update) | async-done | bytes 294928 | tf_op jit(solution)/shard_map/reduce_scatter | solution.py:390
  1200.8 69.8 %reduce-scatter.27.cloned.1.call-done = f32[96,768]{1,0:T(8,128)} async-done(((f32[768,768]{1,0:T(8,128)}), f32[96,768]{1,0:T(8,128)}) %reduce-scatter.27.cloned.1.call-update) | async-done | bytes 294928 | tf_op jit(solution)/shard_map/reduce_scatter | solution.py:384
  1272.2 70.0 %reduce-scatter.19.cloned.1.call-done = f32[96,768]{1,0:T(8,128)} async-done(((f32[768,768]{1,0:T(8,128)}), f32[96,768]{1,0:T(8,128)}) %reduce-scatter.19.cloned.1.call-update) | async-done | bytes 294928 | tf_op jit(solution)/shard_map/reduce_scatter | solution.py:490
  1343.9 69.9 %reduce-scatter.17.cloned.1.call-done = f32[96,768]{1,0:T(8,128)} async-done(((f32[768,768]{1,0:T(8,128)}), f32[96,768]{1,0:T(8,128)}) %reduce-scatter.17.cloned.1.call-update) | async-done | bytes 294928 | tf_op jit(solution)/shard_map/reduce_scatter | solution.py:489
  1415.4 69.8 %reduce-scatter.15.cloned.1.call-done = f32[96,768]{1,0:T(8,128)} async-done(((f32[768,768]{1,0:T(8,128)}), f32[96,768]{1,0:T(8,128)}) %reduce-scatter.15.cloned.1.call-update) | async-done | bytes 294928 | tf_op jit(solution)/shard_map/reduce_scatter | solution.py:488
  1486.9 165.6 %reduce-scatter.25.cloned.1.call-done = f32[384,768]{1,0:T(8,128)} async-done(((f32[3072,768]{1,0:T(8,128)}), f32[384,768]{1,0:T(8,128)}) %reduce-scatter.25.cloned.1.call-update) | async-done | bytes 1179664 | tf_op jit(solution)/shard_map/reduce_scatter | solution.py:494
  1654.6 163.9 %reduce-scatter.23.cloned.1.call-done = f32[96,3072]{1,0:T(8,128)} async-done(((f32[768,3072]{1,0:T(8,128)}), f32[96,3072]{1,0:T(8,128)}) %reduce-scatter.23.cloned.1.call-update) | async-done | bytes 1179664 | tf_op jit(solution)/shard_map/reduce_scatter | solution.py:493
  1820.7 163.7 %reduce-scatter.41.cloned.1.call-done = f32[384,768]{1,0:T(8,128)} async-done(((f32[3072,768]{1,0:T(8,128)}), f32[384,768]{1,0:T(8,128)}) %reduce-scatter.41.cloned.1.call-update) | async-done | bytes 1179664 | tf_op jit(solution)/shard_map/reduce_scatter | solution.py:393
  1986.5 164.0 %reduce-scatter.39.cloned.1.call-done = f32[96,3072]{1,0:T(8,128)} async-done(((f32[768,3072]{1,0:T(8,128)}), f32[96,3072]{1,0:T(8,128)}) %reduce-scatter.39.cloned.1.call-update) | async-done | bytes 1179664 | tf_op jit(solution)/shard_map/reduce_scatter | solution.py:392
  2154.6 28.1 %all-reduce.10 = (bf16[768]{0:T(1024)(128)(2,1)S(1)}, bf16[768]{0:T(1024)(128)(2,1)S(1)}, bf16[768]{0:T(1024)(128)(2,1)S(1)}, bf16[768]{0:T(1024)(128)(2,1)S(1)}, bf16[768]{0:T(1024)(128)(2,1)S(1)}) all-reduce(f32[768]{0:T(1024)S(1)} %get-tuple-element.122, ...), channel_id=2, replica_groups=mesh['dp'=4,'fsdp'=8] {'fsdp'}, use_global_device_ids=true, to_apply=%region_23.24.clone | all-reduce | flops 3840 | bytes 23040
  2183.1 12.7 all-reduce.12
  2200.7 13.2 pad.12
  2213.9 15.4 copy.200
  2229.3 17.6 fusion
  2246.9 36.3 %psum.145 = f32[32,12]{0,1:T(8,128)} all-reduce(f32[32,12]{0,1:T(8,128)S(1)} %fusion), channel_id=1, replica_groups=mesh['dp'=4,'fsdp'=8] {'dp','fsdp'}, use_global_device_ids=true, to_apply=%region_33.34 | all-reduce | flops 384 | bytes 3072 | tf_op jit(solution)/shard_map/psum | solution.py:515
  2284.0 3.7 fusion.50
  (490 shorter events, 188.1 us)
Async XLA Ops:
  7.2 54.7 %copy-start = (f32[32,12]{0,1:T(8,128)S(1)}, f32[32,12]{0,1:T(8,128)}, u32[]{:S(2)}) copy-start(f32[32,12]{0,1:T(8,128)} %param.33) | copy-start | bytes 4612
  7.2 109.3 %all-gather.27.cloned.1.call-start = ((), (), s32[]{:S(2)}) async-start(), calls=%async_computation.20 | async-start | bytes 1327104 | tf_op jit(solution)/shard_map/all_gather | solution.py:204
  8.0 110.2 %all-gather.29.cloned.1.call-start = ((), (), s32[]{:S(2)}) async-start(), calls=%async_computation.21 | async-start | bytes 1327104 | tf_op jit(solution)/shard_map/all_gather | solution.py:205
  8.7 13.1 copy-start.122
  8.7 13.4 copy-start.123
  8.8 13.6 copy-start.124
  8.8 13.8 copy-start.125
  8.8 14.0 copy-start.126
  8.8 127.6 %all-gather.33.cloned.1.call-start = ((), (), s32[]{:S(2)}) async-start(), calls=%async_computation.23 | async-start | bytes 1327104 | tf_op jit(solution)/shard_map/all_gather | solution.py:207
  9.5 168.8 %all-gather.17.cloned.1.call-start = ((), (), s32[]{:S(2)}) async-start(), calls=%async_computation.15 | async-start | bytes 1327104 | tf_op jit(solution)/shard_map/all_gather | solution.py:155
  10.1 210.1 %all-gather.19.cloned.1.call-start = ((), (), s32[]{:S(2)}) async-start(), calls=%async_computation.16 | async-start | bytes 1327104 | tf_op jit(solution)/shard_map/all_gather | solution.py:156
  10.7 251.4 %all-gather.15.cloned.1.call-start = ((), (), s32[]{:S(2)}) async-start(), calls=%async_computation.14 | async-start | bytes 1327104 | tf_op jit(solution)/shard_map/all_gather | solution.py:157
  11.3 292.9 %all-gather.21.cloned.1.call-start = ((), (), s32[]{:S(2)}) async-start(), calls=%async_computation.17 | async-start | bytes 1327104 | tf_op jit(solution)/shard_map/all_gather | solution.py:158
  12.0 373.3 %all-gather.23.cloned.1.call-start = ((), (), s32[]{:S(2)}) async-start(), calls=%async_computation.18 | async-start | bytes 5308416 | tf_op jit(solution)/shard_map/all_gather | solution.py:160
  12.8 452.8 %all-gather.25.cloned.1.call-start = ((), (), s32[]{:S(2)}) async-start(), calls=%async_computation.19 | async-start | bytes 5308416 | tf_op jit(solution)/shard_map/all_gather | solution.py:161
  13.5 493.0 %all-gather.35.cloned.1.call-start = ((), (), s32[]{:S(2)}) async-start(), calls=%async_computation.24 | async-start | bytes 1327104 | tf_op jit(solution)/shard_map/all_gather | solution.py:208
  14.1 534.5 %all-gather.31.cloned.1.call-start = ((), (), s32[]{:S(2)}) async-start(), calls=%async_computation.22 | async-start | bytes 1327104 | tf_op jit(solution)/shard_map/all_gather | solution.py:209
  14.8 575.6 %all-gather.37.cloned.1.call-start = ((), (), s32[]{:S(2)}) async-start(), calls=%async_computation.25 | async-start | bytes 1327104 | tf_op jit(solution)/shard_map/all_gather | solution.py:210
  15.4 656.2 %all-gather.39.cloned.1.call-start = ((), (), s32[]{:S(2)}) async-start(), calls=%async_computation.26 | async-start | bytes 5308416 | tf_op jit(solution)/shard_map/all_gather | solution.py:212
  16.1 735.5 %all-gather.41.cloned.1.call-start = ((), (), s32[]{:S(2)}) async-start(), calls=%async_computation.27 | async-start | bytes 5308416 | tf_op jit(solution)/shard_map/all_gather | solution.py:213
  16.7 973.0 %reduce-scatter.33.cloned.1.call-start = ((), (), s32[]{:S(2)}) async-start(), calls=%async_computation.37 | async-start | bytes 2654208 | tf_op jit(solution)/shard_map/reduce_scatter | solution.py:388
  20.6 96.0 %copy-start.110 = (f32[16]{0:T(128)}, f32[16]{0:T(128)S(1)}, u32[]{:S(2)}) copy-start(f32[16]{0:T(128)S(1)} %rsqrt.61) | copy-start | bytes 196
  54.3 207.8 %copy-start.103 = (f32[768]{0:T(1024)}, f32[768]{0:T(1024)S(1)}, u32[]{:S(2)}) copy-start(f32[768]{0:T(1024)S(1)} %convert_element_type.359) | copy-start | bytes 9220
  54.4 62.2 %copy-start.97 = (f32[768]{0:T(1024)}, f32[768]{0:T(1024)S(1)}, u32[]{:S(2)}) copy-start(f32[768]{0:T(1024)S(1)} %convert_element_type.384) | copy-start | bytes 9220
  54.4 82.0 %copy-start.99 = (f32[768]{0:T(1024)}, f32[768]{0:T(1024)S(1)}, u32[]{:S(2)}) copy-start(f32[768]{0:T(1024)S(1)} %convert_element_type.388) | copy-start | bytes 9220
  54.4 703.2 %copy-start.84 = (f32[768]{0:T(1024)}, f32[768]{0:T(1024)S(1)}, u32[]{:S(2)}) copy-start(f32[768]{0:T(1024)S(1)} %convert_element_type.400) | copy-start | bytes 9220
  59.8 202.3 %copy-start.101 = (f32[1024]{0:T(1024)}, f32[1024]{0:T(1024)S(1)}, u32[]{:S(2)}) copy-start(f32[1024]{0:T(1024)S(1)} %get-tuple-element.179) | copy-start | bytes 12292
  118.1 63.0 %copy-start.88 = (bf16[16,768]{1,0:T(8,128)(2,1)}, bf16[16,768]{1,0:T(8,128)(2,1)S(1)}, u32[]{:S(2)}) copy-start(bf16[16,768]{1,0:T(8,128)(2,1)S(1)} %convolution_convert_fusion.21) | copy-start | bytes 73732
  119.8 61.3 %copy-start.43 = (f32[16,768]{1,0:T(8,128)}, f32[16,768]{1,0:T(8,128)S(1)}, u32[]{:S(2)}) copy-start(f32[16,768]{1,0:T(8,128)S(1)} %get-tuple-element.197) | copy-start | bytes 147460
  120.4 60.8 %copy-start.112 = (f32[16]{0:T(128)}, f32[16]{0:T(128)S(1)}, u32[]{:S(2)}) copy-start(f32[16]{0:T(128)S(1)} %get-tuple-element.187) | copy-start | bytes 196
  138.8 370.5 %copy-start.92 = (bf16[8,12,64]{2,1,0:T(8,128)(2,1)}, bf16[8,12,64]{2,1,0:T(8,128)(2,1)S(1)}, u32[]{:S(2)}) copy-start(bf16[8,12,64]{2,1,0:T(8,128)(2,1)S(1)} %reshape.498) | copy-start | bytes 36868
  223.2 41.9 %copy-start.14 = (bf16[512,768]{0,1:T(8,128)(2,1)}, bf16[512,768]{0,1:T(8,128)(2,1)S(1)}, u32[]{:S(2)}) copy-start(bf16[512,768]{0,1:T(8,128)(2,1)S(1)} %get-tuple-element.169) | copy-start | bytes 2359300
  223.2 51.3 %copy-start.12 = (bf16[512,768]{0,1:T(8,128)(2,1)}, bf16[512,768]{0,1:T(8,128)(2,1)S(1)}, u32[]{:S(2)}) copy-start(bf16[512,768]{0,1:T(8,128)(2,1)S(1)} %get-tuple-element.168) | copy-start | bytes 2359300
  265.1 27.6 %copy-start.16 = (bf16[512,768]{0,1:T(8,128)(2,1)}, bf16[512,768]{0,1:T(8,128)(2,1)S(1)}, u32[]{:S(2)}) copy-start(bf16[512,768]{0,1:T(8,128)(2,1)S(1)} %get-tuple-element.173) | copy-start | bytes 2359300
  265.1 29.7 %copy-start.18 = (bf16[512,768]{0,1:T(8,128)(2,1)}, bf16[512,768]{0,1:T(8,128)(2,1)S(1)}, u32[]{:S(2)}) copy-start(bf16[512,768]{0,1:T(8,128)(2,1)S(1)} %get-tuple-element.172) | copy-start | bytes 2359300
  272.6 20.1 copy-start.2
  476.7 29.8 %copy-start.45 = (bf16[1024,768]{0,1:T(8,128)(2,1)}, bf16[1024,768]{0,1:T(8,128)(2,1)S(1)}, u32[]{:S(2)}) copy-start(bf16[1024,768]{0,1:T(8,128)(2,1)S(1)} %add_convert_fusion) | copy-start | bytes 4718596
  510.4 42.3 %copy-start.90 = (f32[12,8]{1,0:T(8,128)}, f32[12,8]{1,0:T(8,128)S(1)}, u32[]{:S(2)}) copy-start(f32[12,8]{1,0:T(8,128)S(1)} %log_add_fusion.3) | copy-start | bytes 1156
  774.5 216.8 %reduce-scatter.35.cloned.1.call-start = ((), (), s32[]{:S(2)}) async-start(), calls=%async_computation.38 | async-start | bytes 2654208 | tf_op jit(solution)/shard_map/reduce_scatter | solution.py:389
  784.9 208.1 %reduce-scatter.21.cloned.1.call-start = ((), (), s32[]{:S(2)}) async-start(), calls=%async_computation.31 | async-start | bytes 2654208 | tf_op jit(solution)/shard_map/reduce_scatter | solution.py:491
  825.9 230.3 %reduce-scatter.31.cloned.1.call-start = ((), (), s32[]{:S(2)}) async-start(), calls=%async_computation.36 | async-start | bytes 2654208 | tf_op jit(solution)/shard_map/reduce_scatter | solution.py:387
  833.2 294.5 %reduce-scatter.29.cloned.1.call-start = ((), (), s32[]{:S(2)}) async-start(), calls=%async_computation.35 | async-start | bytes 2654208 | tf_op jit(solution)/shard_map/reduce_scatter | solution.py:385
  836.7 362.5 %reduce-scatter.37.cloned.1.call-start = ((), (), s32[]{:S(2)}) async-start(), calls=%async_computation.39 | async-start | bytes 2654208 | tf_op jit(solution)/shard_map/reduce_scatter | solution.py:390
  839.7 430.9 %reduce-scatter.27.cloned.1.call-start = ((), (), s32[]{:S(2)}) async-start(), calls=%async_computation.34 | async-start | bytes 2654208 | tf_op jit(solution)/shard_map/reduce_scatter | solution.py:384
  842.3 500.0 %reduce-scatter.19.cloned.1.call-start = ((), (), s32[]{:S(2)}) async-start(), calls=%async_computation.30 | async-start | bytes 2654208 | tf_op jit(solution)/shard_map/reduce_scatter | solution.py:490
  859.3 554.5 %reduce-scatter.17.cloned.1.call-start = ((), (), s32[]{:S(2)}) async-start(), calls=%async_computation.29 | async-start | bytes 2654208 | tf_op jit(solution)/shard_map/reduce_scatter | solution.py:489
  877.9 26.9 %copy-start.26 = (bf16[512,768]{0,1:T(8,128)(2,1)S(1)}, bf16[512,768]{0,1:T(8,128)(2,1)}, u32[]{:S(2)}) copy-start(bf16[512,768]{0,1:T(8,128)(2,1)} %get-tuple-element.171) | copy-start | bytes 2359300
  914.7 570.5 %reduce-scatter.15.cloned.1.call-start = ((), (), s32[]{:S(2)}) async-start(), calls=%async_computation.28 | async-start | bytes 2654208 | tf_op jit(solution)/shard_map/reduce_scatter | solution.py:488
  927.7 724.8 %reduce-scatter.25.cloned.1.call-start = ((), (), s32[]{:S(2)}) async-start(), calls=%async_computation.33 | async-start | bytes 10616832 | tf_op jit(solution)/shard_map/reduce_scatter | solution.py:494
  942.4 876.1 %reduce-scatter.23.cloned.1.call-start = ((), (), s32[]{:S(2)}) async-start(), calls=%async_computation.32 | async-start | bytes 10616832 | tf_op jit(solution)/shard_map/reduce_scatter | solution.py:493
  952.9 1031.5 %reduce-scatter.41.cloned.1.call-start = ((), (), s32[]{:S(2)}) async-start(), calls=%async_computation.41 | async-start | bytes 10616832 | tf_op jit(solution)/shard_map/reduce_scatter | solution.py:393
  958.9 1191.7 %reduce-scatter.39.cloned.1.call-start = ((), (), s32[]{:S(2)}) async-start(), calls=%async_computation.40 | async-start | bytes 10616832 | tf_op jit(solution)/shard_map/reduce_scatter | solution.py:392
  964.8 1322.9 %all-reduce.16.cloned.1.call-start = ((), (), s32[]{:S(2)}) async-start(), calls=%async_computation.42 | async-start | bytes 7667712 | tf_op jit(solution)/shard_map/psum | solution.py:507
  967.7 12.8 copy-start.77
  967.8 12.8 copy-start.79
  1986.5 168.0 %copy-start.107 = (f32[768]{0:T(1024)S(1)}, f32[768]{0:T(1024)}, u32[]{:S(2)}) copy-start(f32[768]{0:T(1024)} %get-tuple-element.124) | copy-start | bytes 9220
  1986.5 168.0 %copy-start.115 = (f32[768]{0:T(1024)S(1)}, f32[768]{0:T(1024)}, u32[]{:S(2)}) copy-start(f32[768]{0:T(1024)} %get-tuple-element.120) | copy-start | bytes 9220
  1986.5 211.8 %copy-start.9 = (f32[1024,768]{0,1:T(8,128)S(1)}, f32[1024,768]{0,1:T(8,128)}, u32[]{:S(2)}) copy-start(f32[1024,768]{0,1:T(8,128)} %fusion.21) | copy-start | bytes 9437188
  2213.9 15.4 copy-start.7
  2229.3 54.0 %copy-start.69 = (f32[16,768]{1,0:T(8,128)S(1)}, f32[16,768]{1,0:T(8,128)}, u32[]{:S(2)}) copy-start(f32[16,768]{1,0:T(8,128)} %copy-done.68) | copy-start | bytes 147460
  2287.7 12.5 copy-start.95
  2287.7 13.2 copy-start.94
  2287.7 13.9 copy-start.83
  2287.7 15.0 copy-start.82
  (98 other events, 401.5 us)
Sparse Core Ops, SparseCore 0:
  10.2 42.0 all-gather.26
  54.5 39.8 all-gather.28
  96.6 39.8 all-gather.32
  138.5 39.8 all-gather.16
  180.3 39.8 all-gather.18
  222.2 39.8 all-gather.14
  264.3 39.8 all-gather.20
  306.3 78.9 all-gather.22
  387.5 78.0 all-gather.24
  467.5 38.9 all-gather.34
  508.7 39.8 all-gather.30
  550.6 39.8 all-gather.36
  592.6 78.9 all-gather.38
  673.6 78.0 all-gather.40
  774.7 67.1 reduce-scatter.32
  845.2 68.0 reduce-scatter.34
  916.6 68.0 reduce-scatter.20
  988.1 68.0 reduce-scatter.30
  1059.7 68.0 reduce-scatter.28
  1131.1 68.0 reduce-scatter.36
  1202.6 67.9 reduce-scatter.26
  1274.1 68.1 reduce-scatter.18
  1345.8 68.0 reduce-scatter.16
  1417.1 68.0 reduce-scatter.14
  1488.8 163.5 reduce-scatter.24
  1655.9 162.5 reduce-scatter.22
  1821.9 162.3 reduce-scatter.40
  1987.9 162.5 reduce-scatter.38
  2155.6 80.6 all-reduce.15
where the time goes:
time: 2330 us; the launch traced here: 2310 us
  waiting for transfers between devices  1680 us (72%)
  matrix products  279 us (12%)
  local copies, waits for them, and re-layouts  130 us (6%)
  blocking collectives  108 us (5%)
  other arithmetic  95.6 us (4%)
    reduce_scatter x1, waiting for transfers between devices, on_device(): lax.psum_scatter(grad_outer, 'fsdp', scatter_dimension=0, tiled=True)  166 us
    reduce_scatter x1, waiting for transfers between devices, on_device(): lax.psum_scatter(grad_decoder_inner, 'fsdp', scatter_dimension=0, tiled=T...  164 us
    reduce_scatter x1, waiting for transfers between devices, on_device(): lax.psum_scatter(grad_inner, 'fsdp', scatter_dimension=0, tiled=True)  164 us
    reduce_scatter x1, waiting for transfers between devices, on_device(): lax.psum_scatter(grad_decoder_outer, 'fsdp', scatter_dimension=0, tiled=T...  164 us
    unnamed x293, local copies, waits for them, and re-layouts  80.3 us
    all_gather x1, waiting for transfers between devices, on_device(): lax.all_gather(decoder_inner, 'fsdp', axis=0, tiled=True)  78.3 us
    all_gather x1, waiting for transfers between devices, on_device(): lax.all_gather(inner_weight, 'fsdp', axis=0, tiled=True)  76.6 us
    all_gather x1, waiting for transfers between devices, on_device(): lax.all_gather(decoder_outer, 'fsdp', axis=0, tiled=True)  76.3 us
  transfers between devices with their start and end apart: 29, of which 23 were waited for; matrix products, arithmetic and copies ran while one was open for 19% of the time, Pallas kernels for 0%

commit v1 on v0

--- a/solution.py
+++ b/solution.py
@@ -1,6 +1,10 @@
+import functools
+
 import jax
 import jax.numpy as jnp
 from jax import lax
+from jax.experimental import pallas as pl
+from jax.experimental.pallas import tpu as pltpu
 from jax.sharding import PartitionSpec as P
 
 HEADS = 12
@@ -10,6 +14,573 @@
 epsilon = 1e-06
 negative_fill = -1e30
 bucket_edges = (12, 16, 23, 32, 46, 64, 91)
+
+
+MESH = pl.DeviceIdType.MESH
+KINDS = (
+    "square", "square", "square", "square", "wide", "tall", "square", "square",
+    "square", "square", "square", "square", "wide", "tall", "small",
+)
+
+
+def ring_position(index, count):
+    if count == 64:
+        slow, rest = index // 32, index % 32
+        row, column = rest // 8, rest % 8
+        place = row * 8 + column + (row % 2) * (7 - 2 * column)
+        return place + slow * (count - 1 - 2 * place)
+    across, along = index % 2, index // 2
+    return along + across * (count - 1 - 2 * along)
+
+
+def ring_index(position, count):
+    position = lax.rem(position, count)
+    across = position // (count // 2)
+    along = position + across * (count - 1 - 2 * position)
+    if count == 64:
+        row, column = along // 8, along % 8
+        return across * 32 + row * 8 + column + (row % 2) * (7 - 2 * column)
+    return 2 * along + across
+
+
+class Spot:
+    def __init__(self, count):
+        self.count = count
+        self.dp = lax.axis_index("dp")
+        self.fsdp = lax.axis_index("fsdp")
+        self.core = lax.rem(self.dp, 2)
+        self.plane = self.dp // 2
+        self.place = ring_position(self.fsdp, count)
+        self.sibling = (self.dp + 1 - 2 * self.core, self.fsdp)
+        self.opposite = (lax.rem(self.dp + 2, 4), self.fsdp)
+        self.after = (self.dp, ring_index(self.place + 1, count))
+        self.before = (self.dp, ring_index(self.place + count - 1, count))
+
+    def greet(self, others=()):
+        barrier = pltpu.get_barrier_semaphore()
+        partners = (self.sibling, self.opposite, self.after, self.before) + tuple(others)
+        for partner in partners:
+            pl.semaphore_signal(barrier, inc=1, device_id=partner, device_id_type=MESH)
+        pl.semaphore_wait(barrier, len(partners))
+
+
+def cut(kind, ref, plane, core):
+    rows, columns = ref.shape
+    if kind == "small":
+        return ref
+    if kind == "square":
+        half = columns // 2
+        return ref.at[:, pl.ds(pl.multiple_of(core * half, 128), half)]
+    if kind == "wide":
+        quarter = columns // 4
+        return ref.at[:, pl.ds(pl.multiple_of((core * 2 + plane) * quarter, 128), quarter)]
+    half, upper = columns // 2, rows // 2
+    return ref.at[
+        pl.ds(pl.multiple_of(plane * upper, 8), upper),
+        pl.ds(pl.multiple_of(core * half, 128), half),
+    ]
+
+
+def send(source, target, send_sem, recv_sem, device):
+    return pltpu.make_async_remote_copy(
+        src_ref=source,
+        dst_ref=target,
+        send_sem=send_sem,
+        recv_sem=recv_sem,
+        device_id=device,
+        device_id_type=MESH,
+    )
+
+
+def gather_kernel(count, kinds, *refs):
+    total = len(kinds)
+    shards, fulls = refs[:total], refs[total : 2 * total]
+    ring_out, ring_in, near_out, near_in, far_out, far_in, last_out, last_in, own_sem = refs[
+        2 * total :
+    ]
+    spot = Spot(count)
+    split = [i for i in range(total) if kinds[i] in ("wide", "tall")]
+
+    window = min(count, 8)
+
+    def slot_of(i, step):
+        turn = step if i % 2 else count - step
+        return ring_index(spot.place + turn, count)
+
+    def ring_copy(i, step, source=None):
+        here = cut(kinds[i], fulls[i].at[slot_of(i, step)], spot.plane, spot.core)
+        return send(
+            here if source is None else source,
+            here,
+            ring_out.at[i, lax.rem(step, window)],
+            ring_in.at[i, step],
+            spot.before if i % 2 else spot.after,
+        )
+
+    def near_copy(i, step):
+        here = cut(kinds[i], fulls[i].at[slot_of(i, step)], spot.plane, spot.core)
+        out = near_out.at[i, lax.rem(step, window)]
+        return send(here, here, out, near_in.at[i, step], spot.sibling)
+
+    def far_copy(i, step):
+        here = cut(kinds[i], fulls[i].at[slot_of(i, step)], spot.plane, spot.core)
+        at = split.index(i)
+        out = far_out.at[at, lax.rem(step, window)]
+        return send(here, here, out, far_in.at[at, step], spot.opposite)
+
+    def last_copy(i, step):
+        here = cut(kinds[i], fulls[i].at[slot_of(i, step)], 1 - spot.plane, spot.core)
+        at = split.index(i)
+        out = last_out.at[at, lax.rem(step, window)]
+        return send(here, here, out, last_in.at[at, step], spot.sibling)
+
+    def start(copy, i, step, first):
+        if window < count:
+
+            @pl.when(step >= first + window)
+            def _():
+                copy(i, step - window).wait_send()
+
+        copy(i, step).start()
+
+    def finish(copy, i, first, end):
+        def one(step, carry):
+            copy(i, step).wait_send()
+            return carry
+
+        lax.fori_loop(max(first, end - window), end, one, 0)
+
+    owns = []
+    for i in range(total):
+        owns.append(pltpu.make_async_copy(shards[i], fulls[i].at[spot.fsdp], own_sem.at[i]))
+        owns[-1].start()
+    spot.greet()
+    for i in range(total):
+        ring_copy(i, 0, cut(kinds[i], shards[i], spot.plane, spot.core)).start()
+
+    def one_step(step, carry):
+        for i in range(total):
+            ring_copy(i, step - 1).wait_recv()
+
+            @pl.when(step < count - 1)
+            def _():
+                start(ring_copy, i, step, 0)
+
+            if kinds[i] != "small":
+                start(near_copy, i, step, 1)
+            if i in split:
+                start(far_copy, i, step, 1)
+
+        @pl.when(step > 1)
+        def _():
+            for i in split:
+                far_copy(i, step - 1).wait_recv()
+                start(last_copy, i, step - 1, 1)
+
+        return carry
+
+    lax.fori_loop(1, count, one_step, 0)
+    for i in split:
+        far_copy(i, count - 1).wait_recv()
+        start(last_copy, i, count - 1, 1)
+
+    def settle(step, carry):
+        for i in range(total):
+            if kinds[i] != "small":
+                near_copy(i, step).wait_recv()
+            if i in split:
+                last_copy(i, step).wait_recv()
+        return carry
+
+    lax.fori_loop(1, count, settle, 0)
+    for i in range(total):
+        finish(ring_copy, i, 0, count - 1)
+        if kinds[i] != "small":
+            finish(near_copy, i, 1, count)
+        if i in split:
+            finish(far_copy, i, 1, count)
+            finish(last_copy, i, 1, count)
+    for copy in owns:
+        copy.wait()
+
+
+def gather_weights(count, shards, kinds):
+    total = len(shards)
+    split = sum(kind in ("wide", "tall") for kind in kinds)
+    window = min(count, 8)
+    many, few = [
+        [pltpu.SemaphoreType.DMA((rows, window)), pltpu.SemaphoreType.DMA((rows, count))] * 2
+        for rows in (total, split)
+    ]
+    return pl.pallas_call(
+        functools.partial(gather_kernel, count, kinds),
+        out_shape=[jax.ShapeDtypeStruct((count,) + s.shape, s.dtype) for s in shards],
+        in_specs=[pl.BlockSpec(memory_space=pl.ANY)] * total,
+        out_specs=[pl.BlockSpec(memory_space=pl.ANY)] * total,
+        scratch_shapes=many + few + [pltpu.SemaphoreType.DMA((total,))],
+        compiler_params=pltpu.CompilerParams(collective_id=0, has_side_effects=True),
+        name="gather_weights",
+    )(*shards)
+
+def plus(*terms):
+    total = terms[0].astype(jnp.float32)
+    for term in terms[1:]:
+        total = total + term.astype(jnp.float32)
+    return total
+
+
+def half_of(core, columns):
+    half = columns // 2
+    return pl.ds(pl.multiple_of(core * half, 128), half)
+
+
+def plane_part(kind, plane, rows, columns):
+    if kind == "wide":
+        return slice(None), pl.ds(pl.multiple_of(plane * (columns // 2), 128), columns // 2)
+    if kind == "tall":
+        return pl.ds(pl.multiple_of(plane * (rows // 2), 8), rows // 2), slice(None)
+    return slice(None), slice(None)
+
+
+ENCODER_KINDS = ("wide", "tall", "square", "square", "square", "square", "square", "square")
+
+
+def reduce_kernel(count, kinds, spans, *refs):
+    total, pairs = len(kinds), len(spans)
+    refs = list(refs)
+
+    def take(size):
+        got = refs[:size]
+        del refs[:size]
+        return got
+
+    grads = take(total)
+    left_part, right_part, small = take(3)
+    sums = take(total)
+    pair_sums = take(pairs)
+    (small_sum,) = take(1)
+    half, work, final = take(total), take(total), take(total)
+    split = [i for i in range(total) if kinds[i] != "square"]
+    far = take(len(split))
+    left_all, right_all = take(2)
+    pair_half, pair_far, pair_work = take(pairs), take(pairs), take(pairs)
+    small_near, small_mid, small_far, small_all = take(4)
+    (
+        near_sem, ring_out, ring_in, far_sem, end_sem, left_out, left_in,
+        right_out, right_in, pair_sem, small_sem, small_out, small_in,
+    ) = take(13)
+    spot = Spot(count)
+    core, plane = spot.core, spot.plane
+    diagonal = (lax.rem(spot.dp + 2, 4) + 1 - 2 * core, spot.fsdp)
+
+    def peer(k):
+        return (spot.dp, lax.rem(spot.fsdp + k, count))
+
+    barrier = pltpu.get_barrier_semaphore()
+    for partner in (spot.sibling, spot.opposite, diagonal):
+        pl.semaphore_signal(barrier, inc=1, device_id=partner, device_id_type=MESH)
+
+    def greet(k, carry):
+        pl.semaphore_signal(barrier, inc=1, device_id=peer(k), device_id_type=MESH)
+        return carry
+
+    lax.fori_loop(1, count, greet, 0)
+    pl.semaphore_wait(barrier, count + 2)
+
+    def near_copy(i):
+        columns = grads[i].shape[2]
+        return send(
+            grads[i].at[:, :, half_of(1 - core, columns)], half[i],
+            near_sem.at[0, i], near_sem.at[1, i], spot.sibling,
+        )
+
+    def slot_at(i, step):
+        turn = step + 1 if i % 2 else count - 1 - step
+        return ring_index(spot.place + turn, count)
+
+    def far_copy(i, step):
+        at = split.index(i)
+        rows, columns = half[i].shape[1:]
+        part = plane_part(kinds[i], 1 - plane, rows, columns)
+        return send(
+            half[i].at[(slot_at(i, step),) + part], far[at].at[step],
+            far_sem.at[0, at, step], far_sem.at[1, at, step], spot.opposite,
+        )
+
+    def ring_copy(i, step):
+        return send(
+            work[i].at[step], work[i].at[step + 1], ring_out.at[i, step], ring_in.at[i, step],
+            spot.before if i % 2 else spot.after,
+        )
+
+    def left_copy(k):
+        other = lax.rem(spot.fsdp + k, count)
+        return send(
+            left_part.at[other], left_all.at[spot.fsdp], left_out.at[k], left_in.at[k], peer(k)
+        )
+
+    def right_copy(way, step):
+        turn = step if way else count - step
+        slot = ring_index(spot.place + turn, count)
+        width = right_part.shape[1] // 2
+        here = right_all.at[slot, :, way * width : (way + 1) * width]
+        return send(
+            here, here, right_out.at[way, step], right_in.at[way, step],
+            spot.before if way else spot.after,
+        )
+
+    for i in range(total):
+        near_copy(i).start()
+    near_small = send(small, small_near, small_sem.at[0], small_sem.at[1], spot.sibling)
+    near_small.start()
+
+    def left_start(k, carry):
+        left_copy(k).start()
+        return carry
+
+    lax.fori_loop(1, count, left_start, 0)
+    right_all[spot.fsdp] = right_part[...]
+    left_all[spot.fsdp] = left_part[spot.fsdp]
+    for way in range(2):
+        right_copy(way, 0).start()
+    near_small.wait()
+    small_mid[...] = small[...] + small_near[...]
+    far_small = send(small_mid, small_far, small_sem.at[2], small_sem.at[3], spot.opposite)
+    far_small.start()
+
+    for i in range(total):
+        near_copy(i).wait_recv()
+
+        def join(slot, carry):
+            mine = grads[i][slot, :, half_of(core, grads[i].shape[2])]
+            half[i][slot] = plus(half[i][slot], mine).astype(jnp.bfloat16)
+            return carry
+
+        lax.fori_loop(0, count, join, 0)
+        if i in split:
+
+            def far_start(step, carry):
+                far_copy(i, step).start()
+                return carry
+
+            lax.fori_loop(0, count, far_start, 0)
+
+    far_small.wait()
+    small_all[spot.fsdp] = small_mid[...] + small_far[...]
+
+    def small_copy(k):
+        here = small_all.at[spot.fsdp]
+        return send(here, here, small_out.at[k], small_in.at[k], peer(k))
+
+    def small_start(k, carry):
+        small_copy(k).start()
+        return carry
+
+    lax.fori_loop(1, count, small_start, 0)
+
+    def right_step(step, carry):
+        for way in range(2):
+            right_copy(way, step - 1).wait_recv()
+
+            @pl.when(step < count - 1)
+            def _():
+                right_copy(way, step).start()
+
+        return carry
+
+    lax.fori_loop(1, count, right_step, 0)
+
+    def left_wait(k, carry):
+        left_copy(k).wait_recv()
+        return carry
+
+    lax.fori_loop(1, count, left_wait, 0)
+
+    def pair_near(j):
+        columns = pair_sums[j].shape[1]
+        return send(
+            pair_work[j].at[:, half_of(1 - core, columns)], pair_half[j],
+            pair_sem.at[0, j], pair_sem.at[1, j], spot.sibling,
+        )
+
+    def pair_across(j):
+        return send(
+            pair_half[j], pair_far[j], pair_sem.at[2, j], pair_sem.at[3, j], spot.opposite
+        )
+
+    def pair_end(j):
+        here = pair_sums[j].at[:, half_of(core, pair_sums[j].shape[1])]
+        return send(here, here, pair_sem.at[4, j], pair_sem.at[5, j], spot.sibling)
+
+    for j, (left_at, right_at) in enumerate(spans):
+        rows, columns = pair_sums[j].shape
+        span = -(-rows // 128) * 128
+        left = left_all[:, :, left_at : left_at + span].reshape(-1, span)
+        for begin in range(0, columns, 768):
+            right = right_all[:, :, right_at + begin : right_at + begin + 768].reshape(-1, 768)
+            block = lax.dot_general(
+                left, right, (((0,), (0,)), ((), ())), preferred_element_type=jnp.float32
+            )
+            pair_work[j][:, begin : begin + 768] = block[:rows].astype(jnp.bfloat16)
+        pair_near(j).start()
+    for j in range(pairs):
+        pair_near(j).wait()
+        mine = pair_work[j][:, half_of(core, pair_sums[j].shape[1])]
+        pair_half[j][...] = plus(pair_half[j][...], mine).astype(jnp.bfloat16)
+        pair_across(j).start()
+
+    def one_step(step, carry):
+        for i in range(total):
+            rows, columns = half[i].shape[1:]
+            slot = slot_at(i, step)
+            value = half[i][(slot,) + plane_part(kinds[i], plane, rows, columns)]
+            value = value.astype(jnp.float32)
+            if i in split:
+                far_copy(i, step).wait_recv()
+                value = value + far[split.index(i)][step].astype(jnp.float32)
+
+            @pl.when(step > 0)
+            def _():
+                ring_copy(i, step - 1).wait_recv()
+                work[i][step] = plus(value, work[i][step]).astype(jnp.bfloat16)
+
+            @pl.when(step == 0)
+            def _():
+                work[i][step] = value.astype(jnp.bfloat16)
+
+            @pl.when(step < count - 1)
+            def _():
+                ring_copy(i, step).start()
+
+        return carry
+
+    lax.fori_loop(0, count, one_step, 0)
+
+    def end_across(i):
+        return send(
+            work[i].at[count - 1], final[i], end_sem.at[0, i], end_sem.at[1, i], spot.opposite
+        )
+
+    def end_piece(i, mine_plane):
+        rows, columns = sums[i].shape
+        wide = half_of(core, columns)
+        if kinds[i] == "square":
+            return sums[i].at[:, wide]
+        return cut(kinds[i], sums[i], mine_plane, core)
+
+    def end_copies(i):
+        here = end_piece(i, plane)
+        copies = [send(here, here, end_sem.at[2, i], end_sem.at[3, i], spot.sibling)]
+        if i in split:
+            copies.append(send(here, here, end_sem.at[4, i], end_sem.at[5, i], spot.opposite))
+            copies.append(send(here, here, end_sem.at[6, i], end_sem.at[7, i], diagonal))
+        return copies
+
+    for i in range(total):
+        if i not in split:
+            end_across(i).start()
+    for i in split:
+        end_piece(i, plane)[...] = work[i][count - 1]
+        for copy in end_copies(i):
+            copy.start()
+    for j in range(pairs):
+        pair_across(j).wait()
+        here = half_of(core, pair_sums[j].shape[1])
+        pair_sums[j][:, here] = plus(pair_half[j][...], pair_far[j][...]).astype(jnp.bfloat16)
+        pair_end(j).start()
+    for i in range(total):
+        if i not in split:
+            end_across(i).wait()
+            value = plus(work[i][count - 1], final[i][...]).astype(jnp.bfloat16)
+            end_piece(i, plane)[...] = value
+            for copy in end_copies(i):
+                copy.start()
+
+    def small_wait(k, carry):
+        small_copy(k).wait_recv()
+        return carry
+
+    lax.fori_loop(1, count, small_wait, 0)
+    small_sum[...] = lax.fori_loop(
+        1, count, lambda k, so_far: so_far + small_all[k], small_all[0]
+    )
+    for i in range(total):
+        for copy in end_copies(i):
+            copy.wait()
+    for j in range(pairs):
+        pair_end(j).wait()
+    for i in range(total):
+        near_copy(i).wait_send()
+
+    def drain(step, carry):
+        for i in split:
+            far_copy(i, step).wait_send()
+        return carry
+
+    lax.fori_loop(0, count, drain, 0)
+
+    def drain_ring(step, carry):
+        for i in range(total):
+            ring_copy(i, step).wait_send()
+        for way in range(2):
+            right_copy(way, step).wait_send()
+        left_copy(step + 1).wait_send()
+        small_copy(step + 1).wait_send()
+        return carry
+
+    lax.fori_loop(0, count - 1, drain_ring, 0)
+
+
+def reduce_grads(count, kinds, grads, left_part, right_part, pair_shapes, small):
+    total, pairs = len(kinds), len(pair_shapes)
+    spans, left_at, right_at = [], 0, 0
+    for rows, columns in pair_shapes:
+        spans.append((left_at, right_at))
+        left_at, right_at = left_at + -(-rows // 128) * 128, right_at + columns
+    narrow = jnp.bfloat16
+    blocks = [g.shape[1:] for g in grads]
+    pieces = []
+    for kind, (rows, columns) in zip(kinds, blocks):
+        if kind == "wide":
+            pieces.append((rows, columns // 4))
+        elif kind == "tall":
+            pieces.append((rows // 2, columns // 2))
+        else:
+            pieces.append((rows, columns // 2))
+    split = [i for i in range(total) if kinds[i] != "square"]
+    dma = pltpu.SemaphoreType.DMA
+    scratch = [pltpu.VMEM((count, r, c // 2), narrow) for r, c in blocks]
+    scratch += [pltpu.VMEM((count, r, c), narrow) for r, c in pieces]
+    scratch += [pltpu.VMEM((r, c), narrow) for r, c in pieces]
+    scratch += [pltpu.VMEM((count,) + pieces[i], narrow) for i in split]
+    scratch += [
+        pltpu.VMEM(left_part.shape, narrow),
+        pltpu.VMEM((count,) + right_part.shape, narrow),
+    ]
+    scratch += [pltpu.VMEM((r, c // 2), narrow) for r, c in pair_shapes] * 2
+    scratch += [pltpu.VMEM((r, c), narrow) for r, c in pair_shapes]
+    scratch += [pltpu.VMEM(small.shape, jnp.float32)] * 3
+    scratch += [pltpu.VMEM((count,) + small.shape, jnp.float32)]
+    scratch += [
+        dma((2, total)), dma((total, count)), dma((total, count)), dma((2, len(split), count)),
+        dma((8, total)), dma((count,)), dma((count,)), dma((2, count)), dma((2, count)),
+        dma((6, pairs)), dma((4,)), dma((count,)), dma((count,)),
+    ]
+    outs = [jax.ShapeDtypeStruct(b, narrow) for b in blocks]
+    outs += [jax.ShapeDtypeStruct(s, narrow) for s in pair_shapes]
+    outs += [jax.ShapeDtypeStruct(small.shape, jnp.float32)]
+    got = pl.pallas_call(
+        functools.partial(reduce_kernel, count, kinds, spans),
+        out_shape=outs,
+        in_specs=[pl.BlockSpec(memory_space=pltpu.VMEM)] * (total + 3),
+        out_specs=[pl.BlockSpec(memory_space=pltpu.VMEM)] * len(outs),
+        scratch_shapes=scratch,
+        compiler_params=pltpu.CompilerParams(
+            collective_id=1, has_side_effects=True, vmem_limit_bytes=62 * 2**20
+        ),
+        name="reduce_grads",
+    )(*grads, left_part, right_part, small)
+    return got[:total], got[total : total + pairs], got[-1]
 
 
 def relative_buckets(length):
@@ -150,19 +721,27 @@
     length = segment_index.shape[1]
     slot_count = start_vectors.shape[1]
     width = tokens.shape[1]
-    encoder_full = (
-        lax.all_gather(first_gain, "fsdp", axis=0, tiled=True),
-        lax.all_gather(query_weight, "fsdp", axis=0, tiled=True),
-        lax.all_gather(key_weight, "fsdp", axis=0, tiled=True),
-        lax.all_gather(value_weight, "fsdp", axis=0, tiled=True),
-        lax.all_gather(output_weight, "fsdp", axis=0, tiled=True),
-        lax.all_gather(second_gain, "fsdp", axis=0, tiled=True),
-        lax.all_gather(inner_weight, "fsdp", axis=0, tiled=True),
-        lax.all_gather(outer_weight, "fsdp", axis=0, tiled=True),
-    )
-    gain_one, query_full, key_full, value_full, output_full, gain_two, inner_full, outer_full = (
-        encoder_full
-    )
+    count = lax.axis_size("fsdp")
+    depth = first_gain.shape[0]
+    gains = jnp.stack([first_gain, second_gain, start_gain, middle_gain, final_gain])
+    gains = jnp.pad(gains, ((0, 11), (0, 128 - depth)))
+    whole = gather_weights(
+        count,
+        (
+            query_weight, key_weight, value_weight, output_weight, inner_weight, outer_weight,
+            cross_key, cross_value, self_value, self_output, cross_query, cross_output,
+            decoder_inner, decoder_outer, gains,
+        ),
+        KINDS,
+    )
+    gain_parts = whole[14][:, :5, :depth]
+    gain_set = [gain_parts[:, at].reshape(count * depth) for at in range(5)]
+    (
+        query_full, key_full, value_full, output_full, inner_full, outer_full, cross_key_full,
+        cross_value_full, self_value_full, self_output_full, cross_query_full, cross_output_full,
+        decoder_inner_full, decoder_outer_full,
+    ) = [part.reshape(-1, part.shape[2]) for part in whole[:14]]
+    gain_one, gain_two, start_full, middle_full, final_full = gain_set
     gain_one = gain_one.astype(jnp.float32)
     gain_two = gain_two.astype(jnp.float32)
     onehot = bucket_onehot(length, position_table.shape[0])
@@ -199,32 +778,6 @@
     active = jax.nn.gelu(inner_before).astype(jnp.bfloat16)
     encoded_full = hidden + product(active, outer_full)
     memory = encoded_full.astype(jnp.bfloat16)
-    decoder_full = (
-        lax.all_gather(start_gain, "fsdp", axis=0, tiled=True),
-        lax.all_gather(self_value, "fsdp", axis=0, tiled=True),
-        lax.all_gather(self_output, "fsdp", axis=0, tiled=True),
-        lax.all_gather(middle_gain, "fsdp", axis=0, tiled=True),
-        lax.all_gather(cross_query, "fsdp", axis=0, tiled=True),
-        lax.all_gather(cross_key, "fsdp", axis=0, tiled=True),
-        lax.all_gather(cross_value, "fsdp", axis=0, tiled=True),
-        lax.all_gather(cross_output, "fsdp", axis=0, tiled=True),
-        lax.all_gather(final_gain, "fsdp", axis=0, tiled=True),
-        lax.all_gather(decoder_inner, "fsdp", axis=0, tiled=True),
-        lax.all_gather(decoder_outer, "fsdp", axis=0, tiled=True),
-    )
-    (
-        start_full,
-        self_value_full,
-        self_output_full,
-        middle_full,
-        cross_query_full,
-        cross_key_full,
-        cross_value_full,
-        cross_output_full,
-        final_full,
-        decoder_inner_full,
-        decoder_outer_full,
-    ) = decoder_full
     start_full = start_full.astype(jnp.float32)
     middle_full = middle_full.astype(jnp.float32)
     final_full = final_full.astype(jnp.float32)
@@ -263,65 +816,26 @@
     decoder_before = product(normed_fin, decoder_inner_full)
     decoder_active = jax.nn.gelu(decoder_before).astype(jnp.bfloat16)
     decoded_full = second_field + product(decoder_active, decoder_outer_full)
-    decoder_back = (
-        lax.all_gather(start_gain, "fsdp", axis=0, tiled=True),
-        lax.all_gather(self_value, "fsdp", axis=0, tiled=True),
-        lax.all_gather(self_output, "fsdp", axis=0, tiled=True),
-        lax.all_gather(middle_gain, "fsdp", axis=0, tiled=True),
-        lax.all_gather(cross_query, "fsdp", axis=0, tiled=True),
-        lax.all_gather(cross_key, "fsdp", axis=0, tiled=True),
-        lax.all_gather(cross_value, "fsdp", axis=0, tiled=True),
-        lax.all_gather(cross_output, "fsdp", axis=0, tiled=True),
-        lax.all_gather(final_gain, "fsdp", axis=0, tiled=True),
-        lax.all_gather(decoder_inner, "fsdp", axis=0, tiled=True),
-        lax.all_gather(decoder_outer, "fsdp", axis=0, tiled=True),
-    )
-    encoder_back = (
-        lax.all_gather(first_gain, "fsdp", axis=0, tiled=True),
-        lax.all_gather(query_weight, "fsdp", axis=0, tiled=True),
-        lax.all_gather(key_weight, "fsdp", axis=0, tiled=True),
-        lax.all_gather(value_weight, "fsdp", axis=0, tiled=True),
-        lax.all_gather(output_weight, "fsdp", axis=0, tiled=True),
-        lax.all_gather(second_gain, "fsdp", axis=0, tiled=True),
-        lax.all_gather(inner_weight, "fsdp", axis=0, tiled=True),
-        lax.all_gather(outer_weight, "fsdp", axis=0, tiled=True),
-    )
-    (
-        back_start,
-        back_self_value,
-        back_self_output,
-        back_middle,
-        back_cross_query,
-        back_cross_key,
-        back_cross_value,
-        back_cross_output,
-        back_final,
-        back_decoder_inner,
-        back_decoder_outer,
-    ) = decoder_back
-    (
-        back_gain_one,
-        back_query,
-        back_key,
-        back_value,
-        back_output,
-        back_gain_two,
-        back_inner,
-        back_outer,
-    ) = encoder_back
+    back_start, back_middle, back_final = start_full, middle_full, final_full
+    back_gain_one, back_gain_two = gain_one, gain_two
+    back_query, back_key, back_value, back_output = query_full, key_full, value_full, output_full
+    back_inner, back_outer = inner_full, outer_full
+    back_self_value, back_self_output, back_cross_query = self_value_full, self_output_full, cross_query_full
+    back_cross_key, back_cross_value, back_cross_output = cross_key_full, cross_value_full, cross_output_full
+    back_decoder_inner, back_decoder_outer = decoder_inner_full, decoder_outer_full
     grad_second = decoded_cotangent.astype(jnp.float32).reshape(row_count * slot_count, width)
     grad_branch = grad_second.astype(jnp.bfloat16)
-    grad_decoder_outer = product_left(decoder_active, grad_branch)
+    last_branch = grad_branch
     grad_active = product_right(grad_branch, back_decoder_outer)
     grad_before = gelu_back(decoder_before, grad_active).astype(jnp.bfloat16)
-    grad_decoder_inner = product_left(normed_fin, grad_before)
+    decoder_before_grad = grad_before
     grad_normed = product_right(grad_before, back_decoder_inner)
     field_part, grad_final = norm_back(
         grad_normed, second_field, scale_fin, back_final.astype(jnp.float32)
     )
     grad_second = grad_second + field_part
     grad_branch = grad_second.astype(jnp.bfloat16)
-    grad_cross_output = product_left(cross_context, grad_branch)
+    cross_branch = grad_branch
     grad_cross_context = product_right(grad_branch, back_cross_output).astype(jnp.bfloat16)
     ask_parts = []
     key_parts = []
@@ -347,7 +861,6 @@
     grad_asking = jnp.concatenate(ask_parts, axis=0).astype(jnp.bfloat16)
     grad_cross_keys = jnp.concatenate(key_parts, axis=0).astype(jnp.bfloat16)
     grad_cross_values = jnp.concatenate(value_parts, axis=0).astype(jnp.bfloat16)
-    grad_cross_query = product_left(normed_mid, grad_asking)
     grad_cross_key = product_left(memory, grad_cross_keys)
     grad_cross_value = product_left(memory, grad_cross_values)
     grad_memory = product_right(grad_cross_keys, back_cross_key) + product_right(
@@ -359,64 +872,13 @@
     )
     grad_first = grad_second + field_part
     grad_branch = grad_first.astype(jnp.bfloat16)
-    grad_self_output = product_left(own_value, grad_branch)
+    self_branch = grad_branch
     grad_own = product_right(grad_branch, back_self_output).astype(jnp.bfloat16)
-    grad_self_value = product_left(normed_start, grad_own)
     grad_normed = product_right(grad_own, back_self_value)
     field_part, grad_start_gain = norm_back(
         grad_normed, start_field, scale_start, back_start.astype(jnp.float32)
     )
     start_grad = (grad_first + field_part).reshape(row_count, slot_count, width)
-    (
-        start_gain_grad,
-        self_value_grad,
-        self_output_grad,
-        middle_gain_grad,
-        cross_query_grad,
-        cross_key_grad,
-        cross_value_grad,
-        cross_output_grad,
-        final_gain_grad,
-        decoder_inner_grad,
-        decoder_outer_grad,
-    ) = (
-        lax.psum_scatter(grad_start_gain, "fsdp", scatter_dimension=0, tiled=True),
-        lax.psum_scatter(grad_self_value, "fsdp", scatter_dimension=0, tiled=True),
-        lax.psum_scatter(grad_self_output, "fsdp", scatter_dimension=0, tiled=True),
-        lax.psum_scatter(grad_middle, "fsdp", scatter_dimension=0, tiled=True),
-        lax.psum_scatter(grad_cross_query, "fsdp", scatter_dimension=0, tiled=True),
-        lax.psum_scatter(grad_cross_key, "fsdp", scatter_dimension=0, tiled=True),
-        lax.psum_scatter(grad_cross_value, "fsdp", scatter_dimension=0, tiled=True),
-        lax.psum_scatter(grad_cross_output, "fsdp", scatter_dimension=0, tiled=True),
-        lax.psum_scatter(grad_final, "fsdp", scatter_dimension=0, tiled=True),
-        lax.psum_scatter(grad_decoder_inner, "fsdp", scatter_dimension=0, tiled=True),
-        lax.psum_scatter(grad_decoder_outer, "fsdp", scatter_dimension=0, tiled=True),
-    )
-    (
-        start_gain_grad,
-        self_value_grad,
-        self_output_grad,
-        middle_gain_grad,
-        cross_query_grad,
-        cross_key_grad,
-        cross_value_grad,
-        cross_output_grad,
-        final_gain_grad,
-        decoder_inner_grad,
-        decoder_outer_grad,
-    ) = (
-        lax.psum(start_gain_grad.astype(jnp.bfloat16), "dp").astype(jnp.float32),
-        lax.psum(self_value_grad.astype(jnp.bfloat16), "dp").astype(jnp.float32),
-        lax.psum(self_output_grad.astype(jnp.bfloat16), "dp").astype(jnp.float32),
-        lax.psum(middle_gain_grad.astype(jnp.bfloat16), "dp").astype(jnp.float32),
-        lax.psum(cross_query_grad.astype(jnp.bfloat16), "dp").astype(jnp.float32),
-        lax.psum(cross_key_grad.astype(jnp.bfloat16), "dp").astype(jnp.float32),
-        lax.psum(cross_value_grad.astype(jnp.bfloat16), "dp").astype(jnp.float32),
-        lax.psum(cross_output_grad.astype(jnp.bfloat16), "dp").astype(jnp.float32),
-        lax.psum(final_gain_grad.astype(jnp.bfloat16), "dp").astype(jnp.float32),
-        lax.psum(decoder_inner_grad.astype(jnp.bfloat16), "dp").astype(jnp.float32),
-        lax.psum(decoder_outer_grad.astype(jnp.bfloat16), "dp").astype(jnp.float32),
-    )
     grad_encoded = encoded_cotangent.astype(jnp.float32) + grad_memory
     grad_branch = grad_encoded.astype(jnp.bfloat16)
     grad_outer = product_left(active, grad_branch)
@@ -474,45 +936,47 @@
         (((0,), (1,)), ((), ())),
         precision=lax.Precision.HIGHEST,
     )
+    token_count = row_count * slot_count
+    lefts = (normed_fin, decoder_active, normed_start, own_value, normed_mid, cross_context)
+    rights = (decoder_before_grad, last_branch, grad_own, self_branch, grad_asking, cross_branch)
+    pair_shapes = [(left.shape[1] // count, right.shape[1]) for left, right in zip(lefts, rights)]
+    left_cols = []
+    for left, (rows, unused) in zip(lefts, pair_shapes):
+        columns = left.reshape(token_count, count, rows).transpose(1, 0, 2)
+        left_cols.append(jnp.pad(columns, ((0, 0), (0, 0), (0, -rows % 128))))
+    small = jnp.concatenate([
+        jnp.stack([grad_gain_one, grad_gain_two, grad_start_gain, grad_middle, grad_final]),
+        jnp.pad(table_grad.reshape(1, -1), ((0, 2), (0, width - table_grad.size))),
+    ])
+    encoder_grads = (
+        grad_inner, grad_outer, grad_query, grad_key, grad_value, grad_output,
+        grad_cross_key, grad_cross_value,
+    )
+    encoder_sums, decoder_sums, small_sum = reduce_grads(
+        count,
+        ENCODER_KINDS,
+        [
+            g.astype(jnp.bfloat16).reshape(count, g.shape[0] // count, g.shape[1])
+            for g in encoder_grads
+        ],
+        jnp.concatenate(left_cols, axis=2),
+        jnp.concatenate(rights, axis=1),
+        pair_shapes,
+        small,
+    )
     (
-        first_gain_grad,
-        query_weight_grad,
-        key_weight_grad,
-        value_weight_grad,
-        output_weight_grad,
-        second_gain_grad,
-        inner_weight_grad,
-        outer_weight_grad,
-    ) = (
-        lax.psum_scatter(grad_gain_one, "fsdp", scatter_dimension=0, tiled=True),
-        lax.psum_scatter(grad_query, "fsdp", scatter_dimension=0, tiled=True),
-        lax.psum_scatter(grad_key, "fsdp", scatter_dimension=0, tiled=True),
-        lax.psum_scatter(grad_value, "fsdp", scatter_dimension=0, tiled=True),
-        lax.psum_scatter(grad_output, "fsdp", scatter_dimension=0, tiled=True),
-        lax.psum_scatter(grad_gain_two, "fsdp", scatter_dimension=0, tiled=True),
-        lax.psum_scatter(grad_inner, "fsdp", scatter_dimension=0, tiled=True),
-        lax.psum_scatter(grad_outer, "fsdp", scatter_dimension=0, tiled=True),
-    )
+        inner_weight_grad, outer_weight_grad, query_weight_grad, key_weight_grad,
+        value_weight_grad, output_weight_grad, cross_key_grad, cross_value_grad,
+    ) = [part.astype(jnp.float32) for part in encoder_sums]
     (
-        first_gain_grad,
-        query_weight_grad,
-        key_weight_grad,
-        value_weight_grad,
-        output_weight_grad,
-        second_gain_grad,
-        inner_weight_grad,
-        outer_weight_grad,
-    ) = (
-        lax.psum(first_gain_grad.astype(jnp.bfloat16), "dp").astype(jnp.float32),
-        lax.psum(query_weight_grad.astype(jnp.bfloat16), "dp").astype(jnp.float32),
-        lax.psum(key_weight_grad.astype(jnp.bfloat16), "dp").astype(jnp.float32),
-        lax.psum(value_weight_grad.astype(jnp.bfloat16), "dp").astype(jnp.float32),
-        lax.psum(output_weight_grad.astype(jnp.bfloat16), "dp").astype(jnp.float32),
-        lax.psum(second_gain_grad.astype(jnp.bfloat16), "dp").astype(jnp.float32),
-        lax.psum(inner_weight_grad.astype(jnp.bfloat16), "dp").astype(jnp.float32),
-        lax.psum(outer_weight_grad.astype(jnp.bfloat16), "dp").astype(jnp.float32),
-    )
-    position_table_grad = lax.psum(table_grad, ("dp", "fsdp"))
+        decoder_inner_grad, decoder_outer_grad, self_value_grad, self_output_grad,
+        cross_query_grad, cross_output_grad,
+    ) = [part.astype(jnp.float32) for part in decoder_sums]
+    own_gains = lax.dynamic_slice_in_dim(
+        small_sum[:5], lax.axis_index("fsdp") * depth, depth, axis=1
+    )
+    first_gain_grad, second_gain_grad, start_gain_grad, middle_gain_grad, final_gain_grad = own_gains
+    position_table_grad = small_sum[5, : table_grad.size].reshape(table_grad.shape)
     decoded = decoded_full.reshape(row_count, slot_count, width).astype(jnp.bfloat16)
     return (
         encoded_full.astype(jnp.bfloat16),

time: 2330 us -> 702 us (0.30)
  waiting for transfers between devices: 1680 us -> 0 us
  Pallas kernels: 0 us -> 269 us
  blocking collectives: 108 us -> 0 us
  matrix products: 279 us -> 220 us
  other arithmetic: 95.6 us -> 69.3 us
    reduce_scatter x14 -> x0, waiting for transfers between devices: 1140 us -> none  [the longest x1 166 us: on_device(): lax.psum_scatter(grad_outer, 'fsdp', scatter_dimension=0, tiled=True)]
    all_gather x14 -> x0, waiting for transfers between devices: 533 us -> none  [the longest x1 78.3 us: on_device(): lax.all_gather(decoder_inner, 'fsdp', axis=0, tiled=True)]
    pallas_call x0 -> x2, Pallas kernels: none -> 269 us  [the longest x1 146 us: reduce_grads(): pl.pallas_call(functools.partial(reduce_kernel, count, kinds, spans), out...]
    unnamed x2 -> x0, blocking collectives: 59.5 us -> none
    psum x2 -> x0, blocking collectives: 49 us -> none  [the longest x1 36.3 us: on_device(): position_table_grad = lax.psum(table_grad, ('dp', 'fsdp'))]
    dot_general x14 -> x8, matrix products: 63 us -> 35.7 us  [product_left(): lax.dot_general(left, right, (((0,), (0,)), ((), ())), preferred_element_...]
    convert_element_type x36 -> x16, other arithmetic: 45.8 us -> 19 us  [the longest x14 18.2 us: on_device(): part.astype(jnp.float32)]
    unnamed x293 -> x228, local copies, waits for them, and re-layouts: 80.3 us -> 77.5 us
  transfers between devices with their start and end apart: 29 -> 0, of which waited for: 23 -> 0; matrix products, arithmetic and copies ran while one was open for 19% -> 0% of each run, Pallas kernels for 0% -> 0%
where the time goes in v1:
time: 702 us; the launch traced here: 691 us
  Pallas kernels  269 us (38%)
  matrix products  220 us (31%)
  local copies, waits for them, and re-layouts  131 us (19%)
  other arithmetic  69.3 us (10%)
    pallas_call x1, Pallas kernels, reduce_grads(): pl.pallas_call(functools.partial(reduce_kernel, count, kinds, spans), out...  146 us
    pallas_call x1, Pallas kernels, gather_weights(): pl.pallas_call(functools.partial(gather_kernel, count, kinds), out_shape=...  123 us
    unnamed x228, local copies, waits for them, and re-layouts  77.5 us
    dot_general x14, matrix products, product_right(): lax.dot_general(left, right, (((1,), (1,)), ((), ())), preferred_element_...  45.4 us
    dot_general x14, matrix products, product(): return jnp.dot(left, right, preferred_element_type=jnp.float32)  37.5 us
    dot_general x8, matrix products, product_left(): lax.dot_general(left, right, (((0,), (0,)), ((), ())), preferred_element_...  35.7 us
    add x1, other arithmetic, on_device(): bias_grad = bias_grad + grad_scores  26.5 us
    reshape x2, local copies, waits for them, and re-layouts, on_device(): extra = lax.dot_general(position_table, onehot, (((0,), (1,)), ((), ())),...  23.3 us

profile of v1, /device:TPU:1, one launch (start us, length us, event | category | flops | bytes accessed | tf_op | source)
XLA Modules:
  0.0 691.0 jit_solution(18060595873963199001)
XLA Ops:
  8.6 2.1 copy.130
  11.8 2.6 copy.140
  14.5 11.5 %fusion.1 = f32[262144,12]{0,1:T(8,128)S(1)} fusion(f32[32,12]{0,1:T(8,128)S(1)} %copy-done, s32[262144]{0:T(1024)S(1)} %fusion.51), kind=kOutput, calls=%fused_computation.2 | convolution fusion | flops 1216348160 | bytes 13633024 | tf_op jit(solution)/shard_map/dot_general | solution.py:748
  26.0 19.4 %copy.195 = f32[2,8,512,512]{3,2,1,0:T(8,128)} copy(f32[2,8,512,512]{3,1,2,0:T(8,128)S(1)} %bitcast.250) | data formatting | bytes 33554432
  45.4 10.7 %slice.140 = f32[12,512,512]{2,1,0:T(8,128)} slice(f32[16,512,512]{2,1,0:T(8,128)} %bitcast.252), slice={[0:12], [0:512], [0:512]} | slice | bytes 25165824 | tf_op jit(solution)/shard_map/reshape | solution.py:750
  56.1 12.6 %copy.131 = f32[12,512,512]{1,2,0:T(8,128)} copy(f32[12,512,512]{2,1,0:T(8,128)} %slice.140) | data formatting | bytes 25165824 | tf_op jit(solution)/shard_map/reshape | solution.py:750
  68.7 122.9 %gather_weights.1 = (bf16[8,96,768]{2,1,0:T(8,128)(2,1)}, bf16[8,96,768]{2,1,0:T(8,128)(2,1)}, bf16[8,96,768]{2,1,0:T(8,128)(2,1)}, bf16[8,96,768]{2,1,0:T(8,128...) custom-call(bf16[96,768]{1,0:T(8,128)(2,1)} %refs_0_.1, ...), custom_call_target="tpu_custom_call" | custom-call | tf_op jit(solution)/shard_map/gather_weights/pallas_call | solution.py:215
  195.0 1.6 convolution_convert_fusion.29
  197.4 1.7 multiply_reduce_fusion.12
  203.9 1.6 copy-done.77
  205.5 1.6 convolution_convert_fusion.5
  207.3 1.6 copy-done.32
  211.4 6.1 fusion.142
  217.6 13.4 %fusion.143 = (f32[12,512]{1,0:T(8,128)S(1)}, f32[12,512,512]{1,2,0:T(8,128)}) fusion(f32[12,512,512]{1,2,0:T(8,128)} %copy.131, bf16[512,12,64]{0,2,1:T(8,128)(2,1)S(1)} %bitcast.275, bf16[512,12,64]{0,2,1:T(8,128)(2,1)S(1)} %bitcast.263, pred[512,512]{0,1:T(8,128)(4,1)S(1)} %copy-done.34), kind=kOutput, calls=%fused_computation.273 | convolution fusion | flops 412084224 | bytes 27025408 | tf_op jit(solution)/shard_map/qhd,khd->hqk/dot_general | solution.py:641
  231.0 1.8 exponential_reduce_fusion
  232.8 6.3 exponential_reduce_fusion.1
  239.1 2.1 fusion.39
  241.2 6.9 %fusion.33 = bf16[12,64,512]{2,1,0:T(8,128)(2,1)S(1)} fusion(bf16[512,12,64]{0,2,1:T(8,128)(2,1)S(1)} %bitcast.269, f32[12,512,512]{1,2,0:T(8,128)} %get-tuple-element.208, f32[12,512]{1,0:T(8,128)S(1)} %get-tuple-element.239), kind=kOutput, calls=%fused_computation.83 | convolution fusion | flops 409337856 | bytes 14180352 | tf_op jit(solution)/shard_map/hqk,khd->qhd/dot_general | solution.py:659
  248.2 1.6 multiply_reduce_fusion.4
  251.5 5.8 fusion.126
  257.3 4.6 copy-done.8
  261.9 9.0 %add_convert_fusion = bf16[1024,768]{0,1:T(8,128)(2,1)S(1)} fusion(f32[1024,768]{0,1:T(8,128)} %copy-done.9, bf16[3072,768]{1,0:T(8,128)(2,1)} %bitcast.352, f32[1024,3072]{1,0:T(8,128)S(1)} %fusion.126), kind=kOutput, calls=%fused_computation.53 | convolution fusion | flops 4861722624 | bytes 22020096 | tf_op jit(solution)/shard_map/dot_general | solution.py:602
  270.9 1.6 copy.173
  284.2 1.7 multiply_reduce_fusion.11
  289.2 3.2 multiply_convert_fusion.4
  293.3 3.7 fusion.50
  304.3 1.8 multiply_reduce_fusion.8
  307.5 2.5 constant_dynamic-update-slice_fusion.3
  309.9 1.8 fusion.81
  317.2 2.5 convolution_convert_fusion.9
  319.7 2.6 convolution_convert_fusion.8
  324.1 3.0 add_add_fusion.1
  327.1 2.0 slice-done.14
  329.1 17.1 %fusion.10 = bf16[1024,3072]{1,0:T(8,128)(2,1)} fusion(f32[1024,3072]{1,0:T(8,128)S(1)} %bitcast.262, bf16[3072,768]{1,0:T(8,128)(2,1)} %bitcast.353, f32[1024,768]{0,1:T(8,128)} %add_add_fusion.1), kind=kOutput, calls=%fused_computation.13 | convolution fusion | flops 4895539200 | bytes 26738688 | tf_op jit(solution)/shard_map/dot_general | solution.py:612
  346.2 12.1 %convolution_convert_fusion = bf16[3072,768]{1,0:T(8,128)(2,1)} fusion(f32[1024,768]{0,1:T(8,128)} %add_add_fusion.1, f32[1024,3072]{1,0:T(8,128)S(1)} %bitcast.262), kind=kOutput, calls=%fused_computation.33 | convolution fusion | flops 4863295488 | bytes 20447232 | tf_op jit(solution)/shard_map/dot_general | solution.py:606
  358.4 8.3 %multiply_reduce_fusion.2 = (f32[768]{0:T(1024)S(1)}, f32[1024]{0:T(1024)S(1)}, f32[1024,768]{0,1:T(8,128)S(1)}) fusion(f32[1024,768]{0,1:T(8,128)S(1)} %copy-done.10, f32[1024]{0:T(1024)S(1)} %get-tuple-element.198, f32[768]{0:T(1024)S(1)} %reshape.699, bf16[1024,3072]{1,0:T(8,128)(2,1)} %fusion.10, bf16[768,3072]{1,0:T(8,128)(2,1)S(1)} %bitcast.292), kind=kOutput, calls=%fused_computation.48 | convolution fusion | flops 4836554752 | bytes 17315840 | tf_op jit(solution)/shard_map/dot_general | solution.py:612
  366.7 7.3 %convolution_convert_fusion.1 = bf16[768,3072]{1,0:T(8,128)(2,1)} fusion(bf16[1024,3072]{1,0:T(8,128)(2,1)S(1)} %copy-done.85, f32[1024,768]{0,1:T(8,128)S(1)} %copy-done.10, f32[768]{0:T(1024)S(1)} %reshape.699, f32[1024]{0:T(1024)S(1)} %get-tuple-element.198), kind=kOutput, calls=%fused_computation.34 | convolution fusion | flops 4836556800 | bytes 14162944 | tf_op jit(solution)/shard_map/dot_general | solution.py:606
  375.5 2.4 convolution_convert_fusion.10
  380.6 1.9 slice-done.2
  382.5 3.0 fusion.42
  386.4 4.2 fusion.36
  390.6 3.8 convolution_convert_fusion.11
  394.4 8.7 %multiply_reduce_fusion.1 = (f32[12,512]{1,0:T(8,128)S(1)}, f32[12,512,512]{1,2,0:T(8,128)}) fusion(f32[12,512,512]{1,2,0:T(8,128)S(1)} %bitcast.246, f32[12,512]{1,0:T(8,128)S(1)} %get-tuple-element.239, bf16[512,12,64]{0,2,1:T(8,128)(2,1)} %bitcast.274, bf16[512,12,64]{0,2,1:T(8,128)(2,1)} %bitcast.270), kind=kOutput, calls=%fused_computation.17 | convolution fusion | flops 412084224 | bytes 26787840 | tf_op jit(solution)/shard_map/qhd,khd->hqk/dot_general | solution.py:669
  403.0 8.7 %multiply_reduce_fusion = (f32[12,512]{1,0:T(8,128)S(1)}, f32[12,512,512]{1,2,0:T(8,128)}) fusion(f32[12,512,512]{1,2,0:T(8,128)S(1)} %bitcast.244, f32[12,512]{1,0:T(8,128)S(1)} %get-tuple-element.238, bf16[512,12,64]{0,2,1:T(8,128)(2,1)} %bitcast.272, bf16[512,12,64]{0,2,1:T(8,128)(2,1)} %bitcast.268), kind=kOutput, calls=%fused_computation.15 | convolution fusion | flops 412084224 | bytes 26787840 | tf_op jit(solution)/shard_map/qhd,khd->hqk/dot_general | solution.py:669
  411.8 26.5 %fusion.13 = (f32[12,512,512]{1,2,0:T(8,128)}, bf16[12,512,512]{1,2,0:T(8,128)(2,1)}, bf16[12,512,512]{1,2,0:T(8,128)(2,1)}) fusion(f32[12,512,512]{1,2,0:T(8,128)} %get-tuple-element.228, f32[12,512]{1,0:T(8,128)S(1)} %get-tuple-element.227, f32[12,512,512]{1,2,0:T(8,128)} %get-tuple-element.208, f32[12,512]{1,0:T(8,128)S(1)} %get-tuple-element.239, ...), kind=kLoop, calls=%fused_computation.36 | loop fusion | flops 28311552 | bytes 75595776 | tf_op jit(solution)/shard_map/add | solution.py:917
  438.3 12.7 %copy.171 = f32[12,512,512]{2,1,0:T(8,128)} copy(f32[12,512,512]{1,2,0:T(8,128)} %get-tuple-element.171) | data formatting | bytes 25165824 | tf_op jit(solution)/shard_map/add | solution.py:917
  451.1 4.9 convolution_convert_fusion.18
  456.1 4.1 convolution_convert_fusion.20
  460.2 2.0 convolution_convert_fusion.19
  463.6 2.5 convolution_convert_fusion.12
  467.5 2.5 convolution_convert_fusion.13
  471.7 2.0 fusion.24
  474.5 2.4 copy.174
  476.9 12.5 %pad.49 = f32[16,512,512]{2,1,0:T(8,128)} pad(f32[12,512,512]{2,1,0:T(8,128)} %copy.171, f32[]{:T(128)} %constant.24.clone.1), padding=0_4x0_0x0_0 | pad | bytes 29360132
  489.3 15.5 %copy.196 = f32[2,8,512,512]{3,1,2,0:T(8,128)S(1)} copy(f32[2,8,512,512]{3,2,1,0:T(8,128)} %bitcast.251) | data formatting | bytes 33554432
  504.9 17.8 %fusion = f32[32,12]{1,0:T(8,128)S(1)} fusion(f32[12,262144]{1,0:T(8,128)S(1)} %bitcast.249, s32[262144]{0:T(1024)S(1)} %copy-done.7), kind=kOutput, calls=%fused_computation.1 | convolution fusion | flops 1216348160 | bytes 13633024 | tf_op jit(solution)/shard_map/dot_general | solution.py:933
  523.6 145.9 %reduce_grads.1 = (bf16[96,3072]{1,0:T(8,128)(2,1)}, bf16[384,768]{1,0:T(8,128)(2,1)}, bf16[96,768]{1,0:T(8,128)(2,1)}, bf16[96,768]{1,0:T(8,128)(2,1)}, bf16[96...) custom-call(bf16[8,96,3072]{2,1,0:T(8,128)(2,1)} %bitcast.294, ...), custom_call_target="tpu_custom_call" | custom-call | tf_op jit(solution)/shard_map/reduce_grads/pallas_call | solution.py:572
  672.4 1.6 convert_element_type.453
  674.1 1.6 convert_element_type.454
  675.7 1.6 convert_element_type.455
  677.4 1.6 convert_element_type.456
  679.0 1.7 convert_element_type.459
  680.7 1.6 convert_element_type.460
  682.4 1.6 convert_element_type.461
  (349 shorter events, 73.9 us)
Async XLA Ops:
  0.7 13.8 %copy-start = (f32[32,12]{0,1:T(8,128)S(1)}, f32[32,12]{0,1:T(8,128)}, u32[]{:S(2)}) copy-start(f32[32,12]{0,1:T(8,128)} %param.33) | copy-start | bytes 4612
  1.6 192.4 %copy-start.67 = (f32[16]{0:T(128)}, f32[16]{0:T(128)S(1)}, u32[]{:S(2)}) copy-start(f32[16]{0:T(128)S(1)} %rsqrt.64) | copy-start | bytes 196
  8.6 5.9 copy-start.6
  10.7 237.4 %copy-start.3 = (bf16[1024,768]{0,1:T(8,128)(2,1)}, bf16[1024,768]{0,1:T(8,128)(2,1)S(1)}, u32[]{:S(2)}) copy-start(bf16[1024,768]{0,1:T(8,128)(2,1)S(1)} %copy.130) | copy-start | bytes 4718596
  11.8 195.4 %copy-start.58 = (f32[1024]{0:T(1024)}, f32[1024]{0:T(1024)S(1)}, u32[]{:S(2)}) copy-start(f32[1024]{0:T(1024)S(1)} %get-tuple-element.196) | copy-start | bytes 12292
  68.7 126.3 %copy-start.36 = (bf16[2,8,768]{2,1,0:T(8,128)(2,1)S(1)}, bf16[2,8,768]{2,1,0:T(8,128)(2,1)}, u32[]{:S(2)}) copy-start(bf16[2,8,768]{2,1,0:T(8,128)(2,1)} %param.27) | copy-start | bytes 73732
  194.7 7.4 %copy-start.75 = (bf16[8,96,768]{2,1,0:T(8,128)(2,1)S(1)}, bf16[8,96,768]{2,1,0:T(8,128)(2,1)}, u32[]{:S(2)}) copy-start(bf16[8,96,768]{2,1,0:T(8,128)(2,1)} %get-tuple-element.56) | copy-start | bytes 3538948
  194.8 12.5 %copy-start.60 = (f32[768]{0:T(1024)}, f32[768]{0:T(1024)S(1)}, u32[]{:S(2)}) copy-start(f32[768]{0:T(1024)S(1)} %reshape.698) | copy-start | bytes 9220
  202.2 72.5 %copy-start.48 = (bf16[8,12,64]{2,1,0:T(8,128)(2,1)}, bf16[8,12,64]{2,1,0:T(8,128)(2,1)S(1)}, u32[]{:S(2)}) copy-start(bf16[8,12,64]{2,1,0:T(8,128)(2,1)S(1)} %reshape.659) | copy-start | bytes 36868
  203.9 6.7 copy-start.22
  203.9 13.6 %copy-start.20 = (bf16[512,768]{0,1:T(8,128)(2,1)}, bf16[512,768]{0,1:T(8,128)(2,1)S(1)}, u32[]{:S(2)}) copy-start(bf16[512,768]{0,1:T(8,128)(2,1)S(1)} %get-tuple-element.182) | copy-start | bytes 2359300
  207.3 10.3 %copy-start.13 = (bf16[512,768]{0,1:T(8,128)(2,1)}, bf16[512,768]{0,1:T(8,128)(2,1)S(1)}, u32[]{:S(2)}) copy-start(bf16[512,768]{0,1:T(8,128)(2,1)S(1)} %get-tuple-element.180) | copy-start | bytes 2359300
  210.6 28.5 %copy-start.17 = (bf16[512,768]{0,1:T(8,128)(2,1)}, bf16[512,768]{0,1:T(8,128)(2,1)S(1)}, u32[]{:S(2)}) copy-start(bf16[512,768]{0,1:T(8,128)(2,1)S(1)} %get-tuple-element.185) | copy-start | bytes 2359300
  210.6 30.6 %copy-start.18 = (bf16[512,768]{0,1:T(8,128)(2,1)}, bf16[512,768]{0,1:T(8,128)(2,1)S(1)}, u32[]{:S(2)}) copy-start(bf16[512,768]{0,1:T(8,128)(2,1)S(1)} %get-tuple-element.184) | copy-start | bytes 2359300
  211.4 6.1 copy-start.34
  217.5 21.5 %copy-start.2 = (f32[12,512,512]{1,2,0:T(8,128)}, f32[12,512,512]{1,2,0:T(8,128)S(1)}, u32[]{:S(2)}) copy-start(f32[12,512,512]{1,2,0:T(8,128)S(1)} %get-tuple-element.206) | copy-start | bytes 37748740
  239.1 12.4 %slice-start.15 = ((s8[4718592]{0:T(1024)(128)(4,1)}), s8[4194304]{0:T(1024)(128)(4,1)S(1)}, s32[]{:S(2)}) async-start(s8[4718592]{0:T(1024)(128)(4,1)} %bitcast.287), calls=%async_computation.15 | async-start | bytes 8388608
  241.2 7.0 %copy-start.37 = (bf16[12,64,512]{2,1,0:T(8,128)(2,1)}, bf16[12,64,512]{2,1,0:T(8,128)(2,1)S(1)}, u32[]{:S(2)}) copy-start(bf16[12,64,512]{2,1,0:T(8,128)(2,1)S(1)} %fusion.39) | copy-start | bytes 2359300
  241.2 7.0 %copy-start.79 = (bf16[8,96,768]{2,1,0:T(8,128)(2,1)S(1)}, bf16[8,96,768]{2,1,0:T(8,128)(2,1)}, u32[]{:S(2)}) copy-start(bf16[8,96,768]{2,1,0:T(8,128)(2,1)} %get-tuple-element.58) | copy-start | bytes 3538948
  241.2 10.3 %slice-start.16 = ((s8[4718592]{0:T(1024)(128)(4,1)}), s8[524288]{0:T(1024)(128)(4,1)S(1)}, s32[]{:S(2)}) async-start(s8[4718592]{0:T(1024)(128)(4,1)} %bitcast.287), calls=%async_computation.16 | async-start | bytes 1048576
  257.3 4.6 copy-start.8
  278.7 18.4 %slice-start.8 = ((s8[4718592]{0:T(1024)(128)(4,1)}), s8[524288]{0:T(1024)(128)(4,1)S(1)}, s32[]{:S(2)}) async-start(s8[4718592]{0:T(1024)(128)(4,1)} %bitcast.254), calls=%async_computation.8 | async-start | bytes 1048576
  288.4 4.2 copy-start.55
  288.4 4.2 copy-start.56
  289.2 7.9 %slice-start.9 = ((s8[4718592]{0:T(1024)(128)(4,1)}), s8[4194304]{0:T(1024)(128)(4,1)S(1)}, s32[]{:S(2)}) async-start(s8[4718592]{0:T(1024)(128)(4,1)} %bitcast.254), calls=%async_computation.9 | async-start | bytes 8388608
  289.2 9.3 %slice-start.10 = ((s8[4718592]{0:T(1024)(128)(4,1)}), s8[4194304]{0:T(1024)(128)(4,1)S(1)}, s32[]{:S(2)}) async-start(s8[4718592]{0:T(1024)(128)(4,1)} %bitcast.258), calls=%async_computation.10 | async-start | bytes 8388608
  292.5 4.6 copy-start.47
  293.3 5.2 slice-start.11
  302.9 7.1 %copy-start.68 = (f32[16]{0:T(128)S(1)}, f32[16]{0:T(128)}, u32[]{:S(2)}) copy-start(f32[16]{0:T(128)} %copy-done.67) | copy-start | bytes 196
  303.7 11.1 %copy-start.73 = (f32[16]{0:T(128)S(1)}, f32[16]{0:T(128)}, u32[]{:S(2)}) copy-start(f32[16]{0:T(128)} %multiply_multiply_fusion.6) | copy-start | bytes 196
  304.3 12.1 %copy-start.49 = (bf16[8,12,64]{2,1,0:T(8,128)(2,1)S(1)}, bf16[8,12,64]{2,1,0:T(8,128)(2,1)}, u32[]{:S(2)}) copy-start(bf16[8,12,64]{2,1,0:T(8,128)(2,1)} %copy-done.48) | copy-start | bytes 36868
  307.5 9.7 %copy-start.31 = (bf16[1024,768]{0,1:T(8,128)(2,1)S(1)}, bf16[1024,768]{0,1:T(8,128)(2,1)}, u32[]{:S(2)}) copy-start(bf16[1024,768]{0,1:T(8,128)(2,1)} %copy-done.29) | copy-start | bytes 4718596
  322.3 4.8 slice-start.12
  324.1 5.0 slice-start.14
  324.1 34.3 %slice-start.17 = ((s8[4718592]{0:T(1024)(128)(4,1)}), s8[4194304]{0:T(1024)(128)(4,1)S(1)}, s32[]{:S(2)}) async-start(s8[4718592]{0:T(1024)(128)(4,1)} %bitcast.290), calls=%async_computation.17 | async-start | bytes 8388608
  329.1 29.3 %slice-start.18 = ((s8[4718592]{0:T(1024)(128)(4,1)}), s8[524288]{0:T(1024)(128)(4,1)S(1)}, s32[]{:S(2)}) async-start(s8[4718592]{0:T(1024)(128)(4,1)} %bitcast.290), calls=%async_computation.18 | async-start | bytes 1048576
  346.2 12.2 %copy-start.10 = (f32[1024,768]{0,1:T(8,128)S(1)}, f32[1024,768]{0,1:T(8,128)}, u32[]{:S(2)}) copy-start(f32[1024,768]{0,1:T(8,128)} %copy-done.9) | copy-start | bytes 9437188
  358.4 8.3 %copy-start.85 = (bf16[1024,3072]{1,0:T(8,128)(2,1)S(1)}, bf16[1024,3072]{1,0:T(8,128)(2,1)}, u32[]{:S(2)}) copy-start(bf16[1024,3072]{1,0:T(8,128)(2,1)} %fusion.10) | copy-start | bytes 18874372
  366.7 7.4 %copy-start.25 = (f32[1024,768]{0,1:T(8,128)S(1)}, f32[1024,768]{0,1:T(8,128)}, u32[]{:S(2)}) copy-start(f32[1024,768]{0,1:T(8,128)} %add_add_fusion.1) | copy-start | bytes 9437188
  366.7 7.4 %copy-start.63 = (f32[1024]{0:T(1024)S(1)}, f32[1024]{0:T(1024)}, u32[]{:S(2)}) copy-start(f32[1024]{0:T(1024)} %get-tuple-element.197) | copy-start | bytes 12292
  375.5 4.9 slice-start
  375.5 5.1 slice-start.1
  377.9 4.5 slice-start.2
  377.9 7.5 %slice-start.3 = ((s8[12582912]{0:T(1024)(128)(4,1)}), s8[4194304]{0:T(1024)(128)(4,1)S(1)}, s32[]{:S(2)}) async-start(s8[12582912]{0:T(1024)(128)(4,1)} %bitcast.245), calls=%async_computation.3 | async-start | bytes 8388608
  377.9 7.5 %slice-start.4 = ((s8[12582912]{0:T(1024)(128)(4,1)}), s8[4194304]{0:T(1024)(128)(4,1)S(1)}, s32[]{:S(2)}) async-start(s8[12582912]{0:T(1024)(128)(4,1)} %bitcast.245), calls=%async_computation.4 | async-start | bytes 8388608
  380.4 5.1 copy-start.19
  386.4 4.2 copy-start.4
  386.4 4.2 copy-start.59
  386.4 4.2 copy-start.61
  438.3 12.8 %copy-start.23 = (bf16[512,768]{0,1:T(8,128)(2,1)S(1)}, bf16[512,768]{0,1:T(8,128)(2,1)}, u32[]{:S(2)}) copy-start(bf16[512,768]{0,1:T(8,128)(2,1)} %copy-done.22) | copy-start | bytes 2359300
  451.1 4.9 copy-start.16
  451.1 9.0 %slice-start.6 = ((s8[6291456]{0:T(1024)(128)(4,1)}), s8[4194304]{0:T(1024)(128)(4,1)S(1)}, s32[]{:S(2)}) async-start(s8[6291456]{0:T(1024)(128)(4,1)} %bitcast.247), calls=%async_computation.6 | async-start | bytes 8388608
  489.3 15.5 %copy-start.7 = (s32[262144]{0:T(1024)S(1)}, s32[262144]{0:T(1024)}, u32[]{:S(2)}) copy-start(s32[262144]{0:T(1024)} %copy-done.6) | copy-start | bytes 3145732
  504.9 18.0 %copy-start.64 = (f32[1,768]{1,0:T(1,128)S(1)}, f32[1,768]{1,0:T(1,128)}, u32[]{:S(2)}) copy-start(f32[1,768]{1,0:T(1,128)} %stack.43) | copy-start | bytes 9220
  504.9 18.0 %copy-start.65 = (f32[1,768]{1,0:T(1,128)S(1)}, f32[1,768]{1,0:T(1,128)}, u32[]{:S(2)}) copy-start(f32[1,768]{1,0:T(1,128)} %stack.42) | copy-start | bytes 9220
  504.9 18.0 %copy-start.66 = (f32[1,768]{1,0:T(1,128)S(1)}, f32[1,768]{1,0:T(1,128)}, u32[]{:S(2)}) copy-start(f32[1,768]{1,0:T(1,128)} %stack.41) | copy-start | bytes 9220
  669.5 14.6 %copy-start.52 = (bf16[96,768]{1,0:T(8,128)(2,1)S(1)}, bf16[96,768]{1,0:T(8,128)(2,1)}, u32[]{:S(2)}) copy-start(bf16[96,768]{1,0:T(8,128)(2,1)} %get-tuple-element.79) | copy-start | bytes 442372
  669.5 15.3 %copy-start.51 = (bf16[96,768]{1,0:T(8,128)(2,1)S(1)}, bf16[96,768]{1,0:T(8,128)(2,1)}, u32[]{:S(2)}) copy-start(bf16[96,768]{1,0:T(8,128)(2,1)} %get-tuple-element.80) | copy-start | bytes 442372
  669.5 16.0 %copy-start.50 = (bf16[96,768]{1,0:T(8,128)(2,1)S(1)}, bf16[96,768]{1,0:T(8,128)(2,1)}, u32[]{:S(2)}) copy-start(bf16[96,768]{1,0:T(8,128)(2,1)} %get-tuple-element.81) | copy-start | bytes 442372
  669.5 16.7 %copy-start.44 = (bf16[96,3072]{1,0:T(8,128)(2,1)S(1)}, bf16[96,3072]{1,0:T(8,128)(2,1)}, u32[]{:S(2)}) copy-start(bf16[96,3072]{1,0:T(8,128)(2,1)} %get-tuple-element.74) | copy-start | bytes 1769476
  669.5 17.8 %copy-start.43 = (bf16[384,768]{1,0:T(8,128)(2,1)S(1)}, bf16[384,768]{1,0:T(8,128)(2,1)}, u32[]{:S(2)}) copy-start(bf16[384,768]{1,0:T(8,128)(2,1)} %get-tuple-element.75) | copy-start | bytes 1769476
  679.0 9.4 %copy-start.42 = (bf16[96,3072]{1,0:T(8,128)(2,1)S(1)}, bf16[96,3072]{1,0:T(8,128)(2,1)}, u32[]{:S(2)}) copy-start(bf16[96,3072]{1,0:T(8,128)(2,1)} %get-tuple-element.82) | copy-start | bytes 1769476
  684.7 4.8 copy-start.41
  685.5 5.2 copy-start.1
  (41 other events, 90.4 us)

commit v2 on v1

--- a/solution.py
+++ b/solution.py
@@ -9,6 +9,7 @@
 
 HEADS = 12
 KV = 64
+BLOCK = 128
 
 
 epsilon = 1e-06
@@ -583,21 +584,6 @@
     return got[:total], got[total : total + pairs], got[-1]
 
 
-def relative_buckets(length):
-    places = jnp.arange(length, dtype=jnp.int32)
-    offset = places[None, :] - places[:, None]
-    distance = jnp.abs(offset)
-    far_bucket = 8 + sum(((distance >= boundary).astype(jnp.int32) for boundary in bucket_edges))
-    near_bucket = jnp.where(distance < 8, distance, far_bucket)
-    return jnp.where(offset > 0, 16, 0) + near_bucket
-
-
-def bucket_onehot(length, bucket_count):
-    flat_buckets = relative_buckets(length).reshape(length * length)
-    choices_row = jnp.arange(bucket_count, dtype=jnp.int32)
-    return (flat_buckets[:, None] == choices_row[None, :]).astype(jnp.float32)
-
-
 def product(left, right):
     return jnp.dot(left, right, preferred_element_type=jnp.float32)
 
@@ -632,62 +618,304 @@
     return (field_grad, gain_grad)
 
 
-def split_heads(matrix):
-    return matrix.reshape(matrix.shape[0], HEADS, KV)
-
-
-def masked_scores(asking, key_rows, extra, allowed):
-    scores = (
-        jnp.einsum(
-            "qhd,khd->hqk",
-            split_heads(asking),
-            split_heads(key_rows),
-            preferred_element_type=jnp.float32,
+def wide_heads(block):
+    first = lax.broadcasted_iota(jnp.int32, block.shape, 1) < KV
+    none = jnp.zeros_like(block)
+    return jnp.concatenate([jnp.where(first, block, none), jnp.where(first, none, block)], axis=0)
+
+
+def narrow_heads(stacked):
+    half = stacked.shape[0] // 2
+    first = lax.broadcasted_iota(jnp.int32, (half, stacked.shape[1]), 1) < KV
+    return jnp.where(first, stacked[:half], stacked[half:])
+
+
+def reach(at, blocks):
+    low, high = max(0, at - 1), min(blocks, at + 2)
+    begin = (low - at + 1) * BLOCK
+    return slice(low * BLOCK, high * BLOCK), slice(begin, begin + (high - low) * BLOCK)
+
+
+def bias_block(base):
+    heads = []
+    for at in range(2):
+        level = jnp.broadcast_to(base[at : at + 1], (BLOCK, base.shape[1]))
+        heads.append(pltpu.roll(level, 0, axis=1, stride=1, stride_axis=0))
+    return jnp.concatenate(heads, axis=0)
+
+
+def offset_sums(block):
+    rows, width = block.shape
+    while rows > 8:
+        rows = rows // 2
+        block = block[:rows] + pltpu.roll(block[rows:], width - rows, axis=1)
+    place = lax.broadcasted_iota(jnp.int32, block.shape, 0)
+    for bit in (4, 2, 1):
+        block = jnp.where((place & bit) > 0, pltpu.roll(block, width - bit, axis=1), block)
+    return jnp.sum(block, axis=0, keepdims=True)
+
+
+def attend_kernel(column_ref, row_ref, base_ref, query_ref, key_ref, value_ref, out_ref, share_ref):
+    blocks = query_ref.shape[0] // BLOCK
+    bias = bias_block(base_ref[0])
+    for at in range(blocks):
+        keys, places = reach(at, blocks)
+        own = slice(at * BLOCK, (at + 1) * BLOCK)
+        scores = product_right(wide_heads(query_ref[own]), key_ref[keys]) + bias[:, places]
+        allowed = column_ref[own, :1] == row_ref[0, :1, keys]
+        scores = jnp.where(jnp.concatenate([allowed, allowed], axis=0), scores, negative_fill)
+        powers = jnp.exp(scores - jnp.max(scores, axis=1, keepdims=True))
+        shares = powers * (1.0 / jnp.sum(powers, axis=1, keepdims=True))
+        shares = shares.astype(jnp.bfloat16)
+        share_ref[0, 0, at, :, places] = shares
+        mixed = product(shares, value_ref[keys])
+        out_ref[own] = narrow_heads(mixed).astype(jnp.bfloat16)
+
+
+def attend_back_kernel(
+    query_ref, key_ref, value_ref, grad_ref, share_ref,
+    grad_query_ref, grad_key_ref, grad_value_ref, sums_ref, bias_acc, key_acc, value_acc,
+):
+    blocks = query_ref.shape[0] // BLOCK
+
+    @pl.when(pl.program_id(1) == 0)
+    def _():
+        bias_acc[...] = jnp.zeros_like(bias_acc)
+
+    key_acc[...] = jnp.zeros_like(key_acc)
+    value_acc[...] = jnp.zeros_like(value_acc)
+    for at in range(blocks):
+        keys, places = reach(at, blocks)
+        own = slice(at * BLOCK, (at + 1) * BLOCK)
+        query, grad = wide_heads(query_ref[own]), wide_heads(grad_ref[own])
+        narrow_shares = share_ref[0, 0, at, :, places]
+        shares = narrow_shares.astype(jnp.float32)
+        value_acc[keys] += product_left(narrow_shares, grad)
+        moved = shares * product_right(grad, value_ref[keys])
+        grad_scores = moved - shares * jnp.sum(moved, axis=1, keepdims=True)
+        bias_acc[:, places] += grad_scores
+        narrow = grad_scores.astype(jnp.bfloat16)
+        grad_query_ref[own] = narrow_heads(product(narrow, key_ref[keys])).astype(jnp.bfloat16)
+        key_acc[keys] += product_left(narrow, query)
+    grad_key_ref[...] = key_acc[...].astype(jnp.bfloat16)
+    grad_value_ref[...] = value_acc[...].astype(jnp.bfloat16)
+
+    @pl.when(pl.program_id(1) == pl.num_programs(1) - 1)
+    def _():
+        sums_ref[0] = jnp.concatenate(
+            [offset_sums(bias_acc[:BLOCK]), offset_sums(bias_acc[BLOCK:])], axis=0
         )
-        + extra
-    )
-    return jnp.where(allowed[None], scores, negative_fill)
-
-
-def attend_forward(asking, key_rows, value_rows, extra, allowed):
-    scores = masked_scores(asking, key_rows, extra, allowed)
-    highest_score = jnp.max(scores, axis=-1, keepdims=True)
-    log_total = highest_score + jnp.log(
-        jnp.sum(jnp.exp(scores - highest_score), axis=-1, keepdims=True)
-    )
-    shares = jnp.exp(scores - log_total).astype(jnp.bfloat16)
-    mixed = jnp.einsum(
-        "hqk,khd->qhd", shares, split_heads(value_rows), preferred_element_type=jnp.float32
-    )
-    return (mixed.reshape(asking.shape[0], HEADS * KV).astype(jnp.bfloat16), log_total)
-
-
-def attend_backward(asking, key_rows, value_rows, extra, allowed, log_total, grad_mixed):
-    scores = masked_scores(asking, key_rows, extra, allowed)
-    shares = jnp.exp(scores - log_total)
-    grad_heads = split_heads(grad_mixed)
-    grad_shares = jnp.einsum(
-        "qhd,khd->hqk", grad_heads, split_heads(value_rows), preferred_element_type=jnp.float32
-    )
-    grad_value = jnp.einsum(
-        "hqk,qhd->khd", shares.astype(jnp.bfloat16), grad_heads, preferred_element_type=jnp.float32
-    )
-    grad_scores = shares * (grad_shares - jnp.sum(shares * grad_shares, axis=-1, keepdims=True))
-    narrow = grad_scores.astype(jnp.bfloat16)
-    grad_query = jnp.einsum(
-        "hqk,khd->qhd", narrow, split_heads(key_rows), preferred_element_type=jnp.float32
-    )
-    grad_key = jnp.einsum(
-        "hqk,qhd->khd", narrow, split_heads(asking), preferred_element_type=jnp.float32
-    )
-    query_count = asking.shape[0]
-    key_count = key_rows.shape[0]
-    return (
-        grad_query.reshape(query_count, HEADS * KV),
-        grad_key.reshape(key_count, HEADS * KV),
-        grad_value.reshape(key_count, HEADS * KV),
-        grad_scores,
-    )
+
+
+def offset_buckets():
+    offset = jnp.arange(3 * BLOCK, dtype=jnp.int32) - BLOCK
+    distance = jnp.abs(offset)
+    far_bucket = 8 + sum(((distance >= boundary).astype(jnp.int32) for boundary in bucket_edges))
+    near_bucket = jnp.where(distance < 8, distance, far_bucket)
+    return jnp.where(offset > 0, 16, 0) + near_bucket
+
+
+def attend_rows(rows, length, column, segment_index, base, query, key, value):
+    pairs = HEADS // 2
+    part = pl.BlockSpec((length, 2 * KV), lambda r, p: (r, p))
+    return pl.pallas_call(
+        attend_kernel,
+        grid=(rows, pairs),
+        out_shape=[
+            jax.ShapeDtypeStruct(query.shape, jnp.bfloat16),
+            jax.ShapeDtypeStruct(
+                (rows, pairs, length // BLOCK, 2 * BLOCK, 3 * BLOCK), jnp.bfloat16
+            ),
+        ],
+        in_specs=[
+            pl.BlockSpec((length, BLOCK), lambda r, p: (r, 0)),
+            pl.BlockSpec((1, 1, length), lambda r, p: (r, 0, 0)),
+            pl.BlockSpec((1, 2, 3 * BLOCK), lambda r, p: (p, 0, 0)),
+            part, part, part,
+        ],
+        out_specs=[
+            part,
+            pl.BlockSpec(
+                (1, 1, length // BLOCK, 2 * BLOCK, 3 * BLOCK), lambda r, p: (r, p, 0, 0, 0)
+            ),
+        ],
+        compiler_params=pltpu.CompilerParams(vmem_limit_bytes=48 * 2**20),
+        name="attend",
+    )(column, segment_index.reshape(rows, 1, length), base, query, key, value)
+
+
+def attend_rows_back(rows, length, query, key, value, grad, shares):
+    pairs = HEADS // 2
+    part = pl.BlockSpec((length, 2 * KV), lambda p, r: (r, p))
+    return pl.pallas_call(
+        attend_back_kernel,
+        grid=(pairs, rows),
+        out_shape=[jax.ShapeDtypeStruct(query.shape, jnp.bfloat16)] * 3
+        + [jax.ShapeDtypeStruct((pairs, 2, 3 * BLOCK), jnp.float32)],
+        in_specs=[
+            part, part, part, part,
+            pl.BlockSpec(
+                (1, 1, length // BLOCK, 2 * BLOCK, 3 * BLOCK), lambda p, r: (r, p, 0, 0, 0)
+            ),
+        ],
+        out_specs=[part, part, part, pl.BlockSpec((1, 2, 3 * BLOCK), lambda p, r: (p, 0, 0))],
+        scratch_shapes=[
+            pltpu.VMEM((2 * BLOCK, 3 * BLOCK), jnp.float32),
+            pltpu.VMEM((length, 2 * KV), jnp.float32),
+            pltpu.VMEM((length, 2 * KV), jnp.float32),
+        ],
+        compiler_params=pltpu.CompilerParams(vmem_limit_bytes=48 * 2**20),
+        name="attend_back",
+    )(query, key, value, grad, shares)
+
+
+def gelu_parts(before):
+    slope = 0.7978845608028654
+    square = before * before
+    bend = jnp.tanh(slope * (before + 0.044715 * before * square))
+    half = 0.5 * (1.0 + bend)
+    rise = half + 0.5 * before * (1.0 - bend * bend) * slope * (1.0 + 3 * 0.044715 * square)
+    return before * half, rise
+
+
+def slots_of(stacked, count):
+    rows, columns = stacked.shape
+    own = lax.broadcasted_iota(jnp.int32, (rows, columns), 0) // count
+    head = lax.broadcasted_iota(jnp.int32, (rows, columns), 1) // KV
+    return jnp.where(own == head, stacked, 0.0)
+
+
+def decoder_kernel(rows, slots, *refs):
+    (
+        segment_ref, start_ref, cotangent_ref, gain_ref, keys_ref, values_ref,
+        self_value_hbm, self_output_hbm, cross_query_hbm, cross_output_hbm,
+        inner_hbm, outer_hbm,
+        decoded_ref, start_grad_ref, gain_grad_ref,
+        normed_fin_ref, active_ref, normed_start_ref, own_ref, normed_mid_ref, context_ref,
+        before_grad_ref, last_branch_ref, grad_own_ref, self_branch_ref, grad_asking_ref,
+        cross_branch_ref, grad_keys_ref, grad_values_ref,
+        self_value, self_output, cross_query, cross_output, inner, outer, sems,
+    ) = refs
+    loads = []
+    for at, (source, target) in enumerate((
+        (self_value_hbm, self_value), (self_output_hbm, self_output),
+        (cross_query_hbm, cross_query), (cross_output_hbm, cross_output),
+        (inner_hbm, inner), (outer_hbm, outer),
+    )):
+        loads.append(pltpu.make_async_copy(source, target, sems.at[at]))
+        loads[-1].start()
+    narrow = jnp.bfloat16
+    length = keys_ref.shape[0] // rows
+    start_gain, middle_gain, final_gain = gain_ref[0:1], gain_ref[1:2], gain_ref[2:3]
+
+    start_field = start_ref[...].astype(jnp.float32)
+    scale_start = root_scale(start_field)
+    normed_start = (start_field * scale_start * start_gain).astype(narrow)
+    normed_start_ref[...] = normed_start
+    loads[0].wait()
+    own = product(normed_start, self_value[...]).astype(narrow)
+    own_ref[...] = own
+    loads[1].wait()
+    first_field = start_field + product(own, self_output[...])
+    scale_mid = root_scale(first_field)
+    normed_mid = (first_field * scale_mid * middle_gain).astype(narrow)
+    normed_mid_ref[...] = normed_mid
+    loads[2].wait()
+    asking = product(normed_mid, cross_query[...]).astype(narrow).astype(jnp.float32)
+    wides, all_shares, contexts = [], [], []
+    for row in range(rows):
+        part = asking[row * slots : (row + 1) * slots]
+        wide = slots_of(jnp.concatenate([part] * HEADS, axis=0), slots).astype(narrow)
+        span = slice(row * length, (row + 1) * length)
+        scores = product_right(wide, keys_ref[span])
+        slot = lax.rem(lax.broadcasted_iota(jnp.int32, scores.shape, 0), slots)
+        scores = jnp.where(slot == segment_ref[row : row + 1], scores, negative_fill)
+        powers = jnp.exp(scores - jnp.max(scores, axis=1, keepdims=True))
+        shares = powers * (1.0 / jnp.sum(powers, axis=1, keepdims=True))
+        mixed = slots_of(product(shares.astype(narrow), values_ref[span]), slots)
+        contexts.append(jnp.sum(mixed.reshape(HEADS, slots, -1), axis=0))
+        wides.append(wide)
+        all_shares.append(shares)
+    context = jnp.concatenate(contexts, axis=0).astype(narrow)
+    context_ref[...] = context
+    loads[3].wait()
+    second_field = first_field + product(context, cross_output[...])
+    scale_fin = root_scale(second_field)
+    normed_fin = (second_field * scale_fin * final_gain).astype(narrow)
+    normed_fin_ref[...] = normed_fin
+    loads[4].wait()
+    active, rise = gelu_parts(product(normed_fin, inner[...]))
+    active = active.astype(narrow)
+    active_ref[...] = active
+    loads[5].wait()
+    decoded_ref[...] = (second_field + product(active, outer[...])).astype(narrow)
+
+    branch = cotangent_ref[...]
+    last_branch_ref[...] = branch
+    grad_second = branch.astype(jnp.float32)
+    before_grad = (product_right(branch, outer[...]) * rise).astype(narrow)
+    before_grad_ref[...] = before_grad
+    grad_normed = product_right(before_grad, inner[...])
+    moved, final_gain_grad = norm_back(grad_normed, second_field, scale_fin, final_gain)
+    grad_second = grad_second + moved
+    branch = grad_second.astype(narrow)
+    cross_branch_ref[...] = branch
+    grad_context = product_right(branch, cross_output[...]).astype(narrow).astype(jnp.float32)
+    askings = []
+    for row in range(rows):
+        part = grad_context[row * slots : (row + 1) * slots]
+        wide = slots_of(jnp.concatenate([part] * HEADS, axis=0), slots).astype(narrow)
+        span = slice(row * length, (row + 1) * length)
+        shares = all_shares[row]
+        moved = shares * product_right(wide, values_ref[span])
+        grad_scores = moved - shares * jnp.sum(moved, axis=1, keepdims=True)
+        grad_scores = grad_scores.astype(narrow)
+        grad_values_ref[span] = product_left(shares.astype(narrow), wide).astype(narrow)
+        grad_keys_ref[span] = product_left(grad_scores, wides[row]).astype(narrow)
+        mixed = slots_of(product(grad_scores, keys_ref[span]), slots)
+        askings.append(jnp.sum(mixed.reshape(HEADS, slots, -1), axis=0))
+    grad_asking = jnp.concatenate(askings, axis=0).astype(narrow)
+    grad_asking_ref[...] = grad_asking
+    grad_normed = product_right(grad_asking, cross_query[...])
+    moved, middle_gain_grad = norm_back(grad_normed, first_field, scale_mid, middle_gain)
+    grad_first = grad_second + moved
+    branch = grad_first.astype(narrow)
+    self_branch_ref[...] = branch
+    grad_own = product_right(branch, self_output[...]).astype(narrow)
+    grad_own_ref[...] = grad_own
+    grad_normed = product_right(grad_own, self_value[...])
+    moved, start_gain_grad = norm_back(grad_normed, start_field, scale_start, start_gain)
+    start_grad_ref[...] = grad_first + moved
+    gain_grad_ref[...] = jnp.concatenate(
+        [start_gain_grad[None], middle_gain_grad[None], final_gain_grad[None]], axis=0
+    )
+
+
+def decode(segment_index, start, cotangent, gains, keys, values, weights):
+    rows, tokens, width = segment_index.shape[0], start.shape[0], start.shape[1]
+    narrow, hidden = jnp.bfloat16, weights[4].shape[1]
+    few = jax.ShapeDtypeStruct((tokens, width), narrow)
+    many = jax.ShapeDtypeStruct((tokens, hidden), narrow)
+    outs = [
+        few,
+        jax.ShapeDtypeStruct((tokens, width), jnp.float32),
+        jax.ShapeDtypeStruct((3, width), jnp.float32),
+        few, many, few, few, few, few,
+        many, few, few, few, few, few,
+        jax.ShapeDtypeStruct(keys.shape, narrow),
+        jax.ShapeDtypeStruct(values.shape, narrow),
+    ]
+    local = pl.BlockSpec(memory_space=pltpu.VMEM)
+    return pl.pallas_call(
+        functools.partial(decoder_kernel, rows, tokens // rows),
+        out_shape=outs,
+        in_specs=[local] * 6 + [pl.BlockSpec(memory_space=pl.ANY)] * 6,
+        out_specs=[local] * len(outs),
+        scratch_shapes=[pltpu.VMEM(w.shape, narrow) for w in weights]
+        + [pltpu.SemaphoreType.DMA((6,))],
+        compiler_params=pltpu.CompilerParams(vmem_limit_bytes=48 * 2**20),
+        name="decode",
+    )(segment_index, start, cotangent, gains, keys, values, *weights)
 
 
 def on_device(
@@ -744,33 +972,20 @@
     gain_one, gain_two, start_full, middle_full, final_full = gain_set
     gain_one = gain_one.astype(jnp.float32)
     gain_two = gain_two.astype(jnp.float32)
-    onehot = bucket_onehot(length, position_table.shape[0])
-    extra = lax.dot_general(
-        position_table, onehot, (((0,), (1,)), ((), ())), precision=lax.Precision.HIGHEST
-    ).reshape(HEADS, length, length)
+    choices = jnp.arange(position_table.shape[0], dtype=jnp.int32)
+    onehot = (offset_buckets()[None, :] == choices[:, None]).astype(jnp.float32)
+    base = jnp.dot(position_table.T, onehot, precision=lax.Precision.HIGHEST)
+    base = base.reshape(HEADS // 2, 2, 3 * BLOCK)
+    column = jnp.broadcast_to(segment_index.reshape(-1, 1), (row_count * length, BLOCK))
     field = tokens.astype(jnp.float32)
     scale_one = root_scale(field)
     normed_one = (field * scale_one * gain_one).astype(jnp.bfloat16)
     query_all = product(normed_one, query_full).astype(jnp.bfloat16)
     key_all = product(normed_one, key_full).astype(jnp.bfloat16)
     value_all = product(normed_one, value_full).astype(jnp.bfloat16)
-    contexts = []
-    kept_totals = []
-    for row_index in range(row_count):
-        row_begin = row_index * length
-        row_end = row_begin + length
-        segment_row = segment_index[row_index]
-        allowed = segment_row[:, None] == segment_row[None, :]
-        mixed, log_total = attend_forward(
-            query_all[row_begin:row_end],
-            key_all[row_begin:row_end],
-            value_all[row_begin:row_end],
-            extra,
-            allowed,
-        )
-        contexts.append(mixed)
-        kept_totals.append(log_total)
-    context = jnp.concatenate(contexts, axis=0)
+    context, shares = attend_rows(
+        row_count, length, column, segment_index, base, query_all, key_all, value_all
+    )
     hidden = field + product(context, output_full)
     scale_two = root_scale(hidden)
     normed_two = (hidden * scale_two * gain_two).astype(jnp.bfloat16)
@@ -781,104 +996,35 @@
     start_full = start_full.astype(jnp.float32)
     middle_full = middle_full.astype(jnp.float32)
     final_full = final_full.astype(jnp.float32)
-    start_field = start_vectors.astype(jnp.float32).reshape(row_count * slot_count, width)
-    scale_start = root_scale(start_field)
-    normed_start = (start_field * scale_start * start_full).astype(jnp.bfloat16)
-    own_value = product(normed_start, self_value_full).astype(jnp.bfloat16)
-    first_field = start_field + product(own_value, self_output_full)
-    scale_mid = root_scale(first_field)
-    normed_mid = (first_field * scale_mid * middle_full).astype(jnp.bfloat16)
-    asking = product(normed_mid, cross_query_full).astype(jnp.bfloat16)
     cross_keys = product(memory, cross_key_full).astype(jnp.bfloat16)
     cross_values = product(memory, cross_value_full).astype(jnp.bfloat16)
-    slot_index = jnp.arange(slot_count, dtype=jnp.int32)
-    cross_parts = []
-    cross_totals = []
-    for row_index in range(row_count):
-        row_begin = row_index * length
-        row_end = row_begin + length
-        slot_begin = row_index * slot_count
-        slot_end = slot_begin + slot_count
-        allowed = slot_index[:, None] == segment_index[row_index][None, :]
-        mixed, log_total = attend_forward(
-            asking[slot_begin:slot_end],
-            cross_keys[row_begin:row_end],
-            cross_values[row_begin:row_end],
-            0.0,
-            allowed,
-        )
-        cross_parts.append(mixed)
-        cross_totals.append(log_total)
-    cross_context = jnp.concatenate(cross_parts, axis=0)
-    second_field = first_field + product(cross_context, cross_output_full)
-    scale_fin = root_scale(second_field)
-    normed_fin = (second_field * scale_fin * final_full).astype(jnp.bfloat16)
-    decoder_before = product(normed_fin, decoder_inner_full)
-    decoder_active = jax.nn.gelu(decoder_before).astype(jnp.bfloat16)
-    decoded_full = second_field + product(decoder_active, decoder_outer_full)
-    back_start, back_middle, back_final = start_full, middle_full, final_full
     back_gain_one, back_gain_two = gain_one, gain_two
     back_query, back_key, back_value, back_output = query_full, key_full, value_full, output_full
     back_inner, back_outer = inner_full, outer_full
-    back_self_value, back_self_output, back_cross_query = self_value_full, self_output_full, cross_query_full
-    back_cross_key, back_cross_value, back_cross_output = cross_key_full, cross_value_full, cross_output_full
-    back_decoder_inner, back_decoder_outer = decoder_inner_full, decoder_outer_full
-    grad_second = decoded_cotangent.astype(jnp.float32).reshape(row_count * slot_count, width)
-    grad_branch = grad_second.astype(jnp.bfloat16)
-    last_branch = grad_branch
-    grad_active = product_right(grad_branch, back_decoder_outer)
-    grad_before = gelu_back(decoder_before, grad_active).astype(jnp.bfloat16)
-    decoder_before_grad = grad_before
-    grad_normed = product_right(grad_before, back_decoder_inner)
-    field_part, grad_final = norm_back(
-        grad_normed, second_field, scale_fin, back_final.astype(jnp.float32)
-    )
-    grad_second = grad_second + field_part
-    grad_branch = grad_second.astype(jnp.bfloat16)
-    cross_branch = grad_branch
-    grad_cross_context = product_right(grad_branch, back_cross_output).astype(jnp.bfloat16)
-    ask_parts = []
-    key_parts = []
-    value_parts = []
-    for row_index in range(row_count):
-        row_begin = row_index * length
-        row_end = row_begin + length
-        slot_begin = row_index * slot_count
-        slot_end = slot_begin + slot_count
-        allowed = slot_index[:, None] == segment_index[row_index][None, :]
-        grad_ask_row, grad_key_row, grad_value_row, unused_scores = attend_backward(
-            asking[slot_begin:slot_end],
-            cross_keys[row_begin:row_end],
-            cross_values[row_begin:row_end],
-            0.0,
-            allowed,
-            cross_totals[row_index],
-            grad_cross_context[slot_begin:slot_end],
-        )
-        ask_parts.append(grad_ask_row)
-        key_parts.append(grad_key_row)
-        value_parts.append(grad_value_row)
-    grad_asking = jnp.concatenate(ask_parts, axis=0).astype(jnp.bfloat16)
-    grad_cross_keys = jnp.concatenate(key_parts, axis=0).astype(jnp.bfloat16)
-    grad_cross_values = jnp.concatenate(value_parts, axis=0).astype(jnp.bfloat16)
+    back_cross_key, back_cross_value = cross_key_full, cross_value_full
+    token_count = row_count * slot_count
+    (
+        decoded, start_grad, decoder_gain_grads,
+        normed_fin, decoder_active, normed_start, own_value, normed_mid, cross_context,
+        decoder_before_grad, last_branch, grad_own, self_branch, grad_asking, cross_branch,
+        grad_cross_keys, grad_cross_values,
+    ) = decode(
+        segment_index,
+        start_vectors.reshape(token_count, width),
+        decoded_cotangent.reshape(token_count, width),
+        jnp.stack([start_full, middle_full, final_full]),
+        cross_keys,
+        cross_values,
+        (
+            self_value_full, self_output_full, cross_query_full, cross_output_full,
+            decoder_inner_full, decoder_outer_full,
+        ),
+    )
     grad_cross_key = product_left(memory, grad_cross_keys)
     grad_cross_value = product_left(memory, grad_cross_values)
     grad_memory = product_right(grad_cross_keys, back_cross_key) + product_right(
         grad_cross_values, back_cross_value
     )
-    grad_normed = product_right(grad_asking, back_cross_query)
-    field_part, grad_middle = norm_back(
-        grad_normed, first_field, scale_mid, back_middle.astype(jnp.float32)
-    )
-    grad_first = grad_second + field_part
-    grad_branch = grad_first.astype(jnp.bfloat16)
-    self_branch = grad_branch
-    grad_own = product_right(grad_branch, back_self_output).astype(jnp.bfloat16)
-    grad_normed = product_right(grad_own, back_self_value)
-    field_part, grad_start_gain = norm_back(
-        grad_normed, start_field, scale_start, back_start.astype(jnp.float32)
-    )
-    start_grad = (grad_first + field_part).reshape(row_count, slot_count, width)
     grad_encoded = encoded_cotangent.astype(jnp.float32) + grad_memory
     grad_branch = grad_encoded.astype(jnp.bfloat16)
     grad_outer = product_left(active, grad_branch)
@@ -893,31 +1039,9 @@
     grad_branch = grad_hidden.astype(jnp.bfloat16)
     grad_output = product_left(context, grad_branch)
     grad_context = product_right(grad_branch, back_output).astype(jnp.bfloat16)
-    query_parts = []
-    key_parts = []
-    value_parts = []
-    bias_grad = jnp.zeros((HEADS, length, length), jnp.float32)
-    for row_index in range(row_count):
-        row_begin = row_index * length
-        row_end = row_begin + length
-        segment_row = segment_index[row_index]
-        allowed = segment_row[:, None] == segment_row[None, :]
-        grad_query_row, grad_key_row, grad_value_row, grad_scores = attend_backward(
-            query_all[row_begin:row_end],
-            key_all[row_begin:row_end],
-            value_all[row_begin:row_end],
-            extra,
-            allowed,
-            kept_totals[row_index],
-            grad_context[row_begin:row_end],
-        )
-        query_parts.append(grad_query_row)
-        key_parts.append(grad_key_row)
-        value_parts.append(grad_value_row)
-        bias_grad = bias_grad + grad_scores
-    grad_query_all = jnp.concatenate(query_parts, axis=0).astype(jnp.bfloat16)
-    grad_key_all = jnp.concatenate(key_parts, axis=0).astype(jnp.bfloat16)
-    grad_value_all = jnp.concatenate(value_parts, axis=0).astype(jnp.bfloat16)
+    grad_query_all, grad_key_all, grad_value_all, bias_sums = attend_rows_back(
+        row_count, length, query_all, key_all, value_all, grad_context, shares
+    )
     grad_query = product_left(normed_one, grad_query_all)
     grad_key = product_left(normed_one, grad_key_all)
     grad_value = product_left(normed_one, grad_value_all)
@@ -932,11 +1056,10 @@
     tokens_grad = grad_hidden + field_part
     table_grad = lax.dot_general(
         onehot,
-        bias_grad.reshape(HEADS, length * length),
-        (((0,), (1,)), ((), ())),
+        bias_sums.reshape(HEADS, 3 * BLOCK),
+        (((1,), (1,)), ((), ())),
         precision=lax.Precision.HIGHEST,
     )
-    token_count = row_count * slot_count
     lefts = (normed_fin, decoder_active, normed_start, own_value, normed_mid, cross_context)
     rights = (decoder_before_grad, last_branch, grad_own, self_branch, grad_asking, cross_branch)
     pair_shapes = [(left.shape[1] // count, right.shape[1]) for left, right in zip(lefts, rights)]
@@ -945,7 +1068,8 @@
         columns = left.reshape(token_count, count, rows).transpose(1, 0, 2)
         left_cols.append(jnp.pad(columns, ((0, 0), (0, 0), (0, -rows % 128))))
     small = jnp.concatenate([
-        jnp.stack([grad_gain_one, grad_gain_two, grad_start_gain, grad_middle, grad_final]),
+        jnp.stack([grad_gain_one, grad_gain_two]),
+        decoder_gain_grads,
         jnp.pad(table_grad.reshape(1, -1), ((0, 2), (0, width - table_grad.size))),
     ])
     encoder_grads = (
@@ -977,7 +1101,8 @@
     )
     first_gain_grad, second_gain_grad, start_gain_grad, middle_gain_grad, final_gain_grad = own_gains
     position_table_grad = small_sum[5, : table_grad.size].reshape(table_grad.shape)
-    decoded = decoded_full.reshape(row_count, slot_count, width).astype(jnp.bfloat16)
+    decoded = decoded.reshape(start_vectors.shape)
+    start_grad = start_grad.reshape(start_vectors.shape)
     return (
         encoded_full.astype(jnp.bfloat16),
         decoded,

time: 702 us -> 515 us (0.73)
  local copies, waits for them, and re-layouts: 131 us -> 22.8 us
  matrix products: 220 us -> 119 us
  Pallas kernels: 269 us -> 339 us
  other arithmetic: 69.3 us -> 23.3 us
    dot_general x26 -> x2, matrix products: 101 us -> 0.29 us  [the longest x1 0.15 us: on_device(): lax.dot_general(onehot, bias_sums.reshape(HEADS, 3 * BLOCK), (((1,), (1,)...]
    pallas_call x0 -> x3, Pallas kernels: none -> 69.6 us  [the longest x1 28.1 us: attend_rows_back(): pl.pallas_call(attend_back_kernel, grid=(pairs, rows), out_shape=[jax.Sha...]
    unnamed x228 -> x212, local copies, waits for them, and re-layouts: 77.5 us -> 15.9 us
    add x7 -> x1, other arithmetic: 28.2 us -> 0.01 us  [offset_buckets(): return jnp.where(offset > 0, 16, 0) + near_bucket]
    reshape x9 -> x3, local copies, waits for them, and re-layouts: 24.8 us -> 0.04 us  [the longest x1 0.02 us: on_device(): base = base.reshape(HEADS // 2, 2, 3 * BLOCK)]
    add x1 -> x0, local copies, waits for them, and re-layouts: 12.7 us -> none  [on_device(): bias_grad = bias_grad + grad_scores]
    reduce_sum x4 -> x0, other arithmetic: 8.41 us -> none  [attend_forward(): jnp.sum(jnp.exp(scores - highest_score), axis=-1, keepdims=True)]
    dot_general x14 -> x8, matrix products: 45.4 us -> 42.9 us  [product_right(): lax.dot_general(left, right, (((1,), (1,)), ((), ())), preferred_element_...]
where the time goes in v2:
time: 515 us; the launch traced here: 506 us
  Pallas kernels  339 us (66%)
  matrix products  119 us (23%)
  other arithmetic  23.3 us (5%)
  local copies, waits for them, and re-layouts  22.8 us (4%)
    pallas_call x1, Pallas kernels, reduce_grads(): pl.pallas_call(functools.partial(reduce_kernel, count, kinds, spans), out...  146 us
    pallas_call x1, Pallas kernels, gather_weights(): pl.pallas_call(functools.partial(gather_kernel, count, kinds), out_shape=...  123 us
    dot_general x8, matrix products, product_right(): lax.dot_general(left, right, (((1,), (1,)), ((), ())), preferred_element_...  42.9 us
    dot_general x8, matrix products, product(): return jnp.dot(left, right, preferred_element_type=jnp.float32)  39.4 us
    dot_general x8, matrix products, product_left(): lax.dot_general(left, right, (((0,), (0,)), ((), ())), preferred_element_...  36.6 us
    pallas_call x1, Pallas kernels, attend_rows_back(): pl.pallas_call(attend_back_kernel, grid=(pairs, rows), out_shape=[jax.Sha...  28.1 us
    pallas_call x1, Pallas kernels, attend_rows(): pl.pallas_call(attend_kernel, grid=(rows, pairs), out_shape=[jax.ShapeDty...  25.7 us
    unnamed x212, local copies, waits for them, and re-layouts  15.9 us

profile of v2, /device:TPU:1, one launch (start us, length us, event | category | flops | bytes accessed | tf_op | source)
XLA Modules:
  0.0 506.2 jit_solution(8582721528606247014)
XLA Ops:
  0.7 0.7 stack.37
  2.0 122.9 %gather_weights.1 = (bf16[8,96,768]{2,1,0:T(8,128)(2,1)}, bf16[8,96,768]{2,1,0:T(8,128)(2,1)}, bf16[8,96,768]{2,1,0:T(8,128)(2,1)}, bf16[8,96,768]{2,1,0:T(8,128...) custom-call(bf16[96,768]{1,0:T(8,128)(2,1)} %refs_0_.2, ...), custom_call_target="tpu_custom_call" | custom-call | tf_op jit(solution)/shard_map/gather_weights/pallas_call | solution.py:216
  125.0 0.9 convert_reduce_fusion
  125.9 1.7 copy.63
  128.0 0.7 multiply_multiply_fusion.2
  128.8 2.7 convolution_convert_fusion.5.value_ref
  131.5 3.1 convolution_convert_fusion.6.key_ref
  134.7 2.8 convolution_convert_fusion.7.query_ref
  137.9 1.4 copy-done.3
  139.3 25.7 %attend.1 = (bf16[1024,768]{1,0:T(8,128)(2,1)S(1)}, bf16[2,6,4,256,384]{4,3,2,1,0:T(8,128)(2,1)}) custom-call(s32[1024,128]{1,0:T(8,128)S(1)} %broadcast_in_dim.11.column_ref, s32[2,1,512]{2,1,0:T(1,128)S(1)} %reshape.275.row_ref, f32[6,2,384]{2,1,0:T(2,128)S(1)} %reshape.276.base_ref, bf16[1024,768]{1,0:T(8,128)(2,1)S(1)} %copy-done.3, ...), custom_call_target="tpu_custom_call" | custom-call | tf_op jit(solution)/shard_map/attend/pallas_call | solution.py:721
  165.0 3.9 multiply_reduce_fusion.2
  168.9 0.7 multiply_multiply_fusion.3
  169.7 7.7 %fusion.34 = f32[1024,3072]{1,0:T(8,128)S(1)} fusion(bf16[768,3072]{1,0:T(8,128)(2,1)} %bitcast.116, f32[1024,768]{0,1:T(8,128)S(1)} %get-tuple-element.197, f32[768]{0:T(1024)S(1)} %reshape.312, f32[1024]{0:T(1024)S(1)} %get-tuple-element.195), kind=kOutput, calls=%fused_computation.107 | convolution fusion | flops 4834197504 | bytes 20454400 | tf_op jit(solution)/shard_map/dot_general | solution.py:588
  177.4 12.1 %add_convert_fusion = bf16[1024,768]{0,1:T(8,128)(2,1)S(1)} fusion(f32[1024,768]{0,1:T(8,128)S(1)} %get-tuple-element.197, bf16[3072,768]{1,0:T(8,128)(2,1)} %bitcast.144, f32[1024,3072]{1,0:T(8,128)S(1)} %fusion.34), kind=kOutput, calls=%fused_computation.32 | convolution fusion | flops 4861722624 | bytes 22020096 | tf_op jit(solution)/shard_map/dot_general | solution.py:588
  189.5 4.5 convolution_convert_fusion.3.refs_5_
  194.0 2.6 convolution_convert_fusion.4.refs_4_
  196.7 1.5 slice_reduce_fusion.2
  198.3 0.8 convert_element_type.260
  199.2 1.3 copy-done.7
  200.4 0.7 copy-done.13
  201.2 0.7 copy-done.14
  201.9 15.8 %decode.1 = (bf16[16,768]{1,0:T(8,128)(2,1)}, f32[16,768]{1,0:T(8,128)}, f32[3,768]{1,0:T(4,128)S(1)}, bf16[16,768]{1,0:T(8,128)(2,1)S(1)}, bf16[16,3072]{1,0:T(...) custom-call(s32[2,512]{1,0:T(2,128)S(1)} %copy-done.12, ...), custom_call_target="tpu_custom_call" | custom-call | tf_op jit(solution)/shard_map/decode/pallas_call | solution.py:909
  217.9 4.6 fusion.41
  222.6 0.8 copy.65
  223.4 4.3 add_add_fusion.1
  227.8 17.0 %fusion.6 = bf16[1024,3072]{1,0:T(8,128)(2,1)} fusion(f32[1024,3072]{1,0:T(8,128)} %copy-done.45, bf16[3072,768]{1,0:T(8,128)(2,1)} %bitcast.145, f32[1024,768]{0,1:T(8,128)S(1)} %add_add_fusion.1), kind=kOutput, calls=%fused_computation.8 | convolution fusion | flops 4895539200 | bytes 26738688 | tf_op jit(solution)/shard_map/dot_general | solution.py:598
  244.8 8.1 %multiply_reduce_fusion = (f32[768]{0:T(1024)S(1)}, f32[1024]{0:T(1024)S(1)}, f32[1024,768]{0,1:T(8,128)S(1)}) fusion(f32[1024,768]{0,1:T(8,128)S(1)} %copy-done.47, f32[1024]{0:T(1024)S(1)} %copy-done.63, f32[768]{0:T(1024)S(1)} %copy-done.65, bf16[1024,3072]{1,0:T(8,128)(2,1)} %fusion.6, bf16[768,3072]{1,0:T(8,128)(2,1)S(1)} %bitcast.119), kind=kOutput, calls=%fused_computation.27 | convolution fusion | flops 4836554752 | bytes 17315840 | tf_op jit(solution)/shard_map/dot_general | solution.py:598
  252.9 0.7 subtract_add_fusion
  254.1 2.6 convolution_convert_fusion.2.grad_ref
  256.8 28.1 %attend_back.1 = (bf16[1024,768]{1,0:T(8,128)(2,1)S(1)}, bf16[1024,768]{1,0:T(8,128)(2,1)S(1)}, bf16[1024,768]{1,0:T(8,128)(2,1)S(1)}, f32[6,2,384]{2,1,0:T(2,128)S(1)}) custom-call(bf16[1024,768]{1,0:T(8,128)(2,1)} %convolution_convert_fusion.7.query_ref, bf16[1024,768]{1,0:T(8,128)(2,1)} %copy-done.2, ...), custom_call_target="tpu_custom_call" | custom-call | tf_op jit(solution)/shard_map/attend_back/pallas_call | solution.py:750
  284.9 1.4 fusion.43
  287.1 1.4 fusion.42
  289.0 3.5 fusion.15
  292.8 0.6 select_maximum_fusion.refs_10_
  294.4 4.4 convolution_convert_fusion.8
  298.9 2.4 convolution_convert_fusion.9
  301.3 2.5 convolution_convert_fusion.10
  303.8 2.5 convolution_convert_fusion.11
  306.2 2.5 convolution_convert_fusion.12
  308.7 2.5 convolution_convert_fusion.13
  311.2 1.2 copy-done.52
  312.4 10.2 %convolution_convert_fusion = bf16[3072,768]{1,0:T(8,128)(2,1)} fusion(f32[1024,768]{0,1:T(8,128)S(1)} %copy-done.52, f32[1024,3072]{1,0:T(8,128)S(1)} %bitcast.115), kind=kOutput, calls=%fused_computation.16 | convolution fusion | flops 4863295488 | bytes 20447232 | tf_op jit(solution)/shard_map/dot_general | solution.py:592
  322.6 9.7 %convolution_convert_fusion.1 = bf16[768,3072]{1,0:T(8,128)(2,1)} fusion(bf16[1024,3072]{1,0:T(8,128)(2,1)} %fusion.6, f32[1024,768]{0,1:T(8,128)S(1)} %copy-done.48, f32[768]{0:T(1024)S(1)} %copy-done.65, f32[1024]{0:T(1024)S(1)} %copy-done.63), kind=kOutput, calls=%fused_computation.17 | convolution fusion | flops 4836556800 | bytes 14162944 | tf_op jit(solution)/shard_map/dot_general | solution.py:592
  332.3 146.0 %reduce_grads.1 = (bf16[96,3072]{1,0:T(8,128)(2,1)}, bf16[384,768]{1,0:T(8,128)(2,1)}, bf16[96,768]{1,0:T(8,128)(2,1)}, bf16[96,768]{1,0:T(8,128)(2,1)}, bf16[96...) custom-call(bf16[8,96,3072]{2,1,0:T(8,128)(2,1)} %bitcast.121, ...), custom_call_target="tpu_custom_call" | custom-call | tf_op jit(solution)/shard_map/reduce_grads/pallas_call | solution.py:573
  478.4 2.3 convert_element_type.280
  480.6 2.2 convert_element_type.281
  482.9 1.1 convert_element_type.288
  484.0 1.1 convert_element_type.289
  485.1 0.7 convert_element_type.276
  485.8 0.7 convert_element_type.277
  486.6 0.7 convert_element_type.278
  487.3 0.7 convert_element_type.279
  488.0 0.7 convert_element_type.282
  488.8 0.7 convert_element_type.283
  489.5 0.7 convert_element_type.284
  490.3 0.7 convert_element_type.285
  491.0 0.7 convert_element_type.286
  491.7 0.7 convert_element_type.287
  492.5 0.7 slice_reduce_fusion.3
  493.3 0.7 copy.82
  494.0 0.8 constant_dynamic-slice_fusion
  495.3 5.3 %fusion.12 = f32[1024,768]{0,1:T(8,128)} fusion(f32[1024,768]{0,1:T(8,128)} %copy-done.49, bf16[1024,768]{0,1:T(8,128)(2,1)S(1)} %copy-done.44, f32[1024,768]{0,1:T(8,128)} %get-tuple-element.199, f32[1024]{0:T(1024)S(1)} %broadcast_multiply_fusion, f32[1024]{0:T(1024)S(1)} %copy-done.83, f32[768]{0:T(1024)S(1)} %copy-done.80, f32[1024]{0:T(1024)S(1)} %copy-done.78), kind=kLoop, calls=%fused_computation.23 | loop fusion | flops 5505024 | bytes 11025408 | tf_op jit(solution)/shard_map/add | solution.py:1056
  500.6 3.7 copy.81
  504.2 1.6 copy.80
  (237 shorter events, 5.3 us)
Async XLA Ops:
  0.7 136.8 %copy-start = (f32[32,12]{0,1:T(8,128)S(1)}, f32[32,12]{0,1:T(8,128)}, u32[]{:S(2)}) copy-start(f32[32,12]{0,1:T(8,128)} %param.33) | copy-start | bytes 4612
  125.9 8.7 %copy-start.79 = (f32[768]{0:T(1024)}, f32[768]{0:T(1024)S(1)}, u32[]{:S(2)}) copy-start(f32[768]{0:T(1024)S(1)} %reshape.311) | copy-start | bytes 9220
  128.8 5.9 %copy-start.77 = (f32[1024]{0:T(1024)}, f32[1024]{0:T(1024)S(1)}, u32[]{:S(2)}) copy-start(f32[1024]{0:T(1024)S(1)} %get-tuple-element.193) | copy-start | bytes 12292
  137.5 27.5 %copy-start.81 = (s32[384]{0:T(512)}, s32[384]{0:T(512)S(1)}, u32[]{:S(2)}) copy-start(s32[384]{0:T(512)S(1)} %fusion.24) | copy-start | bytes 4612
  168.9 8.5 %copy-start.46 = (f32[1024,768]{0,1:T(8,128)}, f32[1024,768]{0,1:T(8,128)S(1)}, u32[]{:S(2)}) copy-start(f32[1024,768]{0,1:T(8,128)S(1)} %get-tuple-element.197) | copy-start | bytes 9437188
  169.6 7.8 %copy-start.62 = (f32[1024]{0:T(1024)}, f32[1024]{0:T(1024)S(1)}, u32[]{:S(2)}) copy-start(f32[1024]{0:T(1024)S(1)} %get-tuple-element.195) | copy-start | bytes 12292
  169.7 7.7 %copy-start.64 = (f32[768]{0:T(1024)}, f32[768]{0:T(1024)S(1)}, u32[]{:S(2)}) copy-start(f32[768]{0:T(1024)S(1)} %reshape.312) | copy-start | bytes 9220
  177.4 12.1 %copy-start.45 = (f32[1024,3072]{1,0:T(8,128)}, f32[1024,3072]{1,0:T(8,128)S(1)}, u32[]{:S(2)}) copy-start(f32[1024,3072]{1,0:T(8,128)S(1)} %fusion.34) | copy-start | bytes 37748740
  189.5 4.5 copy-start.54
  194.0 5.1 %copy-start.4 = (bf16[8,96,768]{2,1,0:T(8,128)(2,1)S(1)}, bf16[8,96,768]{2,1,0:T(8,128)(2,1)}, u32[]{:S(2)}) copy-start(bf16[8,96,768]{2,1,0:T(8,128)(2,1)} %get-tuple-element.87) | copy-start | bytes 3538948
  194.0 5.1 %copy-start.5 = (bf16[8,96,768]{2,1,0:T(8,128)(2,1)S(1)}, bf16[8,96,768]{2,1,0:T(8,128)(2,1)}, u32[]{:S(2)}) copy-start(bf16[8,96,768]{2,1,0:T(8,128)(2,1)} %get-tuple-element.88) | copy-start | bytes 3538948
  194.0 5.1 %copy-start.6 = (bf16[8,96,768]{2,1,0:T(8,128)(2,1)S(1)}, bf16[8,96,768]{2,1,0:T(8,128)(2,1)}, u32[]{:S(2)}) copy-start(bf16[8,96,768]{2,1,0:T(8,128)(2,1)} %get-tuple-element.89) | copy-start | bytes 3538948
  201.9 16.0 %copy-start.92 = (bf16[8,96,768]{2,1,0:T(8,128)(2,1)S(1)}, bf16[8,96,768]{2,1,0:T(8,128)(2,1)}, u32[]{:S(2)}) copy-start(bf16[8,96,768]{2,1,0:T(8,128)(2,1)} %get-tuple-element.85) | copy-start | bytes 3538948
  217.7 4.8 copy-start.8
  217.8 4.8 copy-start.10
  217.8 4.8 copy-start.15
  217.8 4.8 copy-start.17
  217.8 4.7 copy-start.19
  217.8 4.7 copy-start.21
  217.8 4.7 copy-start.23
  217.8 4.7 copy-start.25
  217.8 4.7 copy-start.27
  217.9 4.7 copy-start.29
  217.9 4.7 copy-start.31
  217.9 4.7 copy-start.33
  217.9 4.7 copy-start.53
  223.4 21.3 %slice-start.3 = ((s8[4718592]{0:T(1024)(128)(4,1)}), s8[4194304]{0:T(1024)(128)(4,1)S(1)}, s32[]{:S(2)}) async-start(s8[4718592]{0:T(1024)(128)(4,1)} %bitcast.117), calls=%async_computation.3 | async-start | bytes 8388608
  227.7 25.1 %copy-start.51 = (f32[1024,768]{0,1:T(8,128)}, f32[1024,768]{0,1:T(8,128)S(1)}, u32[]{:S(2)}) copy-start(f32[1024,768]{0,1:T(8,128)S(1)} %add_add_fusion.1) | copy-start | bytes 9437188
  227.7 17.0 %copy-start.47 = (f32[1024,768]{0,1:T(8,128)S(1)}, f32[1024,768]{0,1:T(8,128)}, u32[]{:S(2)}) copy-start(f32[1024,768]{0,1:T(8,128)} %copy-done.46) | copy-start | bytes 9437188
  227.7 17.0 %slice-start.4 = ((s8[4718592]{0:T(1024)(128)(4,1)}), s8[524288]{0:T(1024)(128)(4,1)S(1)}, s32[]{:S(2)}) async-start(s8[4718592]{0:T(1024)(128)(4,1)} %bitcast.117), calls=%async_computation.4 | async-start | bytes 1048576
  227.7 17.0 %copy-start.63 = (f32[1024]{0:T(1024)S(1)}, f32[1024]{0:T(1024)}, u32[]{:S(2)}) copy-start(f32[1024]{0:T(1024)} %copy-done.62) | copy-start | bytes 12292
  227.7 17.0 %copy-start.65 = (f32[768]{0:T(1024)S(1)}, f32[768]{0:T(1024)}, u32[]{:S(2)}) copy-start(f32[768]{0:T(1024)} %copy-done.64) | copy-start | bytes 9220
  244.8 8.1 %copy-start.84 = (f32[1024]{0:T(1024)S(1)}, f32[1024]{0:T(1024)}, u32[]{:S(2)}) copy-start(f32[1024]{0:T(1024)} %get-tuple-element.194) | copy-start | bytes 12292
  256.8 28.2 %copy-start.89 = (bf16[8,96,768]{2,1,0:T(8,128)(2,1)S(1)}, bf16[8,96,768]{2,1,0:T(8,128)(2,1)}, u32[]{:S(2)}) copy-start(bf16[8,96,768]{2,1,0:T(8,128)(2,1)} %get-tuple-element.79) | copy-start | bytes 3538948
  288.8 4.6 copy-start.11
  288.8 4.6 copy-start.34
  288.9 4.6 copy-start.32
  288.9 4.6 copy-start.30
  288.9 4.6 copy-start.28
  288.9 4.7 copy-start.26
  288.9 4.7 copy-start.24
  288.9 4.8 copy-start.9
  288.9 4.8 copy-start.22
  288.9 5.0 copy-start.20
  289.0 5.1 %copy-start.18 = (bf16[16,768]{1,0:T(8,128)(2,1)S(1)}, bf16[16,768]{1,0:T(8,128)(2,1)}, u32[]{:S(2)}) copy-start(bf16[16,768]{1,0:T(8,128)(2,1)} %copy-done.17) | copy-start | bytes 73732
  289.0 5.3 %copy-start.16 = (bf16[16,768]{1,0:T(8,128)(2,1)S(1)}, bf16[16,768]{1,0:T(8,128)(2,1)}, u32[]{:S(2)}) copy-start(bf16[16,768]{1,0:T(8,128)(2,1)} %copy-done.15) | copy-start | bytes 73732
  293.6 5.3 %copy-start.61 = (bf16[16,6912]{1,0:T(8,128)(2,1)}, bf16[16,6912]{1,0:T(8,128)(2,1)S(1)}, u32[]{:S(2)}) copy-start(bf16[16,6912]{1,0:T(8,128)(2,1)S(1)} %constant_dynamic-update-slice_fusion.refs_9_) | copy-start | bytes 663556
  303.8 7.4 %slice-start = ((s8[12582912]{0:T(1024)(128)(4,1)}), s8[4194304]{0:T(1024)(128)(4,1)S(1)}, s32[]{:S(2)}) async-start(s8[12582912]{0:T(1024)(128)(4,1)} %bitcast.114), calls=%async_computation | async-start | bytes 8388608
  306.2 4.9 slice-start.1
  312.4 10.2 %copy-start.48 = (f32[1024,768]{0,1:T(8,128)S(1)}, f32[1024,768]{0,1:T(8,128)}, u32[]{:S(2)}) copy-start(f32[1024,768]{0,1:T(8,128)} %copy-done.46) | copy-start | bytes 9437188
  478.3 4.5 copy-start.60
  478.3 5.7 %copy-start.59 = (bf16[384,768]{1,0:T(8,128)(2,1)S(1)}, bf16[384,768]{1,0:T(8,128)(2,1)}, u32[]{:S(2)}) copy-start(bf16[384,768]{1,0:T(8,128)(2,1)} %get-tuple-element.129) | copy-start | bytes 1769476
  478.3 6.8 %copy-start.76 = (bf16[96,768]{1,0:T(8,128)(2,1)S(1)}, bf16[96,768]{1,0:T(8,128)(2,1)}, u32[]{:S(2)}) copy-start(bf16[96,768]{1,0:T(8,128)(2,1)} %get-tuple-element.116) | copy-start | bytes 442372
  480.6 5.2 %copy-start.75 = (bf16[96,768]{1,0:T(8,128)(2,1)S(1)}, bf16[96,768]{1,0:T(8,128)(2,1)}, u32[]{:S(2)}) copy-start(bf16[96,768]{1,0:T(8,128)(2,1)} %get-tuple-element.117) | copy-start | bytes 442372
  480.6 5.9 %copy-start.74 = (bf16[96,768]{1,0:T(8,128)(2,1)S(1)}, bf16[96,768]{1,0:T(8,128)(2,1)}, u32[]{:S(2)}) copy-start(bf16[96,768]{1,0:T(8,128)(2,1)} %get-tuple-element.118) | copy-start | bytes 442372
  480.6 6.7 %copy-start.73 = (bf16[96,768]{1,0:T(8,128)(2,1)S(1)}, bf16[96,768]{1,0:T(8,128)(2,1)}, u32[]{:S(2)}) copy-start(bf16[96,768]{1,0:T(8,128)(2,1)} %get-tuple-element.119) | copy-start | bytes 442372
  480.6 7.4 %copy-start.72 = (bf16[96,768]{1,0:T(8,128)(2,1)S(1)}, bf16[96,768]{1,0:T(8,128)(2,1)}, u32[]{:S(2)}) copy-start(bf16[96,768]{1,0:T(8,128)(2,1)} %get-tuple-element.122) | copy-start | bytes 442372
  482.9 5.9 %copy-start.71 = (bf16[96,768]{1,0:T(8,128)(2,1)S(1)}, bf16[96,768]{1,0:T(8,128)(2,1)}, u32[]{:S(2)}) copy-start(bf16[96,768]{1,0:T(8,128)(2,1)} %get-tuple-element.123) | copy-start | bytes 442372
  482.9 6.7 %copy-start.70 = (bf16[96,768]{1,0:T(8,128)(2,1)S(1)}, bf16[96,768]{1,0:T(8,128)(2,1)}, u32[]{:S(2)}) copy-start(bf16[96,768]{1,0:T(8,128)(2,1)} %get-tuple-element.124) | copy-start | bytes 442372
  482.9 7.4 %copy-start.69 = (bf16[96,768]{1,0:T(8,128)(2,1)S(1)}, bf16[96,768]{1,0:T(8,128)(2,1)}, u32[]{:S(2)}) copy-start(bf16[96,768]{1,0:T(8,128)(2,1)} %get-tuple-element.125) | copy-start | bytes 442372
  482.9 8.1 %copy-start.68 = (bf16[96,768]{1,0:T(8,128)(2,1)S(1)}, bf16[96,768]{1,0:T(8,128)(2,1)}, u32[]{:S(2)}) copy-start(bf16[96,768]{1,0:T(8,128)(2,1)} %get-tuple-element.126) | copy-start | bytes 442372
  484.0 7.7 %copy-start.67 = (bf16[96,768]{1,0:T(8,128)(2,1)S(1)}, bf16[96,768]{1,0:T(8,128)(2,1)}, u32[]{:S(2)}) copy-start(bf16[96,768]{1,0:T(8,128)(2,1)} %get-tuple-element.127) | copy-start | bytes 442372
  484.0 11.3 %copy-start.83 = (f32[1024]{0:T(1024)S(1)}, f32[1024]{0:T(1024)}, u32[]{:S(2)}) copy-start(f32[1024]{0:T(1024)} %get-tuple-element.192) | copy-start | bytes 12292
  500.6 5.2 %copy-start.1 = (f32[32,12]{0,1:T(8,128)S(1)}, f32[32,12]{0,1:T(8,128)}, u32[]{:S(2)}) copy-start(f32[32,12]{0,1:T(8,128)} %param.33) | copy-start | bytes 4612
  (34 other events, 90.6 us)

commit v3 on v2

--- a/solution.py
+++ b/solution.py
@@ -600,11 +600,6 @@
     )
 
 
-def gelu_back(before, grad_out):
-    unused, pullback = jax.vjp(jax.nn.gelu, before)
-    return pullback(grad_out)[0]
-
-
 def root_scale(field):
     return lax.rsqrt(jnp.mean(field * field, axis=-1, keepdims=True) + epsilon)
 
@@ -918,6 +913,368 @@
     )(segment_index, start, cotangent, gains, keys, values, *weights)
 
 
+TILE = 256
+
+
+def rows_of(at, size=TILE):
+    return pl.ds(pl.multiple_of(at * size, size), size)
+
+
+class Gather:
+    def __init__(self, spot, kinds, shards, fulls, sems):
+        self.spot, self.kinds, self.shards, self.fulls = spot, kinds, shards, fulls
+        (
+            self.ring_out, self.ring_in, self.near_out, self.near_in,
+            self.far_out, self.far_in, self.last_out, self.last_in, self.own_sem,
+        ) = sems
+        self.split = [i for i in range(len(kinds)) if kinds[i] in ("wide", "tall")]
+
+    def piece(self, i, step, plane):
+        count = self.spot.count
+        slot = ring_index(self.spot.place + (step if i % 2 else count - step), count)
+        rows = self.shards[i].shape[0]
+        block = self.fulls[i].at[pl.ds(pl.multiple_of(slot * rows, 16), rows)]
+        return cut(self.kinds[i], block, plane, self.spot.core)
+
+    def own_copy(self, i):
+        rows = self.shards[i].shape[0]
+        block = self.fulls[i].at[pl.ds(pl.multiple_of(self.spot.fsdp * rows, 16), rows)]
+        return pltpu.make_async_copy(self.shards[i], block, self.own_sem.at[i])
+
+    def ring_copy(self, i, step, source=None):
+        here = self.piece(i, step, self.spot.plane)
+        return send(
+            here if source is None else source, here,
+            self.ring_out.at[i, step], self.ring_in.at[i, step],
+            self.spot.before if i % 2 else self.spot.after,
+        )
+
+    def near_copy(self, i, step):
+        here = self.piece(i, step, self.spot.plane)
+        return send(
+            here, here, self.near_out.at[i, step], self.near_in.at[i, step], self.spot.sibling
+        )
+
+    def far_copy(self, i, step):
+        here, at = self.piece(i, step, self.spot.plane), self.split.index(i)
+        return send(
+            here, here, self.far_out.at[at, step], self.far_in.at[at, step], self.spot.opposite
+        )
+
+    def last_copy(self, i, step):
+        here, at = self.piece(i, step, 1 - self.spot.plane), self.split.index(i)
+        return send(
+            here, here, self.last_out.at[at, step], self.last_in.at[at, step], self.spot.sibling
+        )
+
+    def start(self, group):
+        for i in group:
+            source = cut(self.kinds[i], self.shards[i], self.spot.plane, self.spot.core)
+            self.ring_copy(i, 0, source).start()
+
+    def advance(self, group, step):
+        count = self.spot.count
+
+        @pl.when(step < count)
+        def _():
+            for i in group:
+                self.ring_copy(i, step - 1).wait_recv()
+
+                @pl.when(step < count - 1)
+                def _():
+                    self.ring_copy(i, step).start()
+
+                if self.kinds[i] != "small":
+                    self.near_copy(i, step).start()
+                if i in self.split:
+                    self.far_copy(i, step).start()
+
+        @pl.when(step > 1)
+        def _():
+            for i in group:
+                if i in self.split:
+                    self.far_copy(i, step - 1).wait_recv()
+                    self.last_copy(i, step - 1).start()
+
+    def arrive(self, group):
+        def one(step, carry):
+            for i in group:
+                if self.kinds[i] != "small":
+                    self.near_copy(i, step).wait_recv()
+                if i in self.split:
+                    self.last_copy(i, step).wait_recv()
+            return carry
+
+        lax.fori_loop(1, self.spot.count, one, 0)
+        for i in group:
+            self.own_copy(i).wait()
+
+    def settle(self, group):
+        def one(step, carry):
+            for i in group:
+                self.ring_copy(i, step - 1).wait_send()
+                if self.kinds[i] != "small":
+                    self.near_copy(i, step).wait_send()
+                if i in self.split:
+                    self.far_copy(i, step).wait_send()
+                    self.last_copy(i, step).wait_send()
+            return carry
+
+        lax.fori_loop(1, self.spot.count, one, 0)
+
+
+FIRST, SECOND, THIRD = (0, 1, 2, 3, 14), (4, 5, 6, 7), (8, 9, 10, 11, 12, 13)
+
+
+def forward_kernel(count, rows, *refs):
+    refs = list(refs)
+
+    def take(size):
+        got = refs[:size]
+        del refs[:size]
+        return got
+
+    shards = take(15)
+    tokens, column, segment, base = take(4)
+    weight_outs = take(14)
+    (gain_out,) = take(1)
+    (
+        query_out, key_out, value_out, share_out, context_out, hidden_out, normed_two_out,
+        active_out, rise_out, memory_out, cross_key_out, cross_value_out, normed_one_out,
+    ) = take(13)
+    held = take(8)
+    gain_all, normed_one, query, key, value, context = take(6)
+    hidden, normed_two, active, rise, memory, cross_keys, cross_values, shares = take(8)
+    gather_sems = take(9)
+    save_sem, share_sem = take(2)
+    spot = Spot(count)
+    fulls = held + weight_outs[8:] + [gain_all]
+    gather = Gather(spot, KINDS, shards, fulls, gather_sems)
+    tiles = tokens.shape[0] // TILE
+    length = tokens.shape[0] // rows
+    blocks, pairs = length // BLOCK, HEADS // 2
+    narrow = jnp.bfloat16
+    saves = []
+
+    def save(source, target):
+        copy = pltpu.make_async_copy(source, target, save_sem.at[len(saves)])
+        copy.start()
+        saves.append(copy)
+
+    def each_tile(body):
+        def one(at, carry):
+            body(rows_of(at), at)
+            return carry
+
+        lax.fori_loop(0, tiles, one, 0)
+
+    def run(group, first, last):
+        def one(step, carry):
+            gather.advance(group, step)
+            return carry
+
+        lax.fori_loop(first, last, one, 0)
+
+    for i in FIRST:
+        gather.own_copy(i).start()
+    spot.greet()
+    gather.start(FIRST)
+    for i in SECOND + THIRD:
+        gather.own_copy(i).start()
+    run(FIRST, 1, count - 1)
+    gather.start(SECOND)
+    run(FIRST, count - 1, count + 1)
+    gather.arrive(FIRST)
+    gain = jnp.zeros((16, gain_all.shape[1]), jnp.float32)
+    for slot in range(count):
+        gain = gain + gain_all[slot * 16 : (slot + 1) * 16].astype(jnp.float32)
+    gain_out[...] = gain
+    query_weight, key_weight, value_weight, output_weight = held[:4]
+    inner_weight, outer_weight, cross_key_weight, cross_value_weight = held[4:]
+
+    def first_norm(span, at):
+        field = tokens[span].astype(jnp.float32)
+        normed_one[span] = (field * root_scale(field) * gain_out[0:1]).astype(narrow)
+
+    each_tile(first_norm)
+
+    def project(target, weight):
+        def body(span, at):
+            target[span] = product(normed_one[span], weight[...]).astype(narrow)
+
+        each_tile(body)
+
+    project(query, query_weight)
+    gather.advance(SECOND, 1)
+    project(key, key_weight)
+    project(value, value_weight)
+    gather.advance(SECOND, 2)
+    for source, target in (
+        (normed_one, normed_one_out), (query, query_out), (key, key_out), (value, value_out),
+    ):
+        save(source, target)
+    for i in range(4):
+        save(held[i], weight_outs[i])
+
+    def share_copy(at):
+        return pltpu.make_async_copy(
+            shares.at[lax.rem(at, 2)],
+            share_out.at[at // pairs, lax.rem(at, pairs)],
+            share_sem.at[lax.rem(at, 2)],
+        )
+
+    def attend_pair(at, carry):
+        row, pair, buffer = at // pairs, lax.rem(at, pairs), lax.rem(at, 2)
+
+        @pl.when(lax.rem(at, 3) == 0)
+        def _():
+            gather.advance(SECOND, 3 + at // 3)
+
+        @pl.when(at >= 2)
+        def _():
+            share_copy(at - 2).wait()
+
+        bias = bias_block(base[pair])
+        columns = rows_of(pair, 2 * KV)
+
+        def span(begin, size):
+            return pl.ds(pl.multiple_of(row * length + begin, BLOCK), size)
+
+        for block in range(blocks):
+            keys, places = reach(block, blocks)
+            own = span(block * BLOCK, BLOCK)
+            near = span(keys.start, keys.stop - keys.start)
+            scores = product_right(wide_heads(query[own, columns]), key[near, columns])
+            scores = scores + bias[:, places]
+            allowed = column[own, :1] == segment[row, :, keys]
+            scores = jnp.where(jnp.concatenate([allowed, allowed], axis=0), scores, negative_fill)
+            powers = jnp.exp(scores - jnp.max(scores, axis=1, keepdims=True))
+            part = powers * (1.0 / jnp.sum(powers, axis=1, keepdims=True))
+            part = part.astype(narrow)
+            shares[buffer, block, :, places] = part
+            mixed = product(part, value[near, columns])
+            context[own, columns] = narrow_heads(mixed).astype(narrow)
+        share_copy(at).start()
+        return carry
+
+    lax.fori_loop(0, rows * pairs, attend_pair, 0)
+    save(context, context_out)
+    gather.advance(SECOND, 7)
+    gather.start(THIRD)
+    gather.advance(SECOND, 8)
+
+    def second_norm(span, at):
+        field = tokens[span].astype(jnp.float32) + product(context[span], output_weight[...])
+        hidden[span] = field
+        normed_two[span] = (field * root_scale(field) * gain_out[1:2]).astype(narrow)
+
+    each_tile(second_norm)
+    save(hidden, hidden_out)
+    save(normed_two, normed_two_out)
+    gather.arrive(SECOND)
+    for i in range(4, 8):
+        save(held[i], weight_outs[i])
+    chunk = tokens.shape[1]
+
+    def feed(span, at):
+        gather.advance(THIRD, at + 1)
+        for begin in range(0, active.shape[1], chunk):
+            part = slice(begin, begin + chunk)
+            level, slope = gelu_parts(product(normed_two[span], inner_weight[:, part]))
+            active[span, part] = level.astype(narrow)
+            rise[span, part] = slope.astype(narrow)
+        full = hidden[span] + product(active[span], outer_weight[...])
+        memory[span] = full.astype(narrow)
+
+    each_tile(feed)
+    save(active, active_out)
+    save(rise, rise_out)
+    save(memory, memory_out)
+    gather.advance(THIRD, tiles + 1)
+
+    def cross(span, at):
+        cross_keys[span] = product(memory[span], cross_key_weight[...]).astype(narrow)
+        cross_values[span] = product(memory[span], cross_value_weight[...]).astype(narrow)
+
+    each_tile(cross)
+    save(cross_keys, cross_key_out)
+    save(cross_values, cross_value_out)
+    run(THIRD, tiles + 2, count + 1)
+    gather.arrive(THIRD)
+    for group in (FIRST, SECOND, THIRD):
+        gather.settle(group)
+    for copy in saves:
+        copy.wait()
+    for at in range(rows * pairs - 2, rows * pairs):
+        share_copy(at).wait()
+
+
+def forward(count, shards, tokens, column, segment_index, base):
+    rows, length = segment_index.shape
+    many, width = tokens.shape
+    hidden_width = shards[4].shape[1]
+    narrow, wide = jnp.bfloat16, jnp.float32
+    pairs, total = HEADS // 2, len(shards)
+    split = sum(kind in ("wide", "tall") for kind in KINDS)
+    weights = [(count * s.shape[0], s.shape[1]) for s in shards]
+    few, much = (many, width), (many, hidden_width)
+    share_shape = (rows, pairs, length // BLOCK, 2 * BLOCK, 3 * BLOCK)
+    shapes = [(w, narrow) for w in weights[:14]] + [((16, width), wide)]
+    shapes += [
+        (few, narrow), (few, narrow), (few, narrow), (share_shape, narrow), (few, narrow),
+        (few, wide), (few, narrow), (much, narrow), (much, narrow), (few, narrow), (few, narrow),
+        (few, narrow), (few, narrow),
+    ]
+    dma = pltpu.SemaphoreType.DMA
+    scratch = [pltpu.VMEM(w, narrow) for w in weights[:8]] + [pltpu.VMEM(weights[14], narrow)]
+    scratch += [pltpu.VMEM(few, narrow)] * 5
+    scratch += [
+        pltpu.VMEM(few, wide), pltpu.VMEM(few, narrow), pltpu.VMEM(much, narrow),
+        pltpu.VMEM(much, narrow), pltpu.VMEM(few, narrow), pltpu.VMEM(few, narrow),
+        pltpu.VMEM(few, narrow), pltpu.VMEM((2,) + share_shape[2:], narrow),
+    ]
+    scratch += [dma((total, count))] * 4 + [dma((split, count))] * 4
+    scratch += [dma((total,)), dma((24,)), dma((2,))]
+    anywhere = pl.BlockSpec(memory_space=pl.ANY)
+    local = pl.BlockSpec(memory_space=pltpu.VMEM)
+    got = pl.pallas_call(
+        functools.partial(forward_kernel, count, rows),
+        out_shape=[jax.ShapeDtypeStruct(s, d) for s, d in shapes],
+        in_specs=[anywhere] * total + [local] * 4,
+        out_specs=[anywhere] * 14 + [local] + [anywhere] * 13,
+        scratch_shapes=scratch,
+        compiler_params=pltpu.CompilerParams(
+            collective_id=2, has_side_effects=True, vmem_limit_bytes=62 * 2**20
+        ),
+        name="forward",
+    )(*shards, tokens, column, segment_index.reshape(rows, 1, length), base)
+    return got[:14], got[14], got[15:]
+
+
+def forward_apart(count, shards, tokens, column, segment_index, base):
+    rows, length = segment_index.shape
+    narrow = jnp.bfloat16
+    whole = gather_weights(count, shards, KINDS)
+    gains = jnp.sum(whole[14].astype(jnp.float32), axis=0)
+    whole = [part.reshape(-1, part.shape[2]) for part in whole[:14]]
+    field = tokens.astype(jnp.float32)
+    normed_one = (field * root_scale(field) * gains[0]).astype(narrow)
+    query, key, value = [product(normed_one, weight).astype(narrow) for weight in whole[:3]]
+    context, shares = attend_rows(
+        rows, length, column, segment_index, base, query, key, value
+    )
+    hidden = field + product(context, whole[3])
+    normed_two = (hidden * root_scale(hidden) * gains[1]).astype(narrow)
+    active, rise = gelu_parts(product(normed_two, whole[4]))
+    active = active.astype(narrow)
+    memory = (hidden + product(active, whole[5])).astype(narrow)
+    cross_keys, cross_values = [product(memory, weight).astype(narrow) for weight in whole[6:8]]
+    return whole, gains, (
+        query, key, value, shares, context, hidden, normed_two,
+        active, rise, memory, cross_keys, cross_values, normed_one,
+    )
+
+
 def on_device(
     tokens,
     segment_index,
@@ -951,57 +1308,34 @@
     width = tokens.shape[1]
     count = lax.axis_size("fsdp")
     depth = first_gain.shape[0]
-    gains = jnp.stack([first_gain, second_gain, start_gain, middle_gain, final_gain])
-    gains = jnp.pad(gains, ((0, 11), (0, 128 - depth)))
-    whole = gather_weights(
-        count,
-        (
-            query_weight, key_weight, value_weight, output_weight, inner_weight, outer_weight,
-            cross_key, cross_value, self_value, self_output, cross_query, cross_output,
-            decoder_inner, decoder_outer, gains,
-        ),
-        KINDS,
-    )
-    gain_parts = whole[14][:, :5, :depth]
-    gain_set = [gain_parts[:, at].reshape(count * depth) for at in range(5)]
-    (
-        query_full, key_full, value_full, output_full, inner_full, outer_full, cross_key_full,
-        cross_value_full, self_value_full, self_output_full, cross_query_full, cross_output_full,
-        decoder_inner_full, decoder_outer_full,
-    ) = [part.reshape(-1, part.shape[2]) for part in whole[:14]]
-    gain_one, gain_two, start_full, middle_full, final_full = gain_set
-    gain_one = gain_one.astype(jnp.float32)
-    gain_two = gain_two.astype(jnp.float32)
     choices = jnp.arange(position_table.shape[0], dtype=jnp.int32)
     onehot = (offset_buckets()[None, :] == choices[:, None]).astype(jnp.float32)
     base = jnp.dot(position_table.T, onehot, precision=lax.Precision.HIGHEST)
     base = base.reshape(HEADS // 2, 2, 3 * BLOCK)
     column = jnp.broadcast_to(segment_index.reshape(-1, 1), (row_count * length, BLOCK))
+    gains = jnp.stack([first_gain, second_gain, start_gain, middle_gain, final_gain])
+    place = jnp.arange(width, dtype=jnp.int32) // depth
+    gains = jnp.where(place == lax.axis_index("fsdp"), jnp.tile(gains, (1, count)), 0)
+    shards = (
+        query_weight, key_weight, value_weight, output_weight, inner_weight, outer_weight,
+        cross_key, cross_value, self_value, self_output, cross_query, cross_output,
+        decoder_inner, decoder_outer, jnp.pad(gains, ((0, 11), (0, 0))),
+    )
+    fused = count == 8 and depth % 32 == 0 and (row_count, length) == (2, 512)
+    plan = forward if fused else forward_apart
+    whole, all_gains, kept = plan(count, shards, tokens, column, segment_index, base)
+    (
+        query_full, key_full, value_full, output_full, inner_full, outer_full, cross_key_full,
+        cross_value_full, self_value_full, self_output_full, cross_query_full, cross_output_full,
+        decoder_inner_full, decoder_outer_full,
+    ) = whole
+    (
+        query_all, key_all, value_all, shares, context, hidden, normed_two,
+        active, rise, memory, cross_keys, cross_values, normed_one,
+    ) = kept
+    gain_one, gain_two = all_gains[0], all_gains[1]
     field = tokens.astype(jnp.float32)
-    scale_one = root_scale(field)
-    normed_one = (field * scale_one * gain_one).astype(jnp.bfloat16)
-    query_all = product(normed_one, query_full).astype(jnp.bfloat16)
-    key_all = product(normed_one, key_full).astype(jnp.bfloat16)
-    value_all = product(normed_one, value_full).astype(jnp.bfloat16)
-    context, shares = attend_rows(
-        row_count, length, column, segment_index, base, query_all, key_all, value_all
-    )
-    hidden = field + product(context, output_full)
-    scale_two = root_scale(hidden)
-    normed_two = (hidden * scale_two * gain_two).astype(jnp.bfloat16)
-    inner_before = product(normed_two, inner_full)
-    active = jax.nn.gelu(inner_before).astype(jnp.bfloat16)
-    encoded_full = hidden + product(active, outer_full)
-    memory = encoded_full.astype(jnp.bfloat16)
-    start_full = start_full.astype(jnp.float32)
-    middle_full = middle_full.astype(jnp.float32)
-    final_full = final_full.astype(jnp.float32)
-    cross_keys = product(memory, cross_key_full).astype(jnp.bfloat16)
-    cross_values = product(memory, cross_value_full).astype(jnp.bfloat16)
-    back_gain_one, back_gain_two = gain_one, gain_two
-    back_query, back_key, back_value, back_output = query_full, key_full, value_full, output_full
-    back_inner, back_outer = inner_full, outer_full
-    back_cross_key, back_cross_value = cross_key_full, cross_value_full
+    scale_one, scale_two = root_scale(field), root_scale(hidden)
     token_count = row_count * slot_count
     (
         decoded, start_grad, decoder_gain_grads,
@@ -1012,7 +1346,7 @@
         segment_index,
         start_vectors.reshape(token_count, width),
         decoded_cotangent.reshape(token_count, width),
-        jnp.stack([start_full, middle_full, final_full]),
+        all_gains[2:5],
         cross_keys,
         cross_values,
         (
@@ -1022,23 +1356,23 @@
     )
     grad_cross_key = product_left(memory, grad_cross_keys)
     grad_cross_value = product_left(memory, grad_cross_values)
-    grad_memory = product_right(grad_cross_keys, back_cross_key) + product_right(
-        grad_cross_values, back_cross_value
+    grad_memory = product_right(grad_cross_keys, cross_key_full) + product_right(
+        grad_cross_values, cross_value_full
     )
     grad_encoded = encoded_cotangent.astype(jnp.float32) + grad_memory
     grad_branch = grad_encoded.astype(jnp.bfloat16)
     grad_outer = product_left(active, grad_branch)
-    grad_active = product_right(grad_branch, back_outer)
-    grad_before = gelu_back(inner_before, grad_active).astype(jnp.bfloat16)
+    grad_active = product_right(grad_branch, outer_full)
+    grad_before = (grad_active * rise).astype(jnp.bfloat16)
     grad_inner = product_left(normed_two, grad_before)
-    grad_normed = product_right(grad_before, back_inner)
+    grad_normed = product_right(grad_before, inner_full)
     field_part, grad_gain_two = norm_back(
-        grad_normed, hidden, scale_two, back_gain_two.astype(jnp.float32)
+        grad_normed, hidden, scale_two, gain_two
     )
     grad_hidden = grad_encoded + field_part
     grad_branch = grad_hidden.astype(jnp.bfloat16)
     grad_output = product_left(context, grad_branch)
-    grad_context = product_right(grad_branch, back_output).astype(jnp.bfloat16)
+    grad_context = product_right(grad_branch, output_full).astype(jnp.bfloat16)
     grad_query_all, grad_key_all, grad_value_all, bias_sums = attend_rows_back(
         row_count, length, query_all, key_all, value_all, grad_context, shares
     )
@@ -1046,12 +1380,12 @@
     grad_key = product_left(normed_one, grad_key_all)
     grad_value = product_left(normed_one, grad_value_all)
     grad_normed = (
-        product_right(grad_query_all, back_query)
-        + product_right(grad_key_all, back_key)
-        + product_right(grad_value_all, back_value)
+        product_right(grad_query_all, query_full)
+        + product_right(grad_key_all, key_full)
+        + product_right(grad_value_all, value_full)
     )
     field_part, grad_gain_one = norm_back(
-        grad_normed, field, scale_one, back_gain_one.astype(jnp.float32)
+        grad_normed, field, scale_one, gain_one
     )
     tokens_grad = grad_hidden + field_part
     table_grad = lax.dot_general(
@@ -1104,7 +1438,7 @@
     decoded = decoded.reshape(start_vectors.shape)
     start_grad = start_grad.reshape(start_vectors.shape)
     return (
-        encoded_full.astype(jnp.bfloat16),
+        memory,
         decoded,
         tokens_grad,
         start_grad,

time: 515 us -> 445 us (0.86)
  matrix products: 119 us -> 61.4 us
  Pallas kernels: 339 us -> 333 us
  local copies, waits for them, and re-layouts: 22.8 us -> 17.3 us
    dot_general x8 -> x0, matrix products: 39.4 us -> none  [product(): return jnp.dot(left, right, preferred_element_type=jnp.float32)]
    dot_general x8, matrix products: 42.9 us -> 28.5 us  [product_right(): lax.dot_general(left, right, (((1,), (1,)), ((), ())), preferred_element_...]
    unnamed x212 -> x105, local copies, waits for them, and re-layouts: 15.9 us -> 8.45 us
    pallas_call x2 -> x1, Pallas kernels: 149 us -> 147 us  [forward(): pl.pallas_call(functools.partial(forward_kernel, count, rows), out_shape=...]
where the time goes in v3:
time: 445 us; the launch traced here: 437 us
  Pallas kernels  333 us (75%)
  matrix products  61.4 us (14%)
  other arithmetic  23.5 us (5%)
  local copies, waits for them, and re-layouts  17.3 us (4%)
    pallas_call x1, Pallas kernels, forward(): pl.pallas_call(functools.partial(forward_kernel, count, rows), out_shape=...  147 us
    pallas_call x1, Pallas kernels, reduce_grads(): pl.pallas_call(functools.partial(reduce_kernel, count, kinds, spans), out...  142 us
    dot_general x8, matrix products, product_left(): lax.dot_general(left, right, (((0,), (0,)), ((), ())), preferred_element_...  32.6 us
    dot_general x8, matrix products, product_right(): lax.dot_general(left, right, (((1,), (1,)), ((), ())), preferred_element_...  28.5 us
    pallas_call x1, Pallas kernels, attend_rows_back(): pl.pallas_call(attend_back_kernel, grid=(pairs, rows), out_shape=[jax.Sha...  28 us
    pallas_call x1, Pallas kernels, decode(): pl.pallas_call(functools.partial(decoder_kernel, rows, tokens // rows), o...  15.8 us
    convert_element_type x14, other arithmetic, on_device(): part.astype(jnp.float32)  15.5 us

profile of v3, /device:TPU:1, one launch (start us, length us, event | category | flops | bytes accessed | tf_op | source)
XLA Modules:
  0.0 436.8 jit_solution(7034462924354689515)
XLA Ops:
  0.7 0.7 stack.29
  1.5 0.7 copy.61
  2.2 1.3 reshape.187.refs_17_
  3.4 1.8 fusion
  5.4 0.6 pad.24.refs_14_
  6.0 0.1 convolution_bitcast_fusion
  6.1 0.6 reshape.188.refs_18_
  6.7 1.0 broadcast_in_dim.30.refs_16_
  7.7 147.0 %forward.1 = (bf16[768,768]{1,0:T(8,128)(2,1)}, bf16[768,768]{1,0:T(8,128)(2,1)}, bf16[768,768]{1,0:T(8,128)(2,1)}, bf16[768,768]{1,0:T(8,128)(2,1)}, bf16[768,3...) custom-call(bf16[96,768]{1,0:T(8,128)(2,1)} %refs_0_.2, ...), custom_call_target="tpu_custom_call" | custom-call | tf_op jit(solution)/shard_map/forward/pallas_call | solution.py:1240
  154.8 2.3 multiply_reduce_fusion.2
  157.2 0.8 slice_reduce_fusion
  158.0 0.7 slice.15.refs_3_
  158.8 1.3 copy-done.4
  160.1 1.3 copy-done.5
  161.3 15.8 %decode.1 = (bf16[16,768]{1,0:T(8,128)(2,1)}, f32[16,768]{1,0:T(8,128)}, f32[3,768]{1,0:T(4,128)S(1)}, bf16[16,768]{1,0:T(8,128)(2,1)S(1)}, bf16[16,3072]{1,0:T(...) custom-call(s32[2,512]{1,0:T(2,128)S(1)} %copy-done.6, ...), custom_call_target="tpu_custom_call" | custom-call | tf_op jit(solution)/shard_map/decode/pallas_call | solution.py:904
  177.1 0.1 reshape.201
  178.0 0.6 copy-done.15
  178.5 4.0 convolution_convert_fusion.4
  182.6 1.4 fusion.29
  184.1 0.4 copy-done.18
  184.5 0.3 copy-done.20
  184.8 1.4 add_add_fusion.1
  186.3 10.4 %multiply_convert_fusion = bf16[1024,3072]{1,0:T(8,128)(2,1)} fusion(bf16[1024,3072]{1,0:T(8,128)(2,1)} %get-tuple-element.105, bf16[3072,768]{1,0:T(8,128)(2,1)} %get-tuple-element.104, f32[1024,768]{1,0:T(8,128)S(1)} %add_add_fusion.1), kind=kOutput, calls=%fused_computation | convolution fusion | flops 4842061824 | bytes 20447232 | tf_op jit(solution)/shard_map/dot_general | solution.py:598
  196.7 7.1 %convolution_convert_fusion = bf16[3072,768]{1,0:T(8,128)(2,1)} fusion(bf16[1024,3072]{1,0:T(8,128)(2,1)S(1)} %bitcast.111, f32[1024,768]{1,0:T(8,128)S(1)} %add_add_fusion.1), kind=kOutput, calls=%fused_computation.5 | convolution fusion | flops 4834983936 | bytes 14155776 | tf_op jit(solution)/shard_map/dot_general | solution.py:592
  203.9 7.7 %multiply_reduce_fusion = (f32[768]{0:T(1024)S(1)}, f32[1024]{0:T(1024)S(1)}, f32[1024,768]{1,0:T(8,128)S(1)}) fusion(f32[1024,768]{1,0:T(8,128)S(1)} %copy-done.12, f32[1024]{0:T(1024)S(1)} %get-tuple-element.214, f32[768]{0:T(1024)S(1)} %get-tuple-element.205, bf16[1024,3072]{1,0:T(8,128)(2,1)} %multiply_convert_fusion, bf16[768,3072]{1,0:T(8,128)(2,1)S(1)} %bitcast.113), kind=kOutput, calls=%fused_computation.14 | convolution fusion | flops 4836554752 | bytes 17315840 | tf_op jit(solution)/shard_map/dot_general | solution.py:598
  211.6 7.0 %convolution_convert_fusion.1 = bf16[768,3072]{1,0:T(8,128)(2,1)} fusion(bf16[1024,768]{1,0:T(8,128)(2,1)S(1)} %copy-done.35, bf16[1024,3072]{1,0:T(8,128)(2,1)S(1)} %copy-done.41), kind=kOutput, calls=%fused_computation.6 | convolution fusion | flops 4834197504 | bytes 12582912 | tf_op jit(solution)/shard_map/dot_general | solution.py:592
  218.6 2.4 convolution_convert_fusion.3
  221.1 1.0 subtract_add_fusion
  222.1 0.4 copy-done.34
  222.5 2.5 convolution_convert_fusion.5
  225.0 2.6 convolution_convert_fusion.2.grad_ref
  227.6 28.0 %attend_back.1 = (bf16[1024,768]{1,0:T(8,128)(2,1)S(1)}, bf16[1024,768]{1,0:T(8,128)(2,1)S(1)}, bf16[1024,768]{1,0:T(8,128)(2,1)S(1)}, f32[6,2,384]{2,1,0:T(2,128)S(1)}) custom-call(bf16[1024,768]{1,0:T(8,128)(2,1)} %get-tuple-element.107.query_ref, bf16[1024,768]{1,0:T(8,128)(2,1)} %get-tuple-element.108.key_ref, ...), custom_call_target="tpu_custom_call" | custom-call | tf_op jit(solution)/shard_map/attend_back/pallas_call | solution.py:745
  255.7 1.1 copy-done.9
  256.8 0.2 fusion.12
  257.0 0.1 reshape.208
  257.1 4.5 %convolution_convert_fusion.8 = bf16[768,768]{1,0:T(8,128)(2,1)} fusion(bf16[1024,768]{1,0:T(8,128)(2,1)} %get-tuple-element.121, bf16[1024,768]{1,0:T(8,128)(2,1)} %copy-done.9), kind=kOutput, calls=%fused_computation.26 | convolution fusion | flops 1208549376 | bytes 4325376 | tf_op jit(solution)/shard_map/dot_general | solution.py:592
  261.6 1.4 fusion.30
  263.1 2.5 convolution_convert_fusion.7
  265.5 2.5 convolution_convert_fusion.6
  268.0 1.4 fusion.31
  269.4 0.3 copy-done.19
  269.7 2.1 fusion.6
  271.9 2.2 fusion.3
  274.1 0.6 select_maximum_fusion.refs_10_
  274.7 142.0 %reduce_grads.1 = (bf16[96,3072]{1,0:T(8,128)(2,1)}, bf16[384,768]{1,0:T(8,128)(2,1)}, bf16[96,768]{1,0:T(8,128)(2,1)}, bf16[96,768]{1,0:T(8,128)(2,1)}, bf16[96...) custom-call(bf16[8,96,3072]{2,1,0:T(8,128)(2,1)} %bitcast.91, ...), custom_call_target="tpu_custom_call" | custom-call | tf_op jit(solution)/shard_map/reduce_grads/pallas_call | solution.py:573
  416.8 0.8 slice_reduce_fusion.2
  417.5 0.8 constant_dynamic-slice_fusion
  418.3 0.5 slice_bitcast_fusion
  418.9 0.7 copy.58
  419.6 1.6 convert_element_type.185
  421.3 1.7 convert_element_type.186
  423.0 1.7 convert_element_type.187
  424.6 1.7 convert_element_type.188
  426.3 0.7 convert_element_type.191
  427.1 0.7 convert_element_type.192
  427.8 0.7 convert_element_type.193
  428.6 0.7 convert_element_type.194
  429.3 0.7 convert_element_type.195
  430.0 0.7 convert_element_type.196
  430.8 1.1 convert_element_type.189
  431.9 1.1 convert_element_type.190
  433.0 1.1 convert_element_type.197
  434.1 1.1 convert_element_type.198
  435.2 1.1 copy.84
  (120 shorter events, 1.0 us)
Async XLA Ops:
  0.7 5.3 %copy-start = (f32[32,12]{0,1:T(8,128)S(1)}, f32[32,12]{0,1:T(8,128)}, u32[]{:S(2)}) copy-start(f32[32,12]{0,1:T(8,128)} %param.33) | copy-start | bytes 4612
  154.8 4.0 copy-start.2
  154.8 4.0 copy-start.3
  154.8 4.0 copy-start.6
  154.8 4.0 copy-start.7
  154.8 4.0 copy-start.8
  158.8 1.3 copy-start.4
  160.1 1.3 copy-start.5
  177.1 1.4 copy-start.15
  177.8 4.8 %copy-start.25 = (bf16[16,6912]{1,0:T(8,128)(2,1)}, bf16[16,6912]{1,0:T(8,128)(2,1)S(1)}, u32[]{:S(2)}) copy-start(bf16[16,6912]{1,0:T(8,128)(2,1)S(1)} %constant_dynamic-update-slice_fusion.refs_9_) | copy-start | bytes 663556
  178.5 4.0 copy-start.26
  178.5 4.0 copy-start.36
  178.5 4.1 copy-start.40
  182.6 1.5 copy-start.17
  182.6 1.9 copy-start.18
  182.6 2.2 copy-start.20
  184.8 11.9 %slice-start = ((s8[6291456]{0:T(1024)(128)(4,1)}), s8[2097152]{0:T(1024)(128)(4,1)S(1)}, s32[]{:S(2)}) async-start(s8[6291456]{0:T(1024)(128)(4,1)} %bitcast.110), calls=%async_computation | async-start | bytes 4194304
  186.2 10.4 %slice-start.1 = ((s8[6291456]{0:T(1024)(128)(4,1)}), s8[4194304]{0:T(1024)(128)(4,1)S(1)}, s32[]{:S(2)}) async-start(s8[6291456]{0:T(1024)(128)(4,1)} %bitcast.110), calls=%async_computation.1 | async-start | bytes 8388608
  186.2 17.6 %slice-start.2 = ((s8[4718592]{0:T(1024)(128)(4,1)}), s8[4194304]{0:T(1024)(128)(4,1)S(1)}, s32[]{:S(2)}) async-start(s8[4718592]{0:T(1024)(128)(4,1)} %bitcast.112), calls=%async_computation.2 | async-start | bytes 8388608
  196.7 7.2 %copy-start.12 = (f32[1024,768]{1,0:T(8,128)S(1)}, f32[1024,768]{1,0:T(8,128)}, u32[]{:S(2)}) copy-start(f32[1024,768]{1,0:T(8,128)} %get-tuple-element.103) | copy-start | bytes 9437188
  196.7 7.2 %slice-start.3 = ((s8[4718592]{0:T(1024)(128)(4,1)}), s8[524288]{0:T(1024)(128)(4,1)S(1)}, s32[]{:S(2)}) async-start(s8[4718592]{0:T(1024)(128)(4,1)} %bitcast.112), calls=%async_computation.3 | async-start | bytes 1048576
  203.9 7.7 %copy-start.35 = (bf16[1024,768]{1,0:T(8,128)(2,1)S(1)}, bf16[1024,768]{1,0:T(8,128)(2,1)}, u32[]{:S(2)}) copy-start(bf16[1024,768]{1,0:T(8,128)(2,1)} %get-tuple-element.119) | copy-start | bytes 4718596
  203.9 7.7 %copy-start.41 = (bf16[1024,3072]{1,0:T(8,128)(2,1)S(1)}, bf16[1024,3072]{1,0:T(8,128)(2,1)}, u32[]{:S(2)}) copy-start(bf16[1024,3072]{1,0:T(8,128)(2,1)} %multiply_convert_fusion) | copy-start | bytes 18874372
  221.1 1.4 copy-start.34
  222.5 2.5 copy-start.13
  222.5 2.5 copy-start.39
  255.7 1.1 copy-start.9
  257.1 4.5 %copy-start.10 = (bf16[1024,768]{1,0:T(8,128)(2,1)S(1)}, bf16[1024,768]{1,0:T(8,128)(2,1)}, u32[]{:S(2)}) copy-start(bf16[1024,768]{1,0:T(8,128)(2,1)} %copy-done.9) | copy-start | bytes 4718596
  257.1 4.5 %copy-start.38 = (bf16[768,768]{1,0:T(8,128)(2,1)S(1)}, bf16[768,768]{1,0:T(8,128)(2,1)}, u32[]{:S(2)}) copy-start(bf16[768,768]{1,0:T(8,128)(2,1)} %get-tuple-element.113) | copy-start | bytes 3538948
  261.6 1.4 copy-start.33
  265.5 2.5 copy-start.37
  268.0 1.4 copy-start.11
  268.0 1.7 copy-start.19
  269.7 2.1 copy-start.14
  416.7 9.6 %copy-start.32 = (bf16[96,768]{1,0:T(8,128)(2,1)S(1)}, bf16[96,768]{1,0:T(8,128)(2,1)}, u32[]{:S(2)}) copy-start(bf16[96,768]{1,0:T(8,128)(2,1)} %get-tuple-element.144) | copy-start | bytes 442372
  416.7 10.3 %copy-start.31 = (bf16[96,768]{1,0:T(8,128)(2,1)S(1)}, bf16[96,768]{1,0:T(8,128)(2,1)}, u32[]{:S(2)}) copy-start(bf16[96,768]{1,0:T(8,128)(2,1)} %get-tuple-element.145) | copy-start | bytes 442372
  416.7 11.1 %copy-start.30 = (bf16[96,768]{1,0:T(8,128)(2,1)S(1)}, bf16[96,768]{1,0:T(8,128)(2,1)}, u32[]{:S(2)}) copy-start(bf16[96,768]{1,0:T(8,128)(2,1)} %get-tuple-element.146) | copy-start | bytes 442372
  418.8 9.7 %copy-start.29 = (bf16[96,768]{1,0:T(8,128)(2,1)S(1)}, bf16[96,768]{1,0:T(8,128)(2,1)}, u32[]{:S(2)}) copy-start(bf16[96,768]{1,0:T(8,128)(2,1)} %get-tuple-element.147) | copy-start | bytes 442372
  421.3 8.0 %copy-start.28 = (bf16[96,768]{1,0:T(8,128)(2,1)S(1)}, bf16[96,768]{1,0:T(8,128)(2,1)}, u32[]{:S(2)}) copy-start(bf16[96,768]{1,0:T(8,128)(2,1)} %get-tuple-element.148) | copy-start | bytes 442372
  422.9 7.1 %copy-start.27 = (bf16[96,768]{1,0:T(8,128)(2,1)S(1)}, bf16[96,768]{1,0:T(8,128)(2,1)}, u32[]{:S(2)}) copy-start(bf16[96,768]{1,0:T(8,128)(2,1)} %get-tuple-element.149) | copy-start | bytes 442372
  424.6 6.1 %copy-start.24 = (bf16[96,3072]{1,0:T(8,128)(2,1)S(1)}, bf16[96,3072]{1,0:T(8,128)(2,1)}, u32[]{:S(2)}) copy-start(bf16[96,3072]{1,0:T(8,128)(2,1)} %get-tuple-element.142) | copy-start | bytes 1769476
  428.6 3.3 copy-start.23
  430.8 2.2 copy-start.22
  431.9 2.2 copy-start.21
  433.0 2.2 copy-start.16
  434.1 2.2 copy-start.1

commit v4 on v3

--- a/solution.py
+++ b/solution.py
@@ -1275,6 +1275,725 @@
     )
 
 
+INNER, OUTER = 0, 1
+SQUARES = (2, 3, 4, 5, 6, 7)
+
+
+def backward_kernel(count, rows, spans, *refs):
+    refs = list(refs)
+
+    def take(size):
+        got = refs[:size]
+        del refs[:size]
+        return got
+
+    (
+        inner_hbm, outer_hbm, query_weight_hbm, key_weight_hbm, value_weight_hbm,
+        output_weight_hbm, cross_key_weight_hbm, cross_value_weight_hbm,
+        active_hbm, rise_hbm, normed_two_hbm, context_hbm, query_hbm, key_hbm, value_hbm,
+        normed_one_hbm, tokens_hbm, memory_hbm, grad_keys_hbm, grad_values_hbm, cotangent_hbm,
+        hidden_hbm, shares_hbm,
+    ) = take(23)
+    left_part, right_part, gain, decoder_gains = take(4)
+    sums, pairs = take(8), len(spans)
+    pair_sums = take(pairs)
+    small_sum, tokens_grad_hbm = take(2)
+    big, flat, half, work, final, far = take(1)[0], take(2), take(8), take(8), take(6), take(2)
+    left_all, right_all = take(2)
+    pair_work, pair_half, pair_far = take(pairs), take(pairs), take(pairs)
+    small, small_near, small_mid, small_far, small_all = take(5)
+    pool, level, weights, shares, bias_acc, key_acc, value_acc = take(7)
+    (
+        near_sem, ring_out, ring_in, far_sem, end_sem, left_out, left_in,
+        right_out, right_in, pair_sem, small_sem, small_out, small_in, load_sem, share_sem,
+    ) = take(15)
+    spot = Spot(count)
+    core, plane = spot.core, spot.plane
+    diagonal = (lax.rem(spot.dp + 2, 4) + 1 - 2 * core, spot.fsdp)
+    narrow = jnp.bfloat16
+    many, width = level.shape[1:]
+    tiles, length = many // TILE, many // rows
+    blocks = length // BLOCK
+    depth = width // count
+    products = {2: big.at[0], 3: big.at[1], 4: big.at[2], 5: flat[0], 6: flat[0], 7: flat[1]}
+
+    def peer(k):
+        return (spot.dp, lax.rem(spot.fsdp + k, count))
+
+    def slot_at(i, step):
+        turn = step + 1 if i % 2 else count - 1 - step
+        return ring_index(spot.place + turn, count)
+
+    def near_copy(i):
+        if i == INNER:
+            source = big.at[pl.ds(2 * (1 - core), 2)]
+        elif i == OUTER:
+            source = big.at[:, :, half_of(1 - core, width)]
+        else:
+            source = products[i].at[:, half_of(1 - core, width)]
+        return send(source, half[i], near_sem.at[0, i], near_sem.at[1, i], spot.sibling)
+
+    def part_of(i, slot, side):
+        if i == INNER:
+            return half[i].at[side, pl.ds(pl.multiple_of(slot * depth, 16), depth)]
+        if i == OUTER:
+            own = 4 * depth
+            begin = lax.rem(slot, 2) * own + side * (own // 2)
+            return half[i].at[slot // 2, pl.ds(pl.multiple_of(begin, 16), own // 2)]
+        return half[i].at[pl.ds(pl.multiple_of(slot * depth, 16), depth)]
+
+    def far_copy(i, step):
+        return send(
+            part_of(i, slot_at(i, step), 1 - plane), far[i].at[step],
+            far_sem.at[0, i, step], far_sem.at[1, i, step], spot.opposite,
+        )
+
+    def join(i):
+        near_copy(i).wait()
+        if i == INNER:
+
+            def one(at, carry):
+                side, span = at // 3, rows_of(lax.rem(at, 3))
+                mine = big[2 * core + side, span]
+                half[i][side, span] = plus(half[i][side, span], mine).astype(narrow)
+                return carry
+
+            lax.fori_loop(0, 6, one, 0)
+        elif i == OUTER:
+
+            def one(at, carry):
+                side, span = at // 3, rows_of(lax.rem(at, 3))
+                mine = big[side, span, half_of(core, width)]
+                half[i][side, span] = plus(half[i][side, span], mine).astype(narrow)
+                return carry
+
+            lax.fori_loop(0, 12, one, 0)
+        else:
+
+            def one(at, carry):
+                span = rows_of(at)
+                mine = products[i][span, half_of(core, width)]
+                half[i][span] = plus(half[i][span], mine).astype(narrow)
+                return carry
+
+            lax.fori_loop(0, 3, one, 0)
+        if i in (INNER, OUTER):
+
+            def far_start(step, carry):
+                far_copy(i, step).start()
+                return carry
+
+            lax.fori_loop(0, count, far_start, 0)
+
+    def ring_copy(i, step):
+        return send(
+            work[i].at[step], work[i].at[step + 1], ring_out.at[i, step], ring_in.at[i, step],
+            spot.before if i % 2 else spot.after,
+        )
+
+    def advance(group, step):
+        for i in group:
+            value = part_of(i, slot_at(i, step), plane)[...].astype(jnp.float32)
+            if i in (INNER, OUTER):
+                far_copy(i, step).wait_recv()
+                value = value + far[i][step].astype(jnp.float32)
+
+            @pl.when(step > 0)
+            def _():
+                ring_copy(i, step - 1).wait_recv()
+                work[i][step] = plus(value, work[i][step]).astype(narrow)
+
+            @pl.when(step == 0)
+            def _():
+                work[i][step] = value.astype(narrow)
+
+            @pl.when(step < count - 1)
+            def _():
+                ring_copy(i, step).start()
+
+    def run(group, first, last):
+        def one(step, carry):
+            advance(group, step)
+            return carry
+
+        lax.fori_loop(first, last, one, 0)
+
+    def end_across(i):
+        return send(
+            work[i].at[count - 1], final[i - 2], end_sem.at[0, i], end_sem.at[1, i], spot.opposite
+        )
+
+    def end_piece(i):
+        if i == INNER:
+            return cut("wide", sums[i], plane, core)
+        if i == OUTER:
+            return cut("tall", sums[i], plane, core)
+        return sums[i].at[:, half_of(core, width)]
+
+    def end_copies(i):
+        here = end_piece(i)
+        copies = [send(here, here, end_sem.at[2, i], end_sem.at[3, i], spot.sibling)]
+        if i in (INNER, OUTER):
+            copies.append(send(here, here, end_sem.at[4, i], end_sem.at[5, i], spot.opposite))
+            copies.append(send(here, here, end_sem.at[6, i], end_sem.at[7, i], diagonal))
+        return copies
+
+    def close(i):
+        if i in (INNER, OUTER):
+            end_piece(i)[...] = work[i][count - 1]
+        else:
+            end_across(i).wait()
+            end_piece(i)[...] = plus(work[i][count - 1], final[i - 2][...]).astype(narrow)
+        for copy in end_copies(i):
+            copy.start()
+
+    def left_copy(k):
+        other = lax.rem(spot.fsdp + k, count)
+        return send(
+            left_part.at[other], left_all.at[spot.fsdp], left_out.at[k], left_in.at[k], peer(k)
+        )
+
+    def right_copy(way, step):
+        turn = step if way else count - step
+        slot = ring_index(spot.place + turn, count)
+        wide = right_part.shape[1] // 2
+        here = right_all.at[slot, :, way * wide : (way + 1) * wide]
+        return send(
+            here, here, right_out.at[way, step], right_in.at[way, step],
+            spot.before if way else spot.after,
+        )
+
+    def right_step(step):
+        for way in range(2):
+            right_copy(way, step - 1).wait_recv()
+            if step < count - 1:
+                right_copy(way, step).start()
+
+    def pair_near(j):
+        columns = pair_sums[j].shape[1]
+        return send(
+            pair_work[j].at[:, half_of(1 - core, columns)], pair_half[j],
+            pair_sem.at[0, j], pair_sem.at[1, j], spot.sibling,
+        )
+
+    def pair_across(j):
+        return send(
+            pair_half[j], pair_far[j], pair_sem.at[2, j], pair_sem.at[3, j], spot.opposite
+        )
+
+    def pair_end(j):
+        here = pair_sums[j].at[:, half_of(core, pair_sums[j].shape[1])]
+        return send(here, here, pair_sem.at[4, j], pair_sem.at[5, j], spot.sibling)
+
+    def small_copy(k):
+        here = small_all.at[spot.fsdp]
+        return send(here, here, small_out.at[k], small_in.at[k], peer(k))
+
+    def each_peer(body):
+        def one(k, carry):
+            body(k)
+            return carry
+
+        lax.fori_loop(1, count, one, 0)
+
+    def each_tile(body):
+        def one(at, carry):
+            body(rows_of(at))
+            return carry
+
+        lax.fori_loop(0, tiles, one, 0)
+
+    used = []
+
+    def load(source, target):
+        copy = pltpu.make_async_copy(source, target, load_sem.at[len(used)])
+        copy.start()
+        used.append(copy)
+        return copy
+
+    def fold(target, left, right):
+        def one(at, carry):
+            span = rows_of(at)
+            target[span] = product_left(left[:, span], right[...]).astype(narrow)
+            return carry
+
+        lax.fori_loop(0, width // TILE, one, 0)
+
+    loads = [
+        load(grad_keys_hbm, pool.at[4]), load(cross_key_weight_hbm, weights.at[0]),
+        load(grad_values_hbm, pool.at[5]), load(cross_value_weight_hbm, weights.at[1]),
+        load(cotangent_hbm, pool.at[2]), load(memory_hbm, pool.at[1]),
+    ]
+
+    def chunk_of(source, at):
+        return source.at[:, pl.ds(at * width, width)]
+
+    active_loads = {1: load(chunk_of(active_hbm, 1), pool.at[3])}
+    hidden_load = load(hidden_hbm, level.at[2])
+    out_loads = {0: load(outer_hbm.at[pl.ds(0, width)], weights.at[2])}
+    barrier = pltpu.get_barrier_semaphore()
+    for partner in (spot.sibling, spot.opposite, diagonal):
+        pl.semaphore_signal(barrier, inc=1, device_id=partner, device_id_type=MESH)
+    each_peer(
+        lambda k: pl.semaphore_signal(barrier, inc=1, device_id=peer(k), device_id_type=MESH)
+    )
+    pl.semaphore_wait(barrier, count + 2)
+    each_peer(lambda k: left_copy(k).start())
+    right_all[spot.fsdp] = right_part[...]
+    left_all[spot.fsdp] = left_part[spot.fsdp]
+    for way in range(2):
+        right_copy(way, 0).start()
+    small[...] = jnp.zeros_like(small)
+    small[2:5] = decoder_gains[...]
+    for copy in loads:
+        copy.wait()
+
+    def enter(span):
+        value = pool[2, span].astype(jnp.float32)
+        value = value + product_right(pool[4, span], weights[0])
+        value = value + product_right(pool[5, span], weights[1])
+        level[0, span] = value
+        pool[0, span] = value.astype(narrow)
+
+    each_tile(enter)
+    active_loads[0] = load(chunk_of(active_hbm, 0), pool.at[2])
+    in_loads = {
+        at: load(chunk_of(inner_hbm, at), weights.at[at]) for at in range(2)
+    }
+    fold(flat[0], pool.at[1], pool.at[4])
+    near_copy(6).start()
+    fold(flat[1], pool.at[1], pool.at[5])
+    near_copy(7).start()
+    normed_load = load(normed_two_hbm, pool.at[1])
+    context_load = load(context_hbm, pool.at[4])
+    right_step(1)
+
+    rise_loads = {}
+    for at in range(4):
+        buffer = 2 + at % 2
+        active_loads[at].wait()
+        fold(big.at[at], pool.at[buffer], pool.at[0])
+        if at < 2:
+            active_loads[at + 2] = load(chunk_of(active_hbm, at + 2), pool.at[buffer])
+        else:
+            rise_loads[at - 2] = load(chunk_of(rise_hbm, at - 2), pool.at[buffer])
+        right_step(at + 2)
+        if at == 1:
+            join(6)
+            join(7)
+        if at >= 1:
+            advance((6, 7), at - 1)
+    near_copy(OUTER).start()
+    out_loads[1] = load(outer_hbm.at[pl.ds(width, width)], weights.at[3])
+
+    normed_load.wait()
+    for at in range(4):
+        buffer = 2 + at % 2
+        rise_loads[at].wait()
+        out_loads[at].wait()
+        in_loads[at].wait()
+
+        def back(span):
+            before = product_right(pool[0, span], weights[2 + at % 2])
+            before = (before * pool[buffer, span].astype(jnp.float32)).astype(narrow)
+            pool[buffer, span] = before
+            moved = product_right(before, weights[at % 2])
+            level[1, span] = moved if at == 0 else level[1, span] + moved
+
+        each_tile(back)
+        if at < 2:
+            span = pl.ds((at + 2) * width, width)
+            out_loads[at + 2] = load(outer_hbm.at[span], weights.at[2 + at % 2])
+            in_loads[at + 2] = load(chunk_of(inner_hbm, at + 2), weights.at[at % 2])
+        if at == 0:
+            right_step(6)
+            advance((6, 7), 3)
+            join(OUTER)
+        fold(big.at[at], pool.at[1], pool.at[buffer])
+        if at < 2:
+            rise_loads[at + 2] = load(chunk_of(rise_hbm, at + 2), pool.at[buffer])
+        if at == 0:
+            right_step(7)
+            each_peer(lambda k: left_copy(k).wait_recv())
+            advance((6, 7), 4)
+            for j, (left_at, right_at) in enumerate(spans):
+                own, columns = pair_sums[j].shape
+                wide = -(-own // 128) * 128
+                left = left_all[:, :, left_at : left_at + wide].reshape(-1, wide)
+                for begin in range(0, columns, width):
+                    right = right_all[:, :, right_at + begin : right_at + begin + width]
+                    right = right.reshape(-1, width)
+                    block = product_left(left, right)
+                    pair_work[j][:, begin : begin + width] = block[:own].astype(narrow)
+                pair_near(j).start()
+        elif at == 1:
+            advance((6, 7), 5)
+            advance((OUTER,), 0)
+            advance((OUTER,), 1)
+        elif at == 2:
+            advance((6, 7), 6)
+            advance((OUTER,), 2)
+            advance((OUTER,), 3)
+            for j in range(pairs):
+                pair_near(j).wait()
+                mine = pair_work[j][:, half_of(core, pair_sums[j].shape[1])]
+                pair_half[j][...] = plus(pair_half[j][...], mine).astype(narrow)
+                pair_across(j).start()
+        else:
+            advance((6, 7), 7)
+            advance((OUTER,), 4)
+            for i in (6, 7):
+                end_across(i).start()
+    near_copy(INNER).start()
+    query_load = load(query_hbm, pool.at[1])
+    key_load, value_load = load(key_hbm, pool.at[2]), load(value_hbm, pool.at[3])
+    late_loads = [
+        load(query_weight_hbm, weights.at[0]), load(key_weight_hbm, weights.at[1]),
+        load(value_weight_hbm, weights.at[2]),
+    ]
+    output_load = load(output_weight_hbm, weights.at[3])
+
+    def back_norm(field, moved, gain_row, at):
+        scale = root_scale(field)
+        small[at : at + 1] += jnp.sum(moved * field * scale, axis=0, keepdims=True)
+        weighted = moved * gain_row
+        mean = jnp.mean(weighted * field, axis=-1, keepdims=True)
+        return scale * weighted - field * (scale * scale * scale) * mean
+
+    hidden_load.wait()
+
+    def second(span):
+        value = level[0, span] + back_norm(level[2, span], level[1, span], gain[1:2], 1)
+        level[0, span] = value
+        pool[0, span] = value.astype(narrow)
+
+    each_tile(second)
+    advance((OUTER,), 5)
+    context_load.wait()
+    fold(flat[0], pool.at[4], pool.at[0])
+    near_copy(5).start()
+    normed_one_load = load(normed_one_hbm, pool.at[4])
+    advance((OUTER,), 6)
+    output_load.wait()
+
+    def third(span):
+        pool[5, span] = product_right(pool[0, span], weights[3]).astype(narrow)
+
+    each_tile(third)
+    tokens_load = load(tokens_hbm, pool.at[0])
+    advance((OUTER,), 7)
+    join(INNER)
+    join(5)
+    for copy in (query_load, key_load, value_load):
+        copy.wait()
+
+    def share_copy(at):
+        return pltpu.make_async_copy(
+            shares_hbm.at[lax.rem(at, rows), at // rows],
+            shares.at[lax.rem(at, 2)],
+            share_sem.at[lax.rem(at, 2)],
+        )
+
+    turns = rows * (HEADS // 2)
+    share_copy(0).start()
+
+    def attend_pair(at, carry):
+        pair, row, buffer = at // rows, lax.rem(at, rows), lax.rem(at, 2)
+        share_copy(at).wait()
+
+        @pl.when(at + 1 < turns)
+        def _():
+            share_copy(at + 1).start()
+
+        @pl.when((at >= 1) & (at < count + 1))
+        def _():
+            advance((5,), at - 1)
+
+        @pl.when((at >= 3) & (at < count + 3))
+        def _():
+            advance((INNER,), at - 3)
+
+        @pl.when(row == 0)
+        def _():
+            bias_acc[...] = jnp.zeros_like(bias_acc)
+
+        key_acc[...] = jnp.zeros_like(key_acc)
+        value_acc[...] = jnp.zeros_like(value_acc)
+        columns = rows_of(pair, 2 * KV)
+
+        def span(begin, size):
+            return pl.ds(pl.multiple_of(row * length + begin, BLOCK), size)
+
+        for block in range(blocks):
+            keys, places = reach(block, blocks)
+            own = span(block * BLOCK, BLOCK)
+            near = span(keys.start, keys.stop - keys.start)
+            query, grad = wide_heads(pool[1, own, columns]), wide_heads(pool[5, own, columns])
+            narrow_shares = shares[buffer, block, :, places]
+            part = narrow_shares.astype(jnp.float32)
+            value_acc[keys] += product_left(narrow_shares, grad)
+            moved = part * product_right(grad, pool[3, near, columns])
+            grad_scores = moved - part * jnp.sum(moved, axis=1, keepdims=True)
+            bias_acc[:, places] += grad_scores
+            low = grad_scores.astype(narrow)
+            key_acc[keys] += product_left(low, query)
+            mixed = product(low, pool[2, near, columns])
+            pool[1, own, columns] = narrow_heads(mixed).astype(narrow)
+        pool[2, span(0, length), columns] = key_acc[...].astype(narrow)
+        pool[3, span(0, length), columns] = value_acc[...].astype(narrow)
+
+        @pl.when(row == rows - 1)
+        def _():
+            for head in range(2):
+                block = bias_acc[head * BLOCK : (head + 1) * BLOCK]
+                place = slice(head * 3 * BLOCK, (head + 1) * 3 * BLOCK)
+                small[pl.ds(5 + pair, 1), place] = offset_sums(block)
+
+        return carry
+
+    lax.fori_loop(0, turns, attend_pair, 0)
+    end_across(5).start()
+    normed_one_load.wait()
+    for i, at in ((2, 1), (3, 2), (4, 3)):
+        fold(big.at[i - 2], pool.at[4], pool.at[at])
+        near_copy(i).start()
+    close(INNER)
+    close(OUTER)
+    for i in (5, 6, 7):
+        close(i)
+    for i in (2, 3, 4):
+        join(i)
+    advance((2, 3, 4), 0)
+    tokens_load.wait()
+    for copy in late_loads:
+        copy.wait()
+
+    def save(at):
+        span = rows_of(at)
+        return pltpu.make_async_copy(
+            level.at[1, span], tokens_grad_hbm.at[span], share_sem.at[2 + at]
+        )
+
+    def last(at, carry):
+        span = rows_of(at)
+        moved = product_right(pool[1, span], weights[0])
+        moved = moved + product_right(pool[2, span], weights[1])
+        moved = moved + product_right(pool[3, span], weights[2])
+        field = pool[0, span].astype(jnp.float32)
+        level[1, span] = level[0, span] + back_norm(field, moved, gain[0:1], 0)
+        save(at).start()
+        advance((2, 3, 4), at + 1)
+        return carry
+
+    lax.fori_loop(0, tiles, last, 0)
+    near_small = send(small, small_near, small_sem.at[0], small_sem.at[1], spot.sibling)
+    near_small.start()
+    for j in range(pairs):
+        pair_across(j).wait()
+        here = half_of(core, pair_sums[j].shape[1])
+        pair_sums[j][:, here] = plus(pair_half[j][...], pair_far[j][...]).astype(narrow)
+        pair_end(j).start()
+    advance((2, 3, 4), tiles + 1)
+    near_small.wait()
+    small_mid[...] = small[...] + small_near[...]
+    far_small = send(small_mid, small_far, small_sem.at[2], small_sem.at[3], spot.opposite)
+    far_small.start()
+    advance((2, 3, 4), tiles + 2)
+    far_small.wait()
+    small_all[spot.fsdp] = small_mid[...] + small_far[...]
+    each_peer(lambda k: small_copy(k).start())
+    run((2, 3, 4), tiles + 3, count)
+    for i in (2, 3, 4):
+        end_across(i).start()
+    each_peer(lambda k: small_copy(k).wait_recv())
+    small_sum[...] = lax.fori_loop(
+        1, count, lambda k, so_far: so_far + small_all[k], small_all[0]
+    )
+    for i in (2, 3, 4):
+        close(i)
+    for i in range(8):
+        for copy in end_copies(i):
+            copy.wait()
+    for j in range(pairs):
+        pair_end(j).wait()
+    for at in range(tiles):
+        save(at).wait()
+
+    def drain(step, carry):
+        for i in (INNER, OUTER):
+            far_copy(i, step).wait_send()
+        return carry
+
+    lax.fori_loop(0, count, drain, 0)
+
+    def drain_ring(step, carry):
+        for i in range(8):
+            ring_copy(i, step).wait_send()
+        for way in range(2):
+            right_copy(way, step).wait_send()
+        left_copy(step + 1).wait_send()
+        small_copy(step + 1).wait_send()
+        return carry
+
+    lax.fori_loop(0, count - 1, drain_ring, 0)
+
+
+def backward(
+    count, rows, whole, kept, tokens, cotangent, grad_keys, grad_values,
+    left_part, right_part, pair_shapes, gains, decoder_gains,
+):
+    (
+        query, key, value, shares, context, hidden, normed_two,
+        active, rise, memory, unused_keys, unused_values, normed_one,
+    ) = kept
+    many, width = tokens.shape
+    depth, narrow, wide = width // count, jnp.bfloat16, jnp.float32
+    pairs = len(pair_shapes)
+    spans, left_at, right_at = [], 0, 0
+    for own, columns in pair_shapes:
+        spans.append((left_at, right_at))
+        left_at, right_at = left_at + -(-own // 128) * 128, right_at + columns
+    dma, vmem = pltpu.SemaphoreType.DMA, pltpu.VMEM
+    pieces = [(depth, width), (2 * depth, width // 2)] + [(depth, width // 2)] * 6
+    outs = [(depth, 4 * width), (4 * depth, width)] + [(depth, width)] * 6
+    little = (16, width)
+    scratch = [vmem((4, width, width), narrow)] + [vmem((width, width), narrow)] * 2
+    scratch += [vmem((2, width, width), narrow), vmem((4, width, width // 2), narrow)]
+    scratch += [vmem((width, width // 2), narrow)] * 6
+    scratch += [vmem((count,) + piece, narrow) for piece in pieces]
+    scratch += [vmem(pieces[2], narrow)] * 6
+    scratch += [vmem((count,) + piece, narrow) for piece in pieces[:2]]
+    scratch += [vmem(left_part.shape, narrow), vmem((count,) + right_part.shape, narrow)]
+    scratch += [vmem(s, narrow) for s in pair_shapes]
+    scratch += [vmem((r, c // 2), narrow) for r, c in pair_shapes] * 2
+    scratch += [vmem(little, wide)] * 4 + [vmem((count,) + little, wide)]
+    scratch += [
+        vmem((6, many, width), narrow), vmem((3, many, width), wide),
+        vmem((4, width, width), narrow), vmem((2,) + shares.shape[2:], narrow),
+        vmem((2 * BLOCK, 3 * BLOCK), wide),
+    ]
+    scratch += [vmem((many // rows, 2 * KV), wide)] * 2
+    scratch += [
+        dma((2, 8)), dma((8, count)), dma((8, count)), dma((2, 2, count)), dma((8, 8)),
+        dma((count,)), dma((count,)), dma((2, count)), dma((2, count)), dma((6, pairs)),
+        dma((4,)), dma((count,)), dma((count,)), dma((48,)), dma((2 + many // TILE,)),
+    ]
+    shapes = [jax.ShapeDtypeStruct(s, narrow) for s in outs + list(pair_shapes)]
+    shapes += [jax.ShapeDtypeStruct(little, wide), jax.ShapeDtypeStruct((many, width), wide)]
+    anywhere = pl.BlockSpec(memory_space=pl.ANY)
+    local = pl.BlockSpec(memory_space=pltpu.VMEM)
+    got = pl.pallas_call(
+        functools.partial(backward_kernel, count, rows, spans),
+        out_shape=shapes,
+        in_specs=[anywhere] * 23 + [local] * 4,
+        out_specs=[local] * (len(shapes) - 1) + [anywhere],
+        scratch_shapes=scratch,
+        compiler_params=pltpu.CompilerParams(
+            collective_id=3, has_side_effects=True, vmem_limit_bytes=63 * 2**20
+        ),
+        name="backward",
+    )(
+        whole[4], whole[5], whole[0], whole[1], whole[2], whole[3], whole[6], whole[7],
+        active, rise, normed_two, context, query, key, value, normed_one, tokens, memory,
+        grad_keys, grad_values, cotangent, hidden, shares,
+        left_part, right_part, gains, decoder_gains,
+    )
+    return got[:8], got[8 : 8 + pairs], got[-2], got[-1]
+
+
+def backward_apart(
+    count, rows, whole, kept, tokens, cotangent, grad_cross_keys, grad_cross_values,
+    left_part, right_part, pair_shapes, gains, decoder_gains,
+):
+    (
+        query_full, key_full, value_full, output_full, inner_full, outer_full, cross_key_full,
+        cross_value_full,
+    ) = whole[:8]
+    (
+        query_all, key_all, value_all, shares, context, hidden, normed_two,
+        active, rise, memory, unused_keys, unused_values, normed_one,
+    ) = kept
+    row_count, length = rows, tokens.shape[0] // rows
+    gain_one, gain_two = gains[0], gains[1]
+    field = tokens.astype(jnp.float32)
+    scale_one, scale_two = root_scale(field), root_scale(hidden)
+    grad_cross_key = product_left(memory, grad_cross_keys)
+    grad_cross_value = product_left(memory, grad_cross_values)
+    grad_memory = product_right(grad_cross_keys, cross_key_full) + product_right(
+        grad_cross_values, cross_value_full
+    )
+    grad_encoded = cotangent.astype(jnp.float32) + grad_memory
+    grad_branch = grad_encoded.astype(jnp.bfloat16)
+    grad_outer = product_left(active, grad_branch)
+    grad_active = product_right(grad_branch, outer_full)
+    grad_before = (grad_active * rise).astype(jnp.bfloat16)
+    grad_inner = product_left(normed_two, grad_before)
+    grad_normed = product_right(grad_before, inner_full)
+    field_part, grad_gain_two = norm_back(
+        grad_normed, hidden, scale_two, gain_two
+    )
+    grad_hidden = grad_encoded + field_part
+    grad_branch = grad_hidden.astype(jnp.bfloat16)
+    grad_output = product_left(context, grad_branch)
+    grad_context = product_right(grad_branch, output_full).astype(jnp.bfloat16)
+    grad_query_all, grad_key_all, grad_value_all, bias_sums = attend_rows_back(
+        row_count, length, query_all, key_all, value_all, grad_context, shares
+    )
+    grad_query = product_left(normed_one, grad_query_all)
+    grad_key = product_left(normed_one, grad_key_all)
+    grad_value = product_left(normed_one, grad_value_all)
+    grad_normed = (
+        product_right(grad_query_all, query_full)
+        + product_right(grad_key_all, key_full)
+        + product_right(grad_value_all, value_full)
+    )
+    field_part, grad_gain_one = norm_back(
+        grad_normed, field, scale_one, gain_one
+    )
+    tokens_grad = grad_hidden + field_part
+    small = jnp.concatenate([
+        jnp.stack([grad_gain_one, grad_gain_two]),
+        decoder_gains,
+        bias_sums.reshape(HEADS // 2, -1),
+        jnp.zeros((5, tokens.shape[1]), jnp.float32),
+    ])
+    encoder_grads = (
+        grad_inner, grad_outer, grad_query, grad_key, grad_value, grad_output,
+        grad_cross_key, grad_cross_value,
+    )
+    encoder_sums, decoder_sums, small_sum = reduce_grads(
+        count,
+        ENCODER_KINDS,
+        [
+            g.astype(jnp.bfloat16).reshape(count, g.shape[0] // count, g.shape[1])
+            for g in encoder_grads
+        ],
+        left_part,
+        right_part,
+        pair_shapes,
+        small,
+    )
+    return encoder_sums, decoder_sums, small_sum, tokens_grad
+
+
+def widen_kernel(*refs):
+    half = len(refs) // 2
+    for source, target in zip(refs[:half], refs[half:]):
+        target[...] = source[...].astype(jnp.float32)
+
+
+def widen(parts):
+    local = pl.BlockSpec(memory_space=pltpu.VMEM)
+    return pl.pallas_call(
+        widen_kernel,
+        out_shape=[jax.ShapeDtypeStruct(part.shape, jnp.float32) for part in parts],
+        in_specs=[local] * len(parts),
+        out_specs=[local] * len(parts),
+        compiler_params=pltpu.CompilerParams(vmem_limit_bytes=48 * 2**20),
+        name="widen",
+    )(*parts)
+
+
 def on_device(
     tokens,
     segment_index,
@@ -1324,18 +2043,7 @@
     fused = count == 8 and depth % 32 == 0 and (row_count, length) == (2, 512)
     plan = forward if fused else forward_apart
     whole, all_gains, kept = plan(count, shards, tokens, column, segment_index, base)
-    (
-        query_full, key_full, value_full, output_full, inner_full, outer_full, cross_key_full,
-        cross_value_full, self_value_full, self_output_full, cross_query_full, cross_output_full,
-        decoder_inner_full, decoder_outer_full,
-    ) = whole
-    (
-        query_all, key_all, value_all, shares, context, hidden, normed_two,
-        active, rise, memory, cross_keys, cross_values, normed_one,
-    ) = kept
-    gain_one, gain_two = all_gains[0], all_gains[1]
-    field = tokens.astype(jnp.float32)
-    scale_one, scale_two = root_scale(field), root_scale(hidden)
+    memory, cross_keys, cross_values = kept[9:12]
     token_count = row_count * slot_count
     (
         decoded, start_grad, decoder_gain_grads,
@@ -1349,50 +2057,7 @@
         all_gains[2:5],
         cross_keys,
         cross_values,
-        (
-            self_value_full, self_output_full, cross_query_full, cross_output_full,
-            decoder_inner_full, decoder_outer_full,
-        ),
-    )
-    grad_cross_key = product_left(memory, grad_cross_keys)
-    grad_cross_value = product_left(memory, grad_cross_values)
-    grad_memory = product_right(grad_cross_keys, cross_key_full) + product_right(
-        grad_cross_values, cross_value_full
-    )
-    grad_encoded = encoded_cotangent.astype(jnp.float32) + grad_memory
-    grad_branch = grad_encoded.astype(jnp.bfloat16)
-    grad_outer = product_left(active, grad_branch)
-    grad_active = product_right(grad_branch, outer_full)
-    grad_before = (grad_active * rise).astype(jnp.bfloat16)
-    grad_inner = product_left(normed_two, grad_before)
-    grad_normed = product_right(grad_before, inner_full)
-    field_part, grad_gain_two = norm_back(
-        grad_normed, hidden, scale_two, gain_two
-    )
-    grad_hidden = grad_encoded + field_part
-    grad_branch = grad_hidden.astype(jnp.bfloat16)
-    grad_output = product_left(context, grad_branch)
-    grad_context = product_right(grad_branch, output_full).astype(jnp.bfloat16)
-    grad_query_all, grad_key_all, grad_value_all, bias_sums = attend_rows_back(
-        row_count, length, query_all, key_all, value_all, grad_context, shares
-    )
-    grad_query = product_left(normed_one, grad_query_all)
-    grad_key = product_left(normed_one, grad_key_all)
-    grad_value = product_left(normed_one, grad_value_all)
-    grad_normed = (
-        product_right(grad_query_all, query_full)
-        + product_right(grad_key_all, key_full)
-        + product_right(grad_value_all, value_full)
-    )
-    field_part, grad_gain_one = norm_back(
-        grad_normed, field, scale_one, gain_one
-    )
-    tokens_grad = grad_hidden + field_part
-    table_grad = lax.dot_general(
-        onehot,
-        bias_sums.reshape(HEADS, 3 * BLOCK),
-        (((1,), (1,)), ((), ())),
-        precision=lax.Precision.HIGHEST,
+        whole[8:14],
     )
     lefts = (normed_fin, decoder_active, normed_start, own_value, normed_mid, cross_context)
     rights = (decoder_before_grad, last_branch, grad_own, self_branch, grad_asking, cross_branch)
@@ -1401,40 +2066,30 @@
     for left, (rows, unused) in zip(lefts, pair_shapes):
         columns = left.reshape(token_count, count, rows).transpose(1, 0, 2)
         left_cols.append(jnp.pad(columns, ((0, 0), (0, 0), (0, -rows % 128))))
-    small = jnp.concatenate([
-        jnp.stack([grad_gain_one, grad_gain_two]),
-        decoder_gain_grads,
-        jnp.pad(table_grad.reshape(1, -1), ((0, 2), (0, width - table_grad.size))),
-    ])
-    encoder_grads = (
-        grad_inner, grad_outer, grad_query, grad_key, grad_value, grad_output,
-        grad_cross_key, grad_cross_value,
-    )
-    encoder_sums, decoder_sums, small_sum = reduce_grads(
-        count,
-        ENCODER_KINDS,
-        [
-            g.astype(jnp.bfloat16).reshape(count, g.shape[0] // count, g.shape[1])
-            for g in encoder_grads
-        ],
+    turn_back = backward if fused else backward_apart
+    encoder_sums, decoder_sums, small_sum, tokens_grad = turn_back(
+        count, row_count, whole, kept, tokens, encoded_cotangent,
+        grad_cross_keys, grad_cross_values,
         jnp.concatenate(left_cols, axis=2),
         jnp.concatenate(rights, axis=1),
-        pair_shapes,
-        small,
+        pair_shapes, all_gains, decoder_gain_grads,
     )
     (
         inner_weight_grad, outer_weight_grad, query_weight_grad, key_weight_grad,
         value_weight_grad, output_weight_grad, cross_key_grad, cross_value_grad,
-    ) = [part.astype(jnp.float32) for part in encoder_sums]
-    (
         decoder_inner_grad, decoder_outer_grad, self_value_grad, self_output_grad,
         cross_query_grad, cross_output_grad,
-    ) = [part.astype(jnp.float32) for part in decoder_sums]
+    ) = widen([*encoder_sums, *decoder_sums])
+    position_table_grad = lax.dot_general(
+        onehot,
+        small_sum[5:11].reshape(HEADS, 3 * BLOCK),
+        (((1,), (1,)), ((), ())),
+        precision=lax.Precision.HIGHEST,
+    )
     own_gains = lax.dynamic_slice_in_dim(
         small_sum[:5], lax.axis_index("fsdp") * depth, depth, axis=1
     )
     first_gain_grad, second_gain_grad, start_gain_grad, middle_gain_grad, final_gain_grad = own_gains
-    position_table_grad = small_sum[5, : table_grad.size].reshape(table_grad.shape)
     decoded = decoded.reshape(start_vectors.shape)
     start_grad = start_grad.reshape(start_vectors.shape)
     return (

time: 445 us -> 400 us (0.90)
  matrix products: 61.4 us -> 0.89 us
  Pallas kernels: 333 us -> 360 us
  other arithmetic: 23.5 us -> 0.04 us
  local copies, waits for them, and re-layouts: 17.3 us -> 33 us
    dot_general x17 -> x1, matrix products: 61.2 us -> 0.75 us  [on_device(): lax.dot_general(onehot, small_sum[5:11].reshape(HEADS, 3 * BLOCK), (((1,)...]
    pallas_call x2, Pallas kernels: 170 us -> 198 us  [the longest x1 195 us: backward(): pl.pallas_call(functools.partial(backward_kernel, count, rows, spans), ou...]
    unnamed x105 -> x69, local copies, waits for them, and re-layouts: 8.45 us -> 25.2 us
    convert_element_type x14 -> x0, other arithmetic: 15.5 us -> none  [on_device(): part.astype(jnp.float32)]
where the time goes in v4:
time: 400 us; the launch traced here: 395 us
  Pallas kernels  360 us (90%)
  local copies, waits for them, and re-layouts  33 us (8%)
    pallas_call x1, Pallas kernels, backward(): pl.pallas_call(functools.partial(backward_kernel, count, rows, spans), ou...  195 us
    pallas_call x1, Pallas kernels, forward(): pl.pallas_call(functools.partial(forward_kernel, count, rows), out_shape=...  147 us
    unnamed x69, local copies, waits for them, and re-layouts  25.2 us
    pallas_call x1, Pallas kernels, decode(): pl.pallas_call(functools.partial(decoder_kernel, rows, tokens // rows), o...  15.6 us

profile of v4, /device:TPU:1, one launch (start us, length us, event | category | flops | bytes accessed | tf_op | source)
XLA Modules:
  0.0 395.5 jit_solution(797374009566843992)
XLA Ops:
  0.7 0.0 copy-start
  0.7 0.7 stack.23
  1.5 0.7 copy.56
  2.2 1.3 reshape.124.refs_17_
  3.4 0.1 tile.10
  3.5 0.6 pad.20.refs_14_
  4.2 0.0 copy-done
  4.2 0.1 convolution_bitcast_fusion
  4.3 0.6 reshape.125.refs_18_
  4.9 1.0 broadcast_in_dim.26.refs_16_
  5.9 0.0 copy-start.20
  5.9 0.0 copy-start.21
  5.9 0.0 copy-start.22
  5.9 146.9 %forward.1 = (bf16[768,768]{1,0:T(8,128)(2,1)}, bf16[768,768]{1,0:T(8,128)(2,1)}, bf16[768,768]{1,0:T(8,128)(2,1)}, bf16[768,768]{1,0:T(8,128)(2,1)}, bf16[768,3...) custom-call(bf16[96,768]{1,0:T(8,128)(2,1)} %refs_0_.2, ...), custom_call_target="tpu_custom_call" | custom-call | tf_op jit(solution)/shard_map/forward/pallas_call | solution.py:1240
  152.8 0.7 slice.9.refs_3_
  153.6 0.0 copy-done.20
  153.6 0.0 copy-done.21
  153.6 0.0 copy-done.22
  153.6 0.0 copy-start.2
  153.6 1.3 copy-done.2
  154.9 0.0 copy-start.3
  154.9 1.3 copy-done.3
  156.1 0.0 copy-start.4
  156.1 1.3 copy-done.4
  157.4 0.0 copy-start.5
  157.4 1.3 copy-done.5
  158.7 15.6 %decode.1 = (bf16[16,768]{1,0:T(8,128)(2,1)}, f32[16,768]{1,0:T(8,128)}, f32[3,768]{1,0:T(4,128)S(1)}, bf16[16,768]{1,0:T(8,128)(2,1)S(1)}, bf16[16,3072]{1,0:T(...) custom-call(s32[2,512]{1,0:T(2,128)S(1)} %copy-done.20, ...), custom_call_target="tpu_custom_call" | custom-call | tf_op jit(solution)/shard_map/decode/pallas_call | solution.py:904
  174.3 0.0 copy-start.23
  174.3 0.6 copy-done.23
  174.9 0.1 reshape.129
  175.0 0.1 reshape.131
  175.1 0.1 reshape.132
  175.2 0.1 reshape.133
  175.3 0.1 reshape.134
  175.5 0.0 copy-start.26
  175.7 0.5 copy-done.26
  176.2 0.0 copy-start.27
  176.2 0.7 copy-done.27
  176.9 194.5 %backward.1 = (bf16[96,3072]{1,0:T(8,128)(2,1)}, bf16[384,768]{1,0:T(8,128)(2,1)}, bf16[96,768]{1,0:T(8,128)(2,1)}, bf16[96,768]{1,0:T(8,128)(2,1)}, bf16[96,768...) custom-call(bf16[768,3072]{1,0:T(8,128)(2,1)} %get-tuple-element.110, ...), custom_call_target="tpu_custom_call" | custom-call | tf_op jit(solution)/shard_map/backward/pallas_call | solution.py:1885
  371.5 0.8 slice.11
  372.3 0.7 slice.10
  373.0 0.1 constant_dynamic-slice_fusion
  373.1 0.5 slice_bitcast_fusion
  373.6 0.8 fusion.1
  374.4 1.1 copy-done.6
  375.5 1.1 copy-done.7
  376.5 1.1 copy-done.8
  377.6 1.1 copy-done.9
  378.6 0.9 copy-done.10
  379.6 0.9 copy-done.11
  380.5 0.9 copy-done.12
  381.4 0.9 copy-done.13
  382.3 0.9 copy-done.14
  383.2 0.9 copy-done.15
  384.1 0.9 copy-done.16
  385.0 0.9 copy-done.17
  385.9 0.9 copy-done.18
  386.8 0.9 copy-done.19
  387.8 3.4 widen.1
  391.2 0.0 copy-done.24
  391.2 1.1 copy.80
  392.3 1.3 copy-done.25
  393.6 1.7 copy.81
  395.3 0.0 copy-done.1
  (39 shorter events, 0.2 us)
Async XLA Ops:
  0.7 3.5 copy-start
  5.9 147.6 %copy-start.20 = (s32[2,512]{1,0:T(2,128)S(1)}, s32[2,512]{1,0:T(2,128)}, u32[]{:S(2)}) copy-start(s32[2,512]{1,0:T(2,128)} %refs_0_.3) | copy-start | bytes 12292
  5.9 147.6 %copy-start.21 = (bf16[2,8,768]{2,1,0:T(8,128)(2,1)S(1)}, bf16[2,8,768]{2,1,0:T(8,128)(2,1)}, u32[]{:S(2)}) copy-start(bf16[2,8,768]{2,1,0:T(8,128)(2,1)} %param.27) | copy-start | bytes 73732
  5.9 147.6 %copy-start.22 = (bf16[2,8,768]{2,1,0:T(8,128)(2,1)S(1)}, bf16[2,8,768]{2,1,0:T(8,128)(2,1)}, u32[]{:S(2)}) copy-start(bf16[2,8,768]{2,1,0:T(8,128)(2,1)} %param.49) | copy-start | bytes 73732
  153.6 1.3 copy-start.2
  154.9 1.3 copy-start.3
  156.1 1.3 copy-start.4
  157.4 1.3 copy-start.5
  174.3 0.6 copy-start.23
  175.5 0.7 copy-start.26
  176.2 0.7 copy-start.27
  374.4 1.1 copy-start.6
  375.4 1.1 copy-start.7
  376.5 1.1 copy-start.8
  377.6 1.1 copy-start.9
  378.6 0.9 copy-start.10
  379.6 0.9 copy-start.11
  380.5 0.9 copy-start.12
  381.4 0.9 copy-start.13
  382.3 0.9 copy-start.14
  383.2 0.9 copy-start.15
  384.1 0.9 copy-start.16
  385.0 0.9 copy-start.17
  385.9 0.9 copy-start.18
  386.8 0.9 copy-start.19
  387.7 3.4 copy-start.24
  391.2 2.5 copy-start.25
  393.6 1.7 copy-start.1
